TPU v7x, 128 devices: a whole 4x4x4 slice. The times are simulated.
128 devices in a mesh: wide: 16 (over y, z_hi, core), narrow: 8 (over x, z_lo).
Axes of the slice: x: 4, y: 4, z: 4 (z_hi: 2, z_lo: 2; z = z_hi * 2 + z_lo), core: 2. Of those that a mesh axis runs over, the one named last changes fastest.
Arguments:
- x_pre: bfloat16 [32, 240, 2048], P('wide', None, 'narrow'), may hold values from -64 to 64
- x_act: bfloat16 [32, 50, 1024], P('wide', None, 'narrow'), may hold values from -64 to 64
- lengths: int32 [32], P('wide'), may hold values from 5 to 48, as said below
- cot_pre: float32 [32, 240, 2048], P('wide', None, 'narrow'), may hold values from -6 to 6
- cot_act: float32 [32, 50, 1024], P('wide', None, 'narrow'), may hold values from -6 to 6
- attn_gain_pre: float32 [2048], P('narrow'), may hold values from 0.1 to 1.9
- query_pre: bfloat16 [2048, 2048], P('wide', 'narrow'), may hold values from -0.125 to 0.125
- key_pre: bfloat16 [2048, 256], P('wide', 'narrow'), may hold values from -0.125 to 0.125
- value_pre: bfloat16 [2048, 256], P('wide', 'narrow'), may hold values from -0.125 to 0.125
- out_pre: bfloat16 [2048, 2048], P('narrow', 'wide'), may hold values from -1 to 1
- ffn_gain_pre: float32 [2048], P('narrow'), may hold values from 0.1 to 1.9
- gate_pre: bfloat16 [2048, 16384], P('wide', 'narrow'), may hold values from -0.125 to 0.125
- up_pre: bfloat16 [2048, 16384], P('wide', 'narrow'), may hold values from -0.125 to 0.125
- down_pre: bfloat16 [16384, 2048], P('narrow', 'wide'), may hold values from -0.046875 to 0.046875
- attn_gain_act: float32 [1024], P('narrow'), may hold values from 0.1 to 1.9
- query_act: bfloat16 [1024, 2048], P('wide', 'narrow'), may hold values from -0.1875 to 0.1875
- key_act: bfloat16 [1024, 256], P('wide', 'narrow'), may hold values from -0.1875 to 0.1875
- value_act: bfloat16 [1024, 256], P('wide', 'narrow'), may hold values from -0.1875 to 0.1875
- out_act: bfloat16 [2048, 1024], P('narrow', 'wide'), may hold values from -1 to 1
- ffn_gain_act: float32 [1024], P('narrow'), may hold values from 0.1 to 1.9
- gate_act: bfloat16 [1024, 4096], P('wide', 'narrow'), may hold values from -0.1875 to 0.1875
- up_act: bfloat16 [1024, 4096], P('wide', 'narrow'), may hold values from -0.1875 to 0.1875
- down_act: bfloat16 [4096, 1024], P('narrow', 'wide'), may hold values from -0.09375 to 0.09375
Outputs:
- y_pre: bfloat16 [32, 240, 2048], P('wide', None, 'narrow')
- y_act: bfloat16 [32, 50, 1024], P('wide', None, 'narrow')
- grad_x_pre: float32 [32, 240, 2048], P('wide', None, 'narrow')
- grad_x_act: float32 [32, 50, 1024], P('wide', None, 'narrow')
- grad_attn_gain_pre: float32 [2048], P('narrow')
- grad_query_pre: float32 [2048, 2048], P('wide', 'narrow')
- grad_key_pre: float32 [2048, 256], P('wide', 'narrow')
- grad_value_pre: float32 [2048, 256], P('wide', 'narrow')
- grad_out_pre: float32 [2048, 2048], P('narrow', 'wide')
- grad_ffn_gain_pre: float32 [2048], P('narrow')
- grad_gate_pre: float32 [2048, 16384], P('wide', 'narrow')
- grad_up_pre: float32 [2048, 16384], P('wide', 'narrow')
- grad_down_pre: float32 [16384, 2048], P('narrow', 'wide')
- grad_attn_gain_act: float32 [1024], P('narrow')
- grad_query_act: float32 [1024, 2048], P('wide', 'narrow')
- grad_key_act: float32 [1024, 256], P('wide', 'narrow')
- grad_value_act: float32 [1024, 256], P('wide', 'narrow')
- grad_out_act: float32 [2048, 1024], P('narrow', 'wide')
- grad_ffn_gain_act: float32 [1024], P('narrow')
- grad_gate_act: float32 [1024, 4096], P('wide', 'narrow')
- grad_up_act: float32 [1024, 4096], P('wide', 'narrow')
- grad_down_act: float32 [4096, 1024], P('narrow', 'wide')
Inputs may be any that keep to these rules, and one draw needn't show every extreme that they name: `lengths`: some item has exactly 48 live instruction tokens and another exactly 5.
All inputs are finite; a program needn't handle non-finite values.
Results may differ from a plain program's by a relative error of at most 0.023.
Values may be sent and summed in bfloat16 or wider, within the bound.
A program may use at most 192 MiB of HBM per device.

v0:
```python
import jax
import jax.numpy as jnp
from jax import lax
from jax.sharding import PartitionSpec as P

HEAD = 256
IMG = 192
TXT = 48
ACT = 50
MICRO = 2


EPSILON = 1e-06
MASKED_SCORE = -1000000000.0


def gelu_tanh(values):
    return jax.nn.gelu(values, approximate=True)


def project(inputs, matrix):
    return jnp.einsum("itd,dh->ith", inputs, matrix, preferred_element_type=jnp.float32)


def project_back(inputs, matrix):
    return jnp.einsum("ith,dh->itd", inputs, matrix, preferred_element_type=jnp.float32)


def outer_sum(left_rows, right_rows):
    return jnp.einsum("itd,ith->dh", left_rows, right_rows, preferred_element_type=jnp.float32)


def row_total(prefix_term, action_term):
    return lax.psum((prefix_term, action_term), "narrow")


def spread_normed(prefix_rows, action_rows):
    return (
        lax.all_gather(prefix_rows, "narrow", axis=2, tiled=True),
        lax.all_gather(action_rows, "narrow", axis=2, tiled=True),
    )


def spread_grads(prefix_rows, action_rows):
    return (
        lax.all_gather(prefix_rows, "narrow", axis=2, tiled=True),
        lax.all_gather(action_rows, "narrow", axis=2, tiled=True),
    )


def collect_branch(prefix_rows, action_rows):
    return (
        lax.psum_scatter(prefix_rows, "narrow", scatter_dimension=2, tiled=True),
        lax.psum_scatter(action_rows, "narrow", scatter_dimension=2, tiled=True),
    )


def collect_input(prefix_rows, action_rows):
    return (
        lax.psum_scatter(prefix_rows, "narrow", scatter_dimension=2, tiled=True),
        lax.psum_scatter(action_rows, "narrow", scatter_dimension=2, tiled=True),
    )


def keep_grads(grads):
    return grads


def unit_rows(prefix_rows, action_rows):
    narrow_size = lax.axis_size("narrow")
    total_prefix, total_action = row_total(
        jnp.sum(prefix_rows * prefix_rows, axis=2, keepdims=True),
        jnp.sum(action_rows * action_rows, axis=2, keepdims=True),
    )
    scale_prefix = lax.rsqrt(total_prefix / (prefix_rows.shape[2] * narrow_size) + EPSILON)
    scale_action = lax.rsqrt(total_action / (action_rows.shape[2] * narrow_size) + EPSILON)
    return (prefix_rows * scale_prefix, action_rows * scale_action, scale_prefix, scale_action)


def unit_back(
    grad_prefix,
    grad_action,
    unit_prefix,
    unit_action,
    scale_prefix,
    scale_action,
    gain_prefix,
    gain_action,
):
    narrow_size = lax.axis_size("narrow")
    inner_prefix = grad_prefix * gain_prefix
    inner_action = grad_action * gain_action
    dot_prefix, dot_action = row_total(
        jnp.sum(inner_prefix * unit_prefix, axis=2, keepdims=True),
        jnp.sum(inner_action * unit_action, axis=2, keepdims=True),
    )
    back_prefix = scale_prefix * (
        inner_prefix - unit_prefix * dot_prefix / (unit_prefix.shape[2] * narrow_size)
    )
    back_action = scale_action * (
        inner_action - unit_action * dot_action / (unit_action.shape[2] * narrow_size)
    )
    return (
        back_prefix,
        back_action,
        jnp.sum(grad_prefix * unit_prefix, axis=(0, 1)),
        jnp.sum(grad_action * unit_action, axis=(0, 1)),
    )


def gelu_back(grad_active, gate_values, upper_values):
    activated, pullback = jax.vjp(gelu_tanh, gate_values)
    grad_gate = pullback(grad_active * upper_values)[0]
    return (grad_gate.astype(jnp.bfloat16), (grad_active * activated).astype(jnp.bfloat16))


def visible_keys(lengths):
    prefix = IMG + TXT
    places = jnp.arange(IMG + TXT + ACT, dtype=jnp.int32)
    key_live = (
        (places[None, :] < IMG)
        | (places[None, :] >= prefix)
        | (places[None, :] - IMG < lengths[:, None])
    )
    allowed = (places[None, :] < prefix) | (places[:, None] >= prefix)
    return key_live[:, None, :] & allowed[None]


def micro_step(
    x_prefix,
    x_action,
    lengths,
    cot_prefix,
    cot_action,
    gain_list,
    weights_prefix,
    weights_action,
    ffn_finish,
):
    query_prefix, key_prefix, value_prefix, gate_prefix, up_prefix, out_prefix, down_prefix = (
        weights_prefix
    )
    query_action, key_action, value_action, gate_action, up_action, out_action, down_action = (
        weights_action
    )
    prefix = IMG + TXT
    length_all = IMG + TXT + ACT
    members = x_prefix.shape[0]
    head_count = query_prefix.shape[1] // HEAD
    temper = HEAD ** (-0.5)
    bfloat = jnp.bfloat16
    unit_prefix, unit_action, scale_prefix, scale_action = unit_rows(x_prefix, x_action)
    normed_prefix, normed_action = spread_normed(
        (unit_prefix * gain_list[0]).astype(bfloat), (unit_action * gain_list[2]).astype(bfloat)
    )
    queries = jnp.concatenate(
        [project(normed_prefix, query_prefix), project(normed_action, query_action)], axis=1
    ).astype(bfloat)
    key_local = jnp.concatenate(
        [project(normed_prefix, key_prefix), project(normed_action, key_action)], axis=1
    ).astype(bfloat)
    value_local = jnp.concatenate(
        [project(normed_prefix, value_prefix), project(normed_action, value_action)], axis=1
    ).astype(bfloat)
    key_full, value_full = (
        lax.all_gather(key_local, "narrow", axis=2, tiled=True),
        lax.all_gather(value_local, "narrow", axis=2, tiled=True),
    )
    query_heads = queries.reshape(members, length_all, head_count, HEAD)
    scores = (
        jnp.einsum("ishd,itd->ihst", query_heads, key_full, preferred_element_type=jnp.float32)
        * temper
    )
    scores = jnp.where(visible_keys(lengths)[:, None], scores, MASKED_SCORE)
    attention = jnp.exp(scores - jnp.max(scores, axis=3, keepdims=True))
    attention = attention / jnp.sum(attention, axis=3, keepdims=True)
    rounded = attention.astype(bfloat)
    mixture = jnp.einsum("ihst,itd->ishd", rounded, value_full, preferred_element_type=jnp.float32)
    mixture = mixture.reshape(members, length_all, head_count * HEAD).astype(bfloat)
    branch_prefix, branch_action = collect_branch(
        project(mixture[:, :prefix], out_prefix), project(mixture[:, prefix:], out_action)
    )
    hidden_prefix = x_prefix + branch_prefix
    hidden_action = x_action + branch_action
    second_prefix, second_action, rescale_prefix, rescale_action = unit_rows(
        hidden_prefix, hidden_action
    )
    ffn_prefix, ffn_action = spread_normed(
        (second_prefix * gain_list[1]).astype(bfloat), (second_action * gain_list[3]).astype(bfloat)
    )
    gate_in_prefix = project(ffn_prefix, gate_prefix)
    upper_prefix = project(ffn_prefix, up_prefix)
    gate_in_action = project(ffn_action, gate_action)
    upper_action = project(ffn_action, up_action)
    active_prefix = (gelu_tanh(gate_in_prefix) * upper_prefix).astype(bfloat)
    active_action = (gelu_tanh(gate_in_action) * upper_action).astype(bfloat)
    down_in_prefix, down_in_action = collect_branch(
        project(active_prefix, down_prefix), project(active_action, down_action)
    )
    result_prefix = (hidden_prefix + down_in_prefix).astype(bfloat)
    result_action = (hidden_action + down_in_action).astype(bfloat)
    cot_full_prefix, cot_full_action = spread_grads(
        cot_prefix.astype(bfloat), cot_action.astype(bfloat)
    )
    grad_down_prefix = outer_sum(active_prefix, cot_full_prefix)
    grad_down_action = outer_sum(active_action, cot_full_action)
    gate_grad_prefix, upper_grad_prefix = gelu_back(
        project_back(cot_full_prefix, down_prefix), gate_in_prefix, upper_prefix
    )
    gate_grad_action, upper_grad_action = gelu_back(
        project_back(cot_full_action, down_action), gate_in_action, upper_action
    )
    grad_gate_prefix = outer_sum(ffn_prefix, gate_grad_prefix)
    grad_up_prefix = outer_sum(ffn_prefix, upper_grad_prefix)
    grad_gate_action = outer_sum(ffn_action, gate_grad_action)
    grad_up_action = outer_sum(ffn_action, upper_grad_action)
    back_ffn_prefix, back_ffn_action = collect_input(
        project_back(gate_grad_prefix, gate_prefix) + project_back(upper_grad_prefix, up_prefix),
        project_back(gate_grad_action, gate_action) + project_back(upper_grad_action, up_action),
    )
    norm_prefix, norm_action, grad_ffn_gain_prefix, grad_ffn_gain_action = unit_back(
        back_ffn_prefix,
        back_ffn_action,
        second_prefix,
        second_action,
        rescale_prefix,
        rescale_action,
        gain_list[1],
        gain_list[3],
    )
    dhidden_prefix = cot_prefix + norm_prefix
    dhidden_action = cot_action + norm_action
    mix_full_prefix, mix_full_action = spread_grads(
        dhidden_prefix.astype(bfloat), dhidden_action.astype(bfloat)
    )
    grad_out_prefix = outer_sum(mixture[:, :prefix], mix_full_prefix)
    grad_out_action = outer_sum(mixture[:, prefix:], mix_full_action)
    ffn_result = ffn_finish(
        (
            grad_gate_prefix,
            grad_up_prefix,
            grad_down_prefix,
            grad_gate_action,
            grad_up_action,
            grad_down_action,
            grad_out_prefix,
            grad_out_action,
        )
    )
    grad_mixture = jnp.concatenate(
        [project_back(mix_full_prefix, out_prefix), project_back(mix_full_action, out_action)],
        axis=1,
    ).astype(bfloat)
    grad_heads = grad_mixture.reshape(members, length_all, head_count, HEAD)
    grad_attention = jnp.einsum(
        "ishd,itd->ihst", grad_heads, value_full, preferred_element_type=jnp.float32
    )
    grad_values = jnp.einsum(
        "ihst,ishd->itd", rounded, grad_heads, preferred_element_type=jnp.float32
    )
    grad_scores = (
        attention * (grad_attention - jnp.sum(attention * grad_attention, axis=3, keepdims=True))
    ).astype(bfloat)
    grad_queries = (
        jnp.einsum("ihst,itd->ishd", grad_scores, key_full, preferred_element_type=jnp.float32)
        * temper
    )
    grad_queries = grad_queries.reshape(members, length_all, head_count * HEAD).astype(bfloat)
    grad_keys = (
        jnp.einsum("ihst,ishd->itd", grad_scores, query_heads, preferred_element_type=jnp.float32)
        * temper
    )
    key_share, value_share = (
        lax.psum_scatter(
            grad_keys.astype(jnp.bfloat16), "narrow", scatter_dimension=2, tiled=True
        ).astype(jnp.float32),
        lax.psum_scatter(
            grad_values.astype(jnp.bfloat16), "narrow", scatter_dimension=2, tiled=True
        ).astype(jnp.float32),
    )
    key_share = key_share.astype(bfloat)
    value_share = value_share.astype(bfloat)
    grad_query_prefix = outer_sum(normed_prefix, grad_queries[:, :prefix])
    grad_query_action = outer_sum(normed_action, grad_queries[:, prefix:])
    grad_key_prefix = outer_sum(normed_prefix, key_share[:, :prefix])
    grad_key_action = outer_sum(normed_action, key_share[:, prefix:])
    grad_value_prefix = outer_sum(normed_prefix, value_share[:, :prefix])
    grad_value_action = outer_sum(normed_action, value_share[:, prefix:])
    back_attn_prefix, back_attn_action = collect_input(
        project_back(grad_queries[:, :prefix], query_prefix)
        + project_back(key_share[:, :prefix], key_prefix)
        + project_back(value_share[:, :prefix], value_prefix),
        project_back(grad_queries[:, prefix:], query_action)
        + project_back(key_share[:, prefix:], key_action)
        + project_back(value_share[:, prefix:], value_action),
    )
    first_prefix, first_action, grad_attn_gain_prefix, grad_attn_gain_action = unit_back(
        back_attn_prefix,
        back_attn_action,
        unit_prefix,
        unit_action,
        scale_prefix,
        scale_action,
        gain_list[0],
        gain_list[2],
    )
    input_prefix = dhidden_prefix + first_prefix
    input_action = dhidden_action + first_action
    attn_grads = (
        grad_query_prefix,
        grad_key_prefix,
        grad_value_prefix,
        grad_query_action,
        grad_key_action,
        grad_value_action,
    )
    gain_grads = (
        grad_attn_gain_prefix,
        grad_ffn_gain_prefix,
        grad_attn_gain_action,
        grad_ffn_gain_action,
    )
    return (
        result_prefix,
        result_action,
        input_prefix,
        input_action,
        attn_grads,
        ffn_result,
        gain_grads,
    )


def local(
    x_pre,
    x_act,
    lengths,
    cot_pre,
    cot_act,
    attn_gain_pre,
    query_pre,
    key_pre,
    value_pre,
    out_pre,
    ffn_gain_pre,
    gate_pre,
    up_pre,
    down_pre,
    attn_gain_act,
    query_act,
    key_act,
    value_act,
    out_act,
    ffn_gain_act,
    gate_act,
    up_act,
    down_act,
):
    gathered = (
        lax.all_gather(query_pre, "wide", axis=0, tiled=True),
        lax.all_gather(key_pre, "wide", axis=0, tiled=True),
        lax.all_gather(value_pre, "wide", axis=0, tiled=True),
        lax.all_gather(gate_pre, "wide", axis=0, tiled=True),
        lax.all_gather(up_pre, "wide", axis=0, tiled=True),
        lax.all_gather(query_act, "wide", axis=0, tiled=True),
        lax.all_gather(key_act, "wide", axis=0, tiled=True),
        lax.all_gather(value_act, "wide", axis=0, tiled=True),
        lax.all_gather(gate_act, "wide", axis=0, tiled=True),
        lax.all_gather(up_act, "wide", axis=0, tiled=True),
        lax.all_gather(out_pre, "wide", axis=1, tiled=True),
        lax.all_gather(down_pre, "wide", axis=1, tiled=True),
        lax.all_gather(out_act, "wide", axis=1, tiled=True),
        lax.all_gather(down_act, "wide", axis=1, tiled=True),
    )
    weights_prefix = (
        gathered[0],
        gathered[1],
        gathered[2],
        gathered[3],
        gathered[4],
        gathered[10],
        gathered[11],
    )
    weights_action = (
        gathered[5],
        gathered[6],
        gathered[7],
        gathered[8],
        gathered[9],
        gathered[12],
        gathered[13],
    )
    gain_list = (attn_gain_pre, ffn_gain_pre, attn_gain_act, ffn_gain_act)
    attn_totals = tuple(
        (
            jnp.zeros(matrix.shape, jnp.float32)
            for matrix in (
                weights_prefix[0],
                weights_prefix[1],
                weights_prefix[2],
                weights_action[0],
                weights_action[1],
                weights_action[2],
            )
        )
    )
    ffn_totals = tuple(
        (
            jnp.zeros(matrix.shape, jnp.float32)
            for matrix in (
                weights_prefix[3],
                weights_prefix[4],
                weights_prefix[6],
                weights_action[3],
                weights_action[4],
                weights_action[6],
                weights_prefix[5],
                weights_action[5],
            )
        )
    )
    gain_totals = tuple((jnp.zeros(matrix.shape, jnp.float32) for matrix in gain_list))
    per_micro = x_pre.shape[0] // MICRO
    outputs_prefix = []
    outputs_action = []
    inputs_prefix = []
    inputs_action = []
    for micro_index in range(MICRO):
        lower = micro_index * per_micro
        upper = lower + per_micro
        (
            result_prefix,
            result_action,
            input_prefix,
            input_action,
            attn_grads,
            ffn_result,
            gain_grads,
        ) = micro_step(
            x_pre[lower:upper].astype(jnp.float32),
            x_act[lower:upper].astype(jnp.float32),
            lengths[lower:upper],
            cot_pre[lower:upper],
            cot_act[lower:upper],
            gain_list,
            weights_prefix,
            weights_action,
            keep_grads,
        )
        outputs_prefix.append(result_prefix)
        outputs_action.append(result_action)
        inputs_prefix.append(input_prefix)
        inputs_action.append(input_action)
        gain_totals = tuple((running + update for running, update in zip(gain_totals, gain_grads)))
        attn_totals = tuple((running + update for running, update in zip(attn_totals, attn_grads)))
        ffn_totals = tuple((running + update for running, update in zip(ffn_totals, ffn_result)))
    shards = (
        lax.psum_scatter(
            attn_totals[0].astype(jnp.bfloat16), "wide", scatter_dimension=0, tiled=True
        ).astype(jnp.float32),
        lax.psum_scatter(
            attn_totals[1].astype(jnp.bfloat16), "wide", scatter_dimension=0, tiled=True
        ).astype(jnp.float32),
        lax.psum_scatter(
            attn_totals[2].astype(jnp.bfloat16), "wide", scatter_dimension=0, tiled=True
        ).astype(jnp.float32),
        lax.psum_scatter(
            attn_totals[3].astype(jnp.bfloat16), "wide", scatter_dimension=0, tiled=True
        ).astype(jnp.float32),
        lax.psum_scatter(
            attn_totals[4].astype(jnp.bfloat16), "wide", scatter_dimension=0, tiled=True
        ).astype(jnp.float32),
        lax.psum_scatter(
            attn_totals[5].astype(jnp.bfloat16), "wide", scatter_dimension=0, tiled=True
        ).astype(jnp.float32),
        lax.psum_scatter(
            ffn_totals[0].astype(jnp.bfloat16), "wide", scatter_dimension=0, tiled=True
        ).astype(jnp.float32),
        lax.psum_scatter(
            ffn_totals[1].astype(jnp.bfloat16), "wide", scatter_dimension=0, tiled=True
        ).astype(jnp.float32),
        lax.psum_scatter(
            ffn_totals[2].astype(jnp.bfloat16), "wide", scatter_dimension=1, tiled=True
        ).astype(jnp.float32),
        lax.psum_scatter(
            ffn_totals[3].astype(jnp.bfloat16), "wide", scatter_dimension=0, tiled=True
        ).astype(jnp.float32),
        lax.psum_scatter(
            ffn_totals[4].astype(jnp.bfloat16), "wide", scatter_dimension=0, tiled=True
        ).astype(jnp.float32),
        lax.psum_scatter(
            ffn_totals[5].astype(jnp.bfloat16), "wide", scatter_dimension=1, tiled=True
        ).astype(jnp.float32),
        lax.psum_scatter(
            ffn_totals[6].astype(jnp.bfloat16), "wide", scatter_dimension=1, tiled=True
        ).astype(jnp.float32),
        lax.psum_scatter(
            ffn_totals[7].astype(jnp.bfloat16), "wide", scatter_dimension=1, tiled=True
        ).astype(jnp.float32),
    )
    attn_shards = shards[:6]
    ffn_shards = shards[6:]
    gain_sums = lax.psum((gain_totals[0], gain_totals[1], gain_totals[2], gain_totals[3]), "wide")
    return (
        jnp.concatenate(outputs_prefix, axis=0),
        jnp.concatenate(outputs_action, axis=0),
        jnp.concatenate(inputs_prefix, axis=0),
        jnp.concatenate(inputs_action, axis=0),
        gain_sums[0],
        attn_shards[0],
        attn_shards[1],
        attn_shards[2],
        ffn_shards[6],
        gain_sums[1],
        ffn_shards[0],
        ffn_shards[1],
        ffn_shards[2],
        gain_sums[2],
        attn_shards[3],
        attn_shards[4],
        attn_shards[5],
        ffn_shards[7],
        gain_sums[3],
        ffn_shards[3],
        ffn_shards[4],
        ffn_shards[5],
    )


def solution(mesh):
    placed = (
        P("wide", None, "narrow"),
        P("wide", None, "narrow"),
        P("wide"),
        P("wide", None, "narrow"),
        P("wide", None, "narrow"),
        P("narrow"),
        P("wide", "narrow"),
        P("wide", "narrow"),
        P("wide", "narrow"),
        P("narrow", "wide"),
        P("narrow"),
        P("wide", "narrow"),
        P("wide", "narrow"),
        P("narrow", "wide"),
        P("narrow"),
        P("wide", "narrow"),
        P("wide", "narrow"),
        P("wide", "narrow"),
        P("narrow", "wide"),
        P("narrow"),
        P("wide", "narrow"),
        P("wide", "narrow"),
        P("narrow", "wide"),
    )
    return jax.shard_map(
        local,
        mesh=mesh,
        in_specs=placed,
        out_specs=(
            P("wide", None, "narrow"),
            P("wide", None, "narrow"),
            P("wide", None, "narrow"),
            P("wide", None, "narrow"),
            P("narrow"),
            P("wide", "narrow"),
            P("wide", "narrow"),
            P("wide", "narrow"),
            P("narrow", "wide"),
            P("narrow"),
            P("wide", "narrow"),
            P("wide", "narrow"),
            P("narrow", "wide"),
            P("narrow"),
            P("wide", "narrow"),
            P("wide", "narrow"),
            P("wide", "narrow"),
            P("narrow", "wide"),
            P("narrow"),
            P("wide", "narrow"),
            P("wide", "narrow"),
            P("narrow", "wide"),
        ),
        check_vma=False,
    )
```

profile of v0, /device:TPU:0, one launch (start us, length us, event | category | flops | bytes accessed | tf_op | source)
XLA Modules:
  0.0 2840.4 jit_solution(10006367961026181377)
XLA Ops:
  486.6 43.2 %reduce-scatter.43.cloned.1.call-done = f32[1,240,256]{2,1,0:T(8,128)} async-done(((f32[1,240,2048]{2,1,0:T(8,128)}), f32[1,240,256]{2,1,0:T(8,128)}) %reduce-scatter.43.cloned.1.call-update) | async-done | bytes 245776 | tf_op jit(solution)/shard_map/reduce_scatter | solution.py:53
  529.9 52.6 %reduce-scatter.47.cloned.1.call-done = f32[1,240,256]{2,1,0:T(8,128)} async-done(((f32[1,240,2048]{2,1,0:T(8,128)}), f32[1,240,256]{2,1,0:T(8,128)}) %reduce-scatter.47.cloned.1.call-update) | async-done | bytes 245776 | tf_op jit(solution)/shard_map/reduce_scatter | solution.py:53
  632.8 43.6 %all-gather.23.cloned.1.call-done = bf16[1024,512]{1,0:T(8,128)(2,1)} async-done(((bf16[64,512]{1,0:T(8,128)(2,1)}), bf16[1024,512]{1,0:T(8,128)(2,1)}) %all-gather.23.cloned.1.call-update) | async-done | bytes 1048592 | tf_op jit(solution)/shard_map/all_gather | solution.py:369
  678.6 43.9 %all-gather.25.cloned.1.call-done = bf16[512,1024]{0,1:T(8,128)(2,1)} async-done(((bf16[512,64]{0,1:T(8,128)(2,1)}), bf16[512,1024]{0,1:T(8,128)(2,1)}) %all-gather.25.cloned.1.call-update) | async-done | bytes 1048592 | tf_op jit(solution)/shard_map/all_gather | solution.py:373
  764.1 41.2 %all-gather.15.cloned.1.call-done = bf16[2048,2048]{1,0:T(8,128)(2,1)} async-done(((bf16[128,2048]{1,0:T(8,128)(2,1)}), bf16[2048,2048]{1,0:T(8,128)(2,1)}) %all-gather.15.cloned.1.call-update) | async-done | bytes 8388624 | tf_op jit(solution)/shard_map/all_gather | solution.py:363
  812.5 65.7 %all-gather.17.cloned.1.call-done = bf16[2048,2048]{1,0:T(8,128)(2,1)} async-done(((bf16[128,2048]{1,0:T(8,128)(2,1)}), bf16[2048,2048]{1,0:T(8,128)(2,1)}) %all-gather.17.cloned.1.call-update) | async-done | bytes 8388624 | tf_op jit(solution)/shard_map/all_gather | solution.py:364
  885.4 72.8 %all-gather.19.cloned.1.call-done = bf16[2048,2048]{1,0:T(8,128)(2,1)} async-done(((bf16[2048,128]{1,0:T(8,128)(2,1)}), bf16[2048,2048]{1,0:T(8,128)(2,1)}) %all-gather.19.cloned.1.call-update) | async-done | bytes 8388624 | tf_op jit(solution)/shard_map/all_gather | solution.py:371
  1004.3 44.7 %all_gather.132 = bf16[1,240,2048]{2,1,0:T(8,128)(2,1)} all-gather(bf16[1,240,256]{2,1,0:T(8,128)(2,1)} %get-tuple-element.183), channel_id=1, replica_groups=mesh['wide'=16,'narrow'=8] {'narrow'}, dimensions={2}, use_global_device_ids=true | all-gather | bytes 1105920 | tf_op jit(solution)/shard_map/all_gather | solution.py:46
  1321.7 53.6 %reduce-scatter.49.cloned.1.call-done = f32[1,240,256]{2,1,0:T(8,128)} async-done(((f32[1,240,2048]{2,1,0:T(8,128)}), f32[1,240,256]{2,1,0:T(8,128)}) %reduce-scatter.49.cloned.1.call-update) | async-done | bytes 245776 | tf_op jit(solution)/shard_map/reduce_scatter | solution.py:53
  1497.6 72.3 %all-reduce.12.cloned.1.call-done = (bf16[1,290,256]{1,0,2:T(2,128)(2,1)}, bf16[1,290,256]{1,0,2:T(2,128)(2,1)}, bf16[1,290,256]{1,0,2:T(2,128)(2,1)}, bf16[1,290,256]{1,0,2:T(2,128)(2,1)}) async-done(((bf16[1,290,256]{1,0,2:T(2,128)(2,1)}, bf16[1,290,256]{1,0,2:T(2,128)(2,1)}, bf16[1,290,256]{1,0,2:T(2,128)(2,1)}, bf16[1,290,256]{1,0,2:T(2,128)(2,1)}), (bf16[1,290,256]{1,0,2:T(2,128)(2,1)}, ...) | async-done | bytes 593936
  1712.0 68.0 %reduce-scatter.89.cloned.1.call-done = bf16[512,64]{0,1:T(8,128)(2,1)} async-done(((bf16[512,1024]{0,1:T(8,128)(2,1)}), bf16[512,64]{0,1:T(8,128)(2,1)}) %reduce-scatter.89.cloned.1.call-update) | async-done | bytes 65552 | tf_op jit(solution)/shard_map/reduce_scatter | solution.py:491
  1782.9 65.8 %reduce-scatter.99.cloned.1.call-done = bf16[64,32]{1,0:T(8,128)(2,1)} async-done(((bf16[1024,32]{1,0:T(8,128)(2,1)}), bf16[64,32]{1,0:T(8,128)(2,1)}) %reduce-scatter.99.cloned.1.call-update) | async-done | bytes 4112
  1850.2 66.2 %reduce-scatter.101.cloned.1.call-done = bf16[64,32]{1,0:T(8,128)(2,1)} async-done(((bf16[1024,32]{1,0:T(8,128)(2,1)}), bf16[64,32]{1,0:T(8,128)(2,1)}) %reduce-scatter.101.cloned.1.call-update) | async-done | bytes 4112
  1917.7 67.1 %reduce-scatter.81.cloned.1.call-done = bf16[64,256]{1,0:T(8,128)(2,1)} async-done(((bf16[1024,256]{1,0:T(8,128)(2,1)}), bf16[64,256]{1,0:T(8,128)(2,1)}) %reduce-scatter.81.cloned.1.call-update) | async-done | bytes 32784 | tf_op jit(solution)/shard_map/reduce_scatter | solution.py:467
  1986.2 66.8 %reduce-scatter.83.cloned.1.call-done = bf16[256,64]{0,1:T(8,128)(2,1)} async-done(((bf16[256,1024]{0,1:T(8,128)(2,1)}), bf16[256,64]{0,1:T(8,128)(2,1)}) %reduce-scatter.83.cloned.1.call-update) | async-done | bytes 32784 | tf_op jit(solution)/shard_map/reduce_scatter | solution.py:497
  2054.4 67.3 %reduce-scatter.91.cloned.1.call-done = bf16[128,32]{1,0:T(8,128)(2,1)} async-done(((bf16[2048,32]{1,0:T(8,128)(2,1)}), bf16[128,32]{1,0:T(8,128)(2,1)}) %reduce-scatter.91.cloned.1.call-update) | async-done | bytes 8208
  2123.2 66.6 %reduce-scatter.93.cloned.1.call-done = bf16[128,32]{1,0:T(8,128)(2,1)} async-done(((bf16[2048,32]{1,0:T(8,128)(2,1)}), bf16[128,32]{1,0:T(8,128)(2,1)}) %reduce-scatter.93.cloned.1.call-update) | async-done | bytes 8208
  2267.7 69.2 %reduce-scatter.95.cloned.1.call-done = bf16[128,256]{1,0:T(8,128)(2,1)} async-done(((bf16[2048,256]{1,0:T(8,128)(2,1)}), bf16[128,256]{1,0:T(8,128)(2,1)}) %reduce-scatter.95.cloned.1.call-update) | async-done | bytes 65552
  2338.5 68.6 %reduce-scatter.75.cloned.1.call-done = bf16[128,256]{1,0:T(8,128)(2,1)} async-done(((bf16[2048,256]{1,0:T(8,128)(2,1)}), bf16[128,256]{1,0:T(8,128)(2,1)}) %reduce-scatter.75.cloned.1.call-update) | async-done | bytes 65552 | tf_op jit(solution)/shard_map/reduce_scatter | solution.py:458
  2408.6 49.4 %reduce-scatter.63.cloned.1.call-done = f32[1,240,256]{2,1,0:T(8,128)} async-done(((f32[1,240,2048]{2,1,0:T(8,128)}), f32[1,240,256]{2,1,0:T(8,128)}) %reduce-scatter.63.cloned.1.call-update) | async-done | bytes 245776 | tf_op jit(solution)/shard_map/reduce_scatter | solution.py:60
  2458.1 52.5 %reduce-scatter.69.cloned.1.call-done = f32[1,240,256]{2,1,0:T(8,128)} async-done(((f32[1,240,2048]{2,1,0:T(8,128)}), f32[1,240,256]{2,1,0:T(8,128)}) %reduce-scatter.69.cloned.1.call-update) | async-done | bytes 245776 | tf_op jit(solution)/shard_map/reduce_scatter | solution.py:60
  2568.2 50.5 %reduce-scatter.97.cloned.1.call-done = bf16[128,2048]{1,0:T(8,128)(2,1)} async-done(((bf16[2048,2048]{1,0:T(8,128)(2,1)}), bf16[128,2048]{1,0:T(8,128)(2,1)}) %reduce-scatter.97.cloned.1.call-update) | async-done | bytes 524304
  2621.1 103.8 %reduce-scatter.77.cloned.1.call-done = bf16[128,2048]{1,0:T(8,128)(2,1)} async-done(((bf16[2048,2048]{1,0:T(8,128)(2,1)}), bf16[128,2048]{1,0:T(8,128)(2,1)}) %reduce-scatter.77.cloned.1.call-update) | async-done | bytes 524304 | tf_op jit(solution)/shard_map/reduce_scatter | solution.py:476
  2727.0 103.9 %reduce-scatter.79.cloned.1.call-done = bf16[128,2048]{1,0:T(8,128)(2,1)} async-done(((bf16[2048,2048]{1,0:T(8,128)(2,1)}), bf16[128,2048]{1,0:T(8,128)(2,1)}) %reduce-scatter.79.cloned.1.call-update) | async-done | bytes 524304 | tf_op jit(solution)/shard_map/reduce_scatter | solution.py:479
  (602 shorter events, 1323.5 us)
Async XLA Ops:
  7.2 392.8 %all-gather.11.cloned.1.call-start = ((), (), s32[]{:S(2)}) async-start(), calls=%async_computation.30 | async-start | bytes 1114112 | tf_op jit(solution)/shard_map/all_gather | solution.py:360
  8.0 402.3 %all-gather.13.cloned.1.call-start = ((), (), s32[]{:S(2)}) async-start(), calls=%async_computation.31 | async-start | bytes 1114112 | tf_op jit(solution)/shard_map/all_gather | solution.py:370
  8.7 474.0 %reduce-scatter.55.cloned.1.call-start = ((), (), s32[]{:S(2)}) async-start(), calls=%async_computation.44 | async-start | bytes 258048 | tf_op jit(solution)/shard_map/reduce_scatter | solution.py:54
  418.7 386.6 %all-gather.15.cloned.1.call-start = ((), (), s32[]{:S(2)}) async-start(), calls=%async_computation.33 | async-start | bytes 8912896 | tf_op jit(solution)/shard_map/all_gather | solution.py:363
  419.3 458.9 %all-gather.17.cloned.1.call-start = ((), (), s32[]{:S(2)}) async-start(), calls=%async_computation.34 | async-start | bytes 8912896 | tf_op jit(solution)/shard_map/all_gather | solution.py:364
  420.0 538.2 %all-gather.19.cloned.1.call-start = ((), (), s32[]{:S(2)}) async-start(), calls=%async_computation.35 | async-start | bytes 8912896 | tf_op jit(solution)/shard_map/all_gather | solution.py:371
  420.6 629.6 %reduce-scatter.61.cloned.1.call-start = ((), (), s32[]{:S(2)}) async-start(), calls=%async_computation.47 | async-start | bytes 258048 | tf_op jit(solution)/shard_map/reduce_scatter | solution.py:61
  764.1 318.0 %reduce-scatter.59.cloned.1.call-start = ((), (), s32[]{:S(2)}) async-start(), calls=%async_computation.46 | async-start | bytes 2211840 | tf_op jit(solution)/shard_map/reduce_scatter | solution.py:60
  1164.3 405.5 %all-reduce.12.cloned.1.call-start = ((), (), s32[]{:S(2)}) async-start(), calls=%async_computation.68 | async-start | bytes 3145728
  1491.7 357.0 %reduce-scatter.99.cloned.1.call-start = ((), (), s32[]{:S(2)}) async-start(), calls=%async_computation.66 | async-start | bytes 278528
  1580.1 336.3 %reduce-scatter.101.cloned.1.call-start = ((), (), s32[]{:S(2)}) async-start(), calls=%async_computation.67 | async-start | bytes 278528
  1583.6 401.3 %reduce-scatter.81.cloned.1.call-start = ((), (), s32[]{:S(2)}) async-start(), calls=%async_computation.57 | async-start | bytes 557056 | tf_op jit(solution)/shard_map/reduce_scatter | solution.py:467
  1586.2 466.9 %reduce-scatter.83.cloned.1.call-start = ((), (), s32[]{:S(2)}) async-start(), calls=%async_computation.58 | async-start | bytes 557056 | tf_op jit(solution)/shard_map/reduce_scatter | solution.py:497
  1589.6 532.1 %reduce-scatter.91.cloned.1.call-start = ((), (), s32[]{:S(2)}) async-start(), calls=%async_computation.62 | async-start | bytes 557056
  1599.9 589.9 %reduce-scatter.93.cloned.1.call-start = ((), (), s32[]{:S(2)}) async-start(), calls=%async_computation.63 | async-start | bytes 557056
  1601.7 626.8 %reduce-scatter.71.cloned.1.call-start = ((), (), s32[]{:S(2)}) async-start(), calls=%async_computation.52 | async-start | bytes 258048 | tf_op jit(solution)/shard_map/reduce_scatter | solution.py:61
  1604.8 661.9 %reduce-scatter.73.cloned.1.call-start = ((), (), s32[]{:S(2)}) async-start(), calls=%async_computation.53 | async-start | bytes 258048 | tf_op jit(solution)/shard_map/reduce_scatter | solution.py:61
  1608.7 728.1 %reduce-scatter.95.cloned.1.call-start = ((), (), s32[]{:S(2)}) async-start(), calls=%async_computation.64 | async-start | bytes 1114112
  1614.4 792.8 %reduce-scatter.75.cloned.1.call-start = ((), (), s32[]{:S(2)}) async-start(), calls=%async_computation.54 | async-start | bytes 1114112 | tf_op jit(solution)/shard_map/reduce_scatter | solution.py:458
  1616.8 841.3 %reduce-scatter.63.cloned.1.call-start = ((), (), s32[]{:S(2)}) async-start(), calls=%async_computation.48 | async-start | bytes 2211840 | tf_op jit(solution)/shard_map/reduce_scatter | solution.py:60
  1620.3 890.3 %reduce-scatter.69.cloned.1.call-start = ((), (), s32[]{:S(2)}) async-start(), calls=%async_computation.51 | async-start | bytes 2211840 | tf_op jit(solution)/shard_map/reduce_scatter | solution.py:60
  1624.2 994.5 %reduce-scatter.97.cloned.1.call-start = ((), (), s32[]{:S(2)}) async-start(), calls=%async_computation.65 | async-start | bytes 8912896
  1657.3 1067.5 %reduce-scatter.77.cloned.1.call-start = ((), (), s32[]{:S(2)}) async-start(), calls=%async_computation.55 | async-start | bytes 8912896 | tf_op jit(solution)/shard_map/reduce_scatter | solution.py:476
  1678.5 1152.4 %reduce-scatter.79.cloned.1.call-start = ((), (), s32[]{:S(2)}) async-start(), calls=%async_computation.56 | async-start | bytes 8912896 | tf_op jit(solution)/shard_map/reduce_scatter | solution.py:479
  (157 other events, 17203.8 us)
Sparse Core Ops, SparseCore 0:
  480.5 49.3 reduce-scatter.42
  532.3 50.1 reduce-scatter.46
  724.8 80.4 all-gather.14
  807.7 70.4 all-gather.16
  880.3 77.8 all-gather.18
  999.1 64.7 reduce-scatter.58
  1144.4 48.6 reduce-scatter.64
  1324.1 51.1 reduce-scatter.48
  1481.6 88.1 all-reduce.11
  1574.3 66.0 reduce-scatter.84
  1644.7 65.7 reduce-scatter.86
  1714.2 65.7 reduce-scatter.88
  1784.8 63.9 reduce-scatter.98
  1852.3 63.9 reduce-scatter.100
  1920.4 64.3 reduce-scatter.80
  1988.6 64.4 reduce-scatter.82
  2057.3 64.3 reduce-scatter.90
  2125.3 64.4 reduce-scatter.92
  2271.4 65.3 reduce-scatter.94
  2341.3 65.8 reduce-scatter.74
  2460.3 50.1 reduce-scatter.68
  2515.4 103.3 reduce-scatter.96
  2623.7 101.1 reduce-scatter.76
  2729.7 101.1 reduce-scatter.78
  (15 shorter events, 606.0 us)
where the time goes:
time: 2850 us; the launch traced here: 2840 us
  waiting for transfers between devices  1650 us (58%)
  blocking collectives  822 us (29%)
  matrix products  230 us (8%)
  local copies, waits for them, and re-layouts  65.3 us (2%)
  other arithmetic  49.6 us (2%)
    unnamed x46, waiting for transfers between devices  464 us
    reduce_scatter x4, waiting for transfers between devices, collect_branch(): lax.psum_scatter(prefix_rows, 'narrow', scatter_dimension=2, tiled=True)  171 us
    all_gather x4, blocking collectives, spread_grads(): lax.all_gather(prefix_rows, 'narrow', axis=2, tiled=True)  140 us
    reduce_scatter x4, waiting for transfers between devices, collect_input(): lax.psum_scatter(prefix_rows, 'narrow', scatter_dimension=2, tiled=True)  129 us
    all_gather x4, blocking collectives, spread_normed(): lax.all_gather(prefix_rows, 'narrow', axis=2, tiled=True)  127 us
    reduce_scatter x1, waiting for transfers between devices, local(): lax.psum_scatter(ffn_totals[1].astype(jnp.bfloat16), 'wide', scatter_dime...  104 us
    reduce_scatter x1, waiting for transfers between devices, local(): lax.psum_scatter(ffn_totals[0].astype(jnp.bfloat16), 'wide', scatter_dime...  104 us
    all_gather x4, blocking collectives, spread_grads(): lax.all_gather(action_rows, 'narrow', axis=2, tiled=True)  99.6 us
  transfers between devices with their start and end apart: 39, of which 31 were waited for; matrix products, arithmetic and copies ran while one was open for 11% of the time, Pallas kernels for 0%

commit v1 on v0

v1 whole, which is shorter than its diff:
```python
import functools
import jax
import jax.numpy as jnp
from jax import lax
from jax.experimental import pallas as pl
from jax.experimental.pallas import tpu as pltpu
from jax.sharding import PartitionSpec as P

MESH = pl.DeviceIdType.MESH
BF = jnp.bfloat16
F32 = jnp.float32
SEMS = 256
VMEM_CAP = 62 * 1024 * 1024


class Place:
    def __init__(self):
        wide, narrow = lax.axis_index("wide"), lax.axis_index("narrow")
        self.core = lax.rem(wide, 2)
        self.zh = lax.rem(lax.div(wide, 2), 2)
        self.y = lax.div(wide, 4)
        self.zl = lax.rem(narrow, 2)
        self.x = lax.div(narrow, 2)
        self.z = self.zh * 2 + self.zl

    def wide_at(self, y, zh, core):
        return (y * 2 + zh) * 2 + core

    def coord(self, axis):
        return {"x": self.x, "y": self.y, "z": self.z}[axis]

    def off(self, axis, step):
        return lax.rem(self.coord(axis) + step + 4, 4)

    def peer(self, name):
        if name == "sib":
            return {"wide": self.wide_at(self.y, self.zh, 1 - self.core)}
        if name == "z2":
            return {"wide": self.wide_at(self.y, 1 - self.zh, self.core)}
        if name == "zl":
            return {"narrow": self.x * 2 + 1 - self.zl}
        axis, step = name[0], 1 if name[1] == "+" else -1
        at = self.off(axis, step)
        if axis == "y":
            return {"wide": self.wide_at(at, self.zh, self.core)}
        if axis == "x":
            return {"narrow": at * 2 + self.zl}
        return {"wide": self.wide_at(self.y, lax.div(at, 2), self.core), "narrow": self.x * 2 + lax.rem(at, 2)}


class Link:
    def __init__(self, out, into):
        self.out, self.into = out, into

    def arrive(self):
        self.into.wait_recv()

    def left(self):
        self.out.wait_send()


class Comm:
    def __init__(self, send_sems, recv_sems, local_sems):
        self.place = Place()
        self.send_sems, self.recv_sems, self.local_sems = send_sems, recv_sems, local_sems
        self.count, self.local_count = 0, 0
        self.links = []

    def enter(self, peers):
        barrier = pltpu.get_barrier_semaphore()
        for name in peers:
            pl.semaphore_signal(barrier, inc=1, device_id=self.place.peer(name), device_id_type=MESH)
        pl.semaphore_wait(barrier, len(peers))

    def send(self, src, dst, name, incoming):
        index = self.count
        self.count += 1
        make = lambda to: pltpu.make_async_remote_copy(
            src_ref=src, dst_ref=to, send_sem=self.send_sems.at[index], recv_sem=self.recv_sems.at[index],
            device_id=self.place.peer(name), device_id_type=MESH)
        out = make(dst)
        out.start()
        link = Link(out, make(incoming))
        self.links.append(link)
        return link

    def local(self, src, dst):
        index = self.local_count
        self.local_count += 1
        copy = pltpu.make_async_copy(src, dst, self.local_sems.at[index])
        copy.start()
        return copy

    def close(self):
        for link in self.links:
            link.left()

    def ring_gather(self, axis, view, parts, own=None):
        place = self.place
        at = lambda step: place.off(axis, step)
        src = own if own is not None else (lambda part: view(at(0), part))
        plus = [self.send(src(p), view(at(0), p), axis + "+", view(at(-1), p)) for p, _ in parts]
        minus = [self.send(src(p), view(at(0), p), axis + "-", view(at(1), p)) for p, _ in parts]
        yield
        far = []
        for (p, way), up in zip(parts, plus):
            up.arrive()
            if way > 0:
                far.append(self.send(view(at(-1), p), view(at(-1), p), axis + "+", view(at(-2), p)))
        for (p, way), down in zip(parts, minus):
            down.arrive()
            if way < 0:
                far.append(self.send(view(at(1), p), view(at(1), p), axis + "-", view(at(2), p)))
        yield
        for link in far:
            link.arrive()

    def pair_ring_gather(self, pair, axis, view, parts, own, give, whole):
        place = self.place
        mine = {"z2": place.zh, "zl": place.zl}[pair]
        here = place.coord(axis)
        swap = self.send(give, view(here, mine, whole), pair, view(here, 1 - mine, whole))
        first = self.ring_gather(axis, lambda k, p: view(k, mine, p), parts, own)
        next(first)
        yield
        swap.arrive()
        second = self.ring_gather(axis, lambda k, p: view(k, 1 - mine, p), parts)
        next(second)
        yield
        next(first)
        yield
        next(second)
        yield
        drain(first)
        drain(second)

    def plane_gather(self, view, parts_x, parts_z):
        place = self.place
        every = slice(None)
        ax = self.ring_gather("x", lambda k, p: view(k, place.z, p), parts_x)
        bz = self.ring_gather("z", lambda k, p: view(place.x, k, p), parts_z)
        next(ax), next(bz)
        yield
        next(ax), next(bz)
        yield
        drain(ax)
        az = self.ring_gather("z", lambda k, p: view(every, k, p), parts_x)
        next(az)
        drain(bz)
        bx = self.ring_gather("x", lambda k, p: view(k, every, p), parts_z)
        next(bx)
        yield
        next(az), next(bx)
        yield
        drain(az), drain(bx)

    def ring_sum(self, axis, view, parts, relay, plus, minus):
        place = self.place
        at = lambda step: place.off(axis, step)
        far = []
        for p, way in parts:
            far.append(self.send(view(at(2), p), relay(p), axis + ("+" if way > 0 else "-"), relay(p)))
        yield
        ups, downs = [], []
        for (p, way), link in zip(parts, far):
            link.arrive()
            add_to(view(at(way), p), relay(p))
            if way > 0:
                ups.append(self.send(view(at(1), p), plus(p), axis + "+", plus(p)))
            else:
                downs.append(self.send(view(at(-1), p), minus(p), axis + "-", minus(p)))
        for p, way in parts:
            if way > 0:
                downs.append(self.send(view(at(-1), p), minus(p), axis + "-", minus(p)))
            else:
                ups.append(self.send(view(at(1), p), plus(p), axis + "+", plus(p)))
        yield
        for link in ups + downs:
            link.arrive()
        for p, _ in parts:
            add_to(view(at(0), p), plus(p), minus(p))


def add_to(ref, *others):
    total = ref[...].astype(F32)
    for other in others:
        total = total + other[...].astype(F32)
    ref[...] = total.astype(ref.dtype)


def drain(task):
    for _ in task:
        pass


def rows(lo, hi):
    return pl.ds(lo, hi - lo)
T = 544
CH = 4


def halves(n):
    return [(rows(0, n // 2), 1), (rows(n // 2, n), -1)]


PARTS_8 = [(rows(0, 272), 1), (rows(272, 544), -1)]
PARTS_A = [(rows(0, 144), 1), (rows(144, 272), -1)]
PARTS_B = [(rows(272, 416), 1), (rows(416, 544), -1)]
PEERS = ("y+", "y-", "z2", "sib", "x+", "x-", "z+", "z-")


def wide_gather(comm, out, own, give, n):
    place = comm.place
    core = place.core
    copy = comm.local(own, out.at[place.y, place.zh, core])
    task = comm.pair_ring_gather(
        "z2", "y", lambda k, j, p: out.at[k, j, core, p], halves(n),
        lambda p: own.at[p], give, slice(None))
    yield from task
    copy.wait()
    link = comm.send(out.at[:, :, core], out.at[:, :, core], "sib", out.at[:, :, 1 - core])
    yield
    link.arrive()


def block_gather(comm, out, own, parts):
    place = comm.place
    copy = comm.local(own, out.at[place.x, place.zl])
    yield from comm.pair_ring_gather(
        "zl", "x", lambda k, j, p: out.at[k, j, p], parts, lambda p: own.at[p], own, slice(None))
    copy.wait()


def plane_spread(comm, out, own):
    place = comm.place
    copy = comm.local(own, out.at[place.x, place.z])
    copy.wait()
    yield from comm.plane_gather(lambda k, j, p: out.at[k, j, p], PARTS_A, PARTS_B)


def run(tasks):
    tasks = list(tasks)
    while tasks:
        left = []
        for task in tasks:
            try:
                next(task)
                left.append(task)
            except StopIteration:
                pass
        tasks = left


def gather_kernel(wf, wfa, wq, wqa, kvs, xb, cb, gb, out_f, out_fa, out_q, out_qa, out_kv, out_kva, out_x, out_c, out_g,
                  kv8, kvf, send_sems, recv_sems, local_sems):
    comm = Comm(send_sems, recv_sems, local_sems)
    place = comm.place
    comm.enter(PEERS)
    zh = place.zh
    every = slice(None)

    def kv_task():
        yield from block_gather(comm, kv8, kvs, halves(192))
        total = jnp.zeros((192, 512), F32)
        for n in range(8):
            lane = lax.broadcasted_iota(jnp.int32, (128, 512), 0)
            col = lax.broadcasted_iota(jnp.int32, (128, 512), 1)
            pick = ((lane < 32) & (col == 32 * n + lane)) | ((lane >= 32) & (lane < 64) & (col == 224 + 32 * n + lane))
            total = total + jnp.dot(kv8[n // 2, n % 2], pick.astype(F32).astype(BF), preferred_element_type=F32)
        kvf[...] = total.astype(BF)
        a, b = kvf.at[0:128], kvf.at[128:192]
        one = wide_gather(comm, out_kv, a, a, 128)
        two = wide_gather(comm, out_kva, b, b, 64)
        for _ in one:
            next(two, None)
            yield
        drain(two)

    tasks = [
        block_gather(comm, out_x, xb, PARTS_8),
        block_gather(comm, out_g, gb, [(slice(None), 1)]),
        kv_task(),
        wide_gather(comm, out_q, wq, wq, 128),
        wide_gather(comm, out_qa, wqa, wqa, 64),
        wide_gather(comm, out_fa, wfa.at[zh], wfa.at[1 - zh], 64),
    ]
    for i in range(CH):
        tasks.append(wide_gather(comm, out_f.at[i], wf.at[zh, i], wf.at[1 - zh, i], 128))
    tasks.append(plane_spread(comm, out_c, cb))
    run(tasks)
    comm.close()


def gather_all(wf, wfa, wq, wqa, kvs, xb, cb, gb):
    any_ = pl.BlockSpec(memory_space=pl.ANY)
    vm = pl.BlockSpec(memory_space=pltpu.VMEM)
    shapes = [(CH, 4, 2, 2, 128, 768), (4, 2, 2, 64, 768), (4, 2, 2, 128, 512), (4, 2, 2, 64, 512),
              (4, 2, 2, 128, 512), (4, 2, 2, 64, 512), (4, 2, T, 256), (4, 4, T, 256)]
    return pl.pallas_call(
        gather_kernel,
        out_shape=[jax.ShapeDtypeStruct(s, BF) for s in shapes] + [jax.ShapeDtypeStruct((4, 2, 8, 256), F32)],
        in_specs=[any_] * 8,
        out_specs=[any_] * 9,
        scratch_shapes=[pltpu.VMEM((4, 2, 192, 128), BF), pltpu.VMEM((192, 512), BF),
                        pltpu.SemaphoreType.DMA((SEMS,)), pltpu.SemaphoreType.DMA((SEMS,)), pltpu.SemaphoreType.DMA((32,))],
        compiler_params=pltpu.CompilerParams(collective_id=0, has_side_effects=True, vmem_limit_bytes=VMEM_CAP),
    )(wf, wfa, wq, wqa, kvs, xb, cb, gb)


def pack_hidden(gate, up, down):
    n, hidden = gate.shape
    cut = lambda m: m.reshape(n, 2, hidden // 512, 256)
    return jnp.concatenate([cut(gate), cut(up), cut(down.T)], axis=-1).transpose(1, 2, 0, 3)


def pack_tokens(pre, act):
    low = jnp.concatenate([act[0], act[1]], axis=1)
    low = jnp.pad(low, ((0, 14), (0, 0)))
    return jnp.concatenate([pre.reshape(480, 256), low], axis=0).astype(BF)
def whole(ref):
    return ref


def loop_add(ref, n, *others):
    def step(i, carry):
        add_to(ref.at[i], *[other.at[i] for other in others])
        return carry
    lax.fori_loop(0, n, step, 0)


def pair_ring_sum(comm, pair, axis, view, parts, lands, swap):
    relay, plus, minus = lands
    yield from comm.ring_sum(axis, view, parts, lambda p: relay.at[:, p], lambda p: plus.at[:, p], lambda p: minus.at[:, p])


def block_sum(comm, blocks, lands, swap):
    place = comm.place
    relay, plus, minus = lands
    yield from comm.ring_sum(
        "x", lambda k, p: blocks.at[k, :, p], PARTS_8,
        lambda p: relay.at[:, p], lambda p: plus.at[:, p], lambda p: minus.at[:, p])
    link = comm.send(blocks.at[place.x, 1 - place.zl], swap, "zl", swap)
    yield
    link.arrive()
    add_to(blocks.at[place.x, place.zl], swap)


def plane_sum(comm, blocks, lands_far, lands_near):
    place = comm.place
    az = comm.ring_sum("z", lambda k, p: blocks.at[:, k, p], PARTS_A,
                       lambda p: lands_far.at[0, :, p], lambda p: lands_far.at[1, :, p], lambda p: lands_far.at[2, :, p])
    bx = comm.ring_sum("x", lambda k, p: blocks.at[k, :, p], PARTS_B,
                       lambda p: lands_far.at[0, :, p], lambda p: lands_far.at[1, :, p], lambda p: lands_far.at[2, :, p])
    next(az), next(bx)
    yield
    next(az), next(bx)
    yield
    drain(az)
    ax = comm.ring_sum("x", lambda k, p: blocks.at[k, place.z, p], PARTS_A,
                       lambda p: lands_near.at[0, p], lambda p: lands_near.at[1, p], lambda p: lands_near.at[2, p])
    next(ax)
    drain(bx)
    bz = comm.ring_sum("z", lambda k, p: blocks.at[place.x, k, p], PARTS_B,
                       lambda p: lands_near.at[0, p], lambda p: lands_near.at[1, p], lambda p: lands_near.at[2, p])
    next(bz)
    yield
    next(ax), next(bz)
    yield
    drain(ax), drain(bz)


def wide_sum(comm, grad, half, relay, plus, minus, swap, n, add):
    place = comm.place
    core, zh = place.core, place.zh
    link = comm.send(grad.at[1 - core], half, "sib", half)
    yield
    link.arrive()
    loop_add(grad.at[core], 4, half)
    yield from comm.ring_sum(
        "y", lambda k, p: grad.at[core, k, :, p], halves(n),
        lambda p: relay.at[:, p], lambda p: plus.at[:, p], lambda p: minus.at[:, p])
    link = comm.send(grad.at[core, place.y, 1 - zh], swap, "z2", swap)
    yield
    link.arrive()
    if add:
        add_to(grad.at[core, place.y, zh], swap)


SEM_SCRATCH = [pltpu.SemaphoreType.DMA((SEMS,)), pltpu.SemaphoreType.DMA((SEMS,)), pltpu.SemaphoreType.DMA((32,))]
ANY = pl.BlockSpec(memory_space=pl.ANY)


def call(kernel, shapes, scratch, ident, *args):
    return pl.pallas_call(
        kernel,
        out_shape=[jax.ShapeDtypeStruct(s, d) for s, d in shapes],
        in_specs=[ANY] * len(args),
        out_specs=[ANY] * len(shapes),
        scratch_shapes=list(scratch) + SEM_SCRATCH,
        compiler_params=pltpu.CompilerParams(collective_id=ident, has_side_effects=True, vmem_limit_bytes=VMEM_CAP),
    )(*args)


LAND_8 = [pltpu.VMEM((2, T, 256), BF)] * 3 + [pltpu.VMEM((T, 256), BF)]


def hidden_kernel(terms, xb, out_h, out_full, blocks, xv, hv, full, r0, r1, r2, r3, *sems):
    comm = Comm(*sems)
    place = comm.place
    one, two = comm.local(terms, blocks), comm.local(xb, xv)
    comm.enter(PEERS)
    one.wait(), two.wait()
    drain(block_sum(comm, blocks, (r0, r1, r2), r3))
    hv[...] = xv[...].astype(F32) + blocks[place.x, place.zl].astype(F32)
    three = comm.local(hv, out_h)
    full[place.x, place.z] = hv[...].astype(BF)
    drain(comm.plane_gather(lambda k, j, p: full.at[k, j, p], PARTS_A, PARTS_B))
    four = comm.local(full, out_full)
    three.wait(), four.wait()
    comm.close()


def hidden_exchange(terms, xb):
    return call(hidden_kernel, [((T, 256), F32), ((4, 4, T, 256), BF)],
                [pltpu.VMEM((4, 2, T, 256), BF), pltpu.VMEM((T, 256), BF), pltpu.VMEM((T, 256), F32),
                 pltpu.VMEM((4, 4, T, 256), BF)] + LAND_8, 1, terms, xb)


LAND_16 = [pltpu.VMEM((3, 4, T, 256), BF), pltpu.VMEM((3, T, 256), BF)]


def feed_kernel(back, down, out_b, out_y, bb, yb, full, bf, bn, yf, yn, *sems):
    comm = Comm(*sems)
    place = comm.place
    one, two = comm.local(back, bb), comm.local(down, yb)
    comm.enter(PEERS)
    one.wait(), two.wait()
    run([plane_sum(comm, bb, bf, bn), plane_sum(comm, yb, yf, yn)])
    full[place.x, place.zl] = bb[place.x, place.z]
    three = comm.local(yb.at[place.x, place.z], out_y)
    drain(comm.pair_ring_gather("zl", "x", lambda k, j, p: full.at[k, j, p], PARTS_8,
                                lambda p: full.at[place.x, place.zl, p], full.at[place.x, place.zl], slice(None)))
    four = comm.local(full, out_b)
    three.wait(), four.wait()
    comm.close()


def feed_exchange(back, down):
    return call(feed_kernel, [((4, 2, T, 256), BF), ((T, 256), BF)],
                [pltpu.VMEM((4, 4, T, 256), BF)] * 2 + [pltpu.VMEM((4, 2, T, 256), BF)] + LAND_16 * 2, 2, back, down)


def sum_scratch(n, c):
    return [pltpu.VMEM((2, 4, 2, n, c), BF), pltpu.VMEM((4, 2, n, c), BF)] + [pltpu.VMEM((2, n, c), BF)] * 3 + [pltpu.VMEM((n, c), BF)]


PIECES = [(128, 768)] * CH + [(64, 768), (128, 512), (128, 512), (64, 512), (64, 512)]


def sum_kernel(*refs):
    count = len(PIECES)
    ins, terms = refs[:count], refs[count]
    outs, out_t = refs[count + 1:2 * count + 1], refs[2 * count + 1]
    scratch = refs[2 * count + 2:]
    comm = Comm(*scratch[-3:])
    place = comm.place
    blocks, r0, r1, r2, r3 = scratch[6 * count:6 * count + 5]
    copies = [comm.local(terms, blocks)]
    sets = [scratch[6 * i:6 * i + 6] for i in range(count)]
    for i in range(count):
        copies.append(comm.local(ins[i], sets[i][0]))
    comm.enter(PEERS)
    for copy in copies:
        copy.wait()
    tasks = [wide_sum(comm, *sets[i], PIECES[i][0], i > CH) for i in range(count)]
    run(tasks + [block_sum(comm, blocks, (r0, r1, r2), r3)])
    copies = [comm.local(blocks.at[place.x, place.zl], out_t)]
    for i in range(count):
        own = sets[i][0].at[place.core, place.y, place.zh]
        if i > CH:
            copies.append(comm.local(own, outs[i]))
        else:
            copies.append(comm.local(own, outs[i].at[place.zh]))
            copies.append(comm.local(sets[i][5], outs[i].at[1 - place.zh]))
    for copy in copies:
        copy.wait()
    comm.close()


def sum_exchange(grads, terms):
    shapes = [((n, c) if i > CH else (2, n, c), BF) for i, (n, c) in enumerate(PIECES)] + [((T, 256), BF)]
    scratch = []
    for n, c in PIECES:
        scratch += sum_scratch(n, c)
    scratch += [pltpu.VMEM((4, 2, T, 256), BF)] + LAND_8
    return call(sum_kernel, shapes, scratch, 3, *grads, terms)
EPSILON = 1e-06
MASKED = -1000000000.0


def dot(a, b, ca, cb):
    return lax.dot_general(a, b, (((ca,), (cb,)), ((), ())), preferred_element_type=F32)


def unblock(blocks):
    both = blocks.reshape(8, T, 256)
    pre = both[:, :480].transpose(1, 0, 2).reshape(480, 2048)
    act = both[:, 480:].reshape(8, 64, 2, 128).transpose(2, 1, 0, 3).reshape(128, 1024)
    return pre, act


def unblock16(full):
    pairs = [unblock(full[:, 2 * zh:2 * zh + 2]) for zh in range(2)]
    return jnp.concatenate([p for p, _ in pairs]), jnp.concatenate([a for _, a in pairs])


def block(pre, act):
    low = act.reshape(2, 64, 8, 128).transpose(2, 1, 0, 3).reshape(8, 64, 256)
    top = pre.reshape(480, 8, 256).transpose(1, 0, 2)
    return jnp.concatenate([top, low], axis=1).reshape(4, 2, T, 256)


def block16(pre, act):
    parts = [block(pre[480 * zh:480 * zh + 480], act[128 * zh:128 * zh + 128]) for zh in range(2)]
    return jnp.concatenate(parts, axis=1)


def inv(v):
    return lax.rsqrt(jnp.mean(v * v, axis=1, keepdims=True) + EPSILON)


def norm_back(grad, gain, unit, scale):
    inner = grad * gain
    return scale * (inner - unit * jnp.mean(inner * unit, axis=1, keepdims=True))


def gelu_parts(z):
    a, b = 0.7978845608028654, 0.044715
    t = jnp.tanh(a * (z + b * z * z * z))
    half = 0.5 * (1.0 + t)
    return z * half, half + 0.5 * z * (1.0 - t * t) * a * (1.0 + 3.0 * b * z * z)


def seen(length):
    s = lax.broadcasted_iota(jnp.int32, (304, 304), 0)
    t = lax.broadcasted_iota(jnp.int32, (304, 304), 1)
    live = (t < 192) | ((t >= 240) & (t < 290)) | (t - 192 < length)
    return live & ((t < 240) | (s >= 240))


def soft(q, k, length):
    scores = dot(q, k, 1, 1) * 0.0625
    scores = jnp.where(seen(length), scores, MASKED)
    weights = jnp.exp(scores - jnp.max(scores, axis=1, keepdims=True))
    return weights / jnp.sum(weights, axis=1, keepdims=True)


def hidden_unit(n2, gc, w):
    gate, up, dact = dot(n2, w[:, :256], 1, 0), dot(n2, w[:, 256:512], 1, 0), dot(gc, w[:, 512:], 1, 0)
    value, slope = gelu_parts(gate)
    return (value * up).astype(BF), (dact * up * slope).astype(BF), (dact * value).astype(BF)


def by_core(grad):
    n = grad.shape[0] // 16
    return grad.astype(BF).reshape(4, 2, 2, n, grad.shape[1]).transpose(2, 0, 1, 3, 4)


def local(x_pre, x_act, lengths, cot_pre, cot_act, attn_gain_pre, query_pre, key_pre, value_pre, out_pre, ffn_gain_pre,
          gate_pre, up_pre, down_pre, attn_gain_act, query_act, key_act, value_act, out_act, ffn_gain_act, gate_act,
          up_act, down_act):
    wf, wfa = pack_hidden(gate_pre, up_pre, down_pre), pack_hidden(gate_act, up_act, down_act)[:, 0]
    wq, wqa = jnp.concatenate([query_pre, out_pre.T], axis=1), jnp.concatenate([query_act, out_act.T], axis=1)
    kvs = jnp.concatenate([jnp.concatenate([key_pre, value_pre], axis=1), jnp.concatenate([key_act, value_act], axis=1)])
    kvs = jnp.pad(kvs, ((0, 0), (0, 64)))
    xb, cb = pack_tokens(x_pre, x_act), pack_tokens(cot_pre, cot_act)
    gb = jnp.pad(jnp.stack([attn_gain_pre, ffn_gain_pre, jnp.concatenate([attn_gain_act, ffn_gain_act])]), ((0, 5), (0, 0)))
    f, fa, qo, qoa, kv, kva, x8, c16, g8 = gather_all(wf, wfa, wq, wqa, kvs, xb, cb, gb)
    f, fa = f.reshape(CH, 2048, 768), fa.reshape(1024, 768)
    qo, qoa, kv, kva = qo.reshape(2048, 512), qoa.reshape(1024, 512), kv.reshape(2048, 512), kva.reshape(1024, 512)
    g8 = g8.reshape(8, 8, 256)
    gains = g8[:, 0].reshape(2048), g8[:, 1].reshape(2048), g8[:, 2, :128].reshape(1024), g8[:, 2, 128:].reshape(1024)
    zh = lax.rem(lax.div(lax.axis_index("wide"), 2), 2)
    xp, xa = unblock(x8.astype(F32))
    r1p, r1a = inv(xp), inv(xa)
    u1p, u1a = xp * r1p, xa * r1a
    n1p, n1a = (u1p * gains[0]).astype(BF), (u1a * gains[2]).astype(BF)
    def items(pre, act):
        return [jnp.concatenate([pre[240 * i:240 * i + 240], act[64 * i:64 * i + 64]]) for i in range(2)]
    def split(pair):
        return jnp.concatenate([v[:240] for v in pair]), jnp.concatenate([v[240:] for v in pair])
    q = items(dot(n1p, qo[:, :256], 1, 0).astype(BF), dot(n1a, qoa[:, :256], 1, 0).astype(BF))
    k = items(dot(n1p, kv[:, :256], 1, 0).astype(BF), dot(n1a, kva[:, :256], 1, 0).astype(BF))
    v = items(dot(n1p, kv[:, 256:], 1, 0).astype(BF), dot(n1a, kva[:, 256:], 1, 0).astype(BF))
    probs = [soft(q[i], k[i], lengths[i]) for i in range(2)]
    op, oa = split([dot(probs[i].astype(BF), v[i], 1, 0).astype(BF) for i in range(2)])
    terms = block(dot(op, qo[:, 256:], 1, 1).astype(BF), dot(oa, qoa[:, 256:], 1, 1).astype(BF))
    h_own, h16 = hidden_exchange(terms, xb)
    hp, ha = unblock16(h16.astype(F32))
    r2p, r2a = inv(hp), inv(ha)
    n2p, n2a = (hp * r2p * gains[1]).astype(BF), (ha * r2a * gains[3]).astype(BF)
    gcp, gca = unblock16(c16)
    units = [hidden_unit(n2p, gcp, f[i]) for i in range(CH)]
    ua = hidden_unit(n2a, gca, fa)
    down = sum(dot(units[i][0], f[i, :, 512:], 1, 1) for i in range(CH))
    back = sum(dot(units[i][1], f[i, :, :256], 1, 1) + dot(units[i][2], f[i, :, 256:512], 1, 1) for i in range(CH))
    down_a = dot(ua[0], fa[:, 512:], 1, 1)
    back_a = dot(ua[1], fa[:, :256], 1, 1) + dot(ua[2], fa[:, 256:512], 1, 1)
    b8, y_add = feed_exchange(block16(back.astype(BF), back_a.astype(BF)), block16(down.astype(BF), down_a.astype(BF)))
    grads = [jnp.concatenate([dot(n2p, u[1], 0, 0), dot(n2p, u[2], 0, 0), dot(gcp, u[0], 0, 0)], axis=1) for u in units]
    grads.append(jnp.concatenate([dot(n2a, ua[1], 0, 0), dot(n2a, ua[2], 0, 0), dot(gca, ua[0], 0, 0)], axis=1))
    own = lambda m: lax.dynamic_slice_in_dim(m, zh * (m.shape[0] // 2), m.shape[0] // 2, 0)
    bp, ba = unblock(b8.astype(F32))
    hp, ha, r2p, r2a = own(hp), own(ha), own(r2p), own(r2a)
    dhp = own(gcp).astype(F32) + norm_back(bp, gains[1], hp * r2p, r2p)
    dha = own(gca).astype(F32) + norm_back(ba, gains[3], ha * r2a, r2a)
    ghp, gha = dhp.astype(BF), dha.astype(BF)
    dop, doa = dot(ghp, qo[:, 256:], 1, 0).astype(BF), dot(gha, qoa[:, 256:], 1, 0).astype(BF)
    do = items(dop, doa)
    dq, dk, dv = [], [], []
    for i in range(2):
        low = probs[i].astype(BF)
        dprobs = dot(do[i], v[i], 1, 1)
        dscores = (probs[i] * (dprobs - jnp.sum(probs[i] * dprobs, axis=1, keepdims=True))).astype(BF)
        dq.append((dot(dscores, k[i], 1, 0) * 0.0625).astype(BF))
        dk.append((dot(dscores, q[i], 0, 0) * 0.0625).astype(BF))
        dv.append(dot(low, do[i], 0, 0).astype(BF))
    (dqp, dqa), (dkp, dka), (dvp, dva) = split(dq), split(dk), split(dv)
    grads.append(jnp.concatenate([dot(n1p, dqp, 0, 0), dot(ghp, op, 0, 0)], axis=1))
    grads.append(jnp.concatenate([dot(n1p, dkp, 0, 0), dot(n1p, dvp, 0, 0)], axis=1))
    grads.append(jnp.concatenate([dot(n1a, dqa, 0, 0), dot(gha, oa, 0, 0)], axis=1))
    grads.append(jnp.concatenate([dot(n1a, dka, 0, 0), dot(n1a, dva, 0, 0)], axis=1))
    dn1p = dot(dqp, qo[:, :256], 1, 1) + dot(dkp, kv[:, :256], 1, 1) + dot(dvp, kv[:, 256:], 1, 1)
    dn1a = dot(dqa, qoa[:, :256], 1, 1) + dot(dka, kva[:, :256], 1, 1) + dot(dva, kva[:, 256:], 1, 1)
    *sums, d1 = sum_exchange([by_core(g) for g in grads], block(dn1p.astype(BF), dn1a.astype(BF)))
    narrow = lax.axis_index("narrow")
    def slab(pre, act):
        p = lax.dynamic_slice_in_dim(pre, narrow * 256, 256, 1)
        a = lax.dynamic_slice_in_dim(act, narrow * 128, 128, 1)
        return p, a
    d1p, d1a = d1[:480].astype(F32), d1[480:].astype(F32).reshape(64, 2, 128).transpose(1, 0, 2).reshape(128, 128)
    xps, xas = slab(u1p, u1a)
    dhps, dhas = slab(dhp - own(gcp).astype(F32), dha - own(gca).astype(F32))
    dhps = dhps + cot_pre.reshape(480, 256)
    dhas = dhas + jnp.pad(cot_act, ((0, 0), (0, 14), (0, 0))).reshape(128, 128)
    innp, inna = d1p * attn_gain_pre, d1a * attn_gain_act
    meanp, meana = lax.psum((jnp.sum(innp * xps, axis=1, keepdims=True), jnp.sum(inna * xas, axis=1, keepdims=True)), "narrow")
    gxp = dhps + r1p * (innp - xps * (meanp / 2048))
    gxa = dhas + r1a * (inna - xas * (meana / 1024))
    u2ps, u2as = slab(hp * r2p, ha * r2a)
    b2ps, b2as = slab(bp, ba)
    gg = lax.psum((jnp.sum(d1p * xps, axis=0), jnp.sum(b2ps * u2ps, axis=0), jnp.sum(d1a * xas, axis=0), jnp.sum(b2as * u2as, axis=0)), "wide")
    y = h_own + y_add.astype(F32)
    unact = lambda m: m.reshape(64, 2, 128)[:50].transpose(1, 0, 2)
    yp, ya = y[:480].reshape(2, 240, 256).astype(BF), unact(y[480:]).astype(BF)
    def open_hidden(m, n):
        m = m.astype(F32).reshape(2, -1, n, 768).transpose(2, 0, 1, 3)
        gate, up, down = (m[..., 256 * j:256 * j + 256].reshape(n, -1) for j in range(3))
        return gate, up, down.T
    fg = jnp.stack(sums[:CH], axis=1)
    dgate_p, dup_p, ddown_p = open_hidden(fg, 128)
    dgate_a, dup_a, ddown_a = open_hidden(sums[CH], 64)
    qp, kvp, qa, kva_ = (m.astype(F32) for m in sums[CH + 1:CH + 5])
    def kv_share(a, b):
        both = jnp.concatenate([a, b])
        both = both.reshape(192, 2, 8, 32).astype(BF)
        s = lax.psum_scatter(both, "narrow", scatter_dimension=2).astype(F32)
        return s[:128, 0], s[:128, 1], s[128:, 0], s[128:, 1]
    dkey_p, dval_p, dkey_a, dval_a = kv_share(kvp, kva_)
    return (yp, ya, gxp.reshape(2, 240, 256), gxa.reshape(2, 64, 128)[:, :50], gg[0], qp[:, :256], dkey_p, dval_p,
            qp[:, 256:].T, gg[1], dgate_p, dup_p, ddown_p, gg[2], qa[:, :256], dkey_a, dval_a, qa[:, 256:].T, gg[3],
            dgate_a, dup_a, ddown_a)


def solution(mesh):
    tok, row, col, vec = P("wide", None, "narrow"), P("wide", "narrow"), P("narrow", "wide"), P("narrow")
    expert = (vec, row, row, row, col, vec, row, row, col)
    return jax.shard_map(
        local, mesh=mesh, in_specs=(tok, tok, P("wide"), tok, tok) + expert + expert,
        out_specs=(tok,) * 4 + expert + expert, check_vma=False)
```

time: 2850 us -> 802 us (0.28)
  waiting for transfers between devices: 1650 us -> 0.02 us
  blocking collectives: 822 us -> 54.3 us
  Pallas kernels: 0 us -> 374 us
  matrix products: 230 us -> 181 us
  local copies, waits for them, and re-layouts: 65.3 us -> 98.3 us
    reduce_scatter x24 -> x0, waiting for transfers between devices: 921 us -> none  [the longest x4 171 us: collect_branch(): lax.psum_scatter(prefix_rows, 'narrow', scatter_dimension=2, tiled=True)]
    all_gather x26 -> x0, blocking collectives: 715 us -> none  [the longest x4 140 us: spread_grads(): lax.all_gather(prefix_rows, 'narrow', axis=2, tiled=True)]
    unnamed x46 -> x2, waiting for transfers between devices: 464 us -> 0.02 us
    pallas_call x0 -> x4, Pallas kernels: none -> 374 us  [the longest x3 249 us: call(): pl.pallas_call(kernel, out_shape=[jax.ShapeDtypeStruct(s, d) for s, d in...]
    all_gather x8 -> x0, waiting for transfers between devices: 270 us -> none  [the longest x1 72.8 us: local(): lax.all_gather(down_pre, 'wide', axis=1, tiled=True)]
    psum x5 -> x2, blocking collectives: 107 us -> 54.3 us  [the longest x1 36.2 us: local(): lax.psum((jnp.sum(d1p * xps, axis=0), jnp.sum(b2ps * u2ps, axis=0), jnp.s...]
    dot_general x96 -> x81, matrix products: 230 us -> 181 us  [dot(): lax.dot_general(a, b, (((ca,), (cb,)), ((), ())), preferred_element_type=...]
  transfers between devices with their start and end apart: 39 -> 1, of which waited for: 31 -> 0; matrix products, arithmetic and copies ran while one was open for 11% -> 4% of each run, Pallas kernels for 0% -> 0%
where the time goes in v1:
time: 802 us; the launch traced here: 791 us
  Pallas kernels  374 us (47%)
  matrix products  181 us (23%)
  local copies, waits for them, and re-layouts  98.3 us (12%)
  other arithmetic  66.5 us (8%)
  blocking collectives  54.3 us (7%)
  between operations  17.2 us (2%)
    pallas_call x3, Pallas kernels, call(): pl.pallas_call(kernel, out_shape=[jax.ShapeDtypeStruct(s, d) for s, d in...  249 us
    dot_general x81, matrix products, dot(): lax.dot_general(a, b, (((ca,), (cb,)), ((), ())), preferred_element_type=...  181 us
    pallas_call x1, Pallas kernels, gather_all(): pl.pallas_call(gather_kernel, out_shape=[jax.ShapeDtypeStruct(s, BF) for...  126 us
    unnamed x375, local copies, waits for them, and re-layouts  38.6 us
    psum x1, blocking collectives, local(): lax.psum((jnp.sum(d1p * xps, axis=0), jnp.sum(b2ps * u2ps, axis=0), jnp.s...  36.2 us
    psum x1, blocking collectives, local(): lax.psum((jnp.sum(innp * xps, axis=1, keepdims=True), jnp.sum(inna * xas,...  18.2 us
  transfers between devices with their start and end apart: 1, of which 0 were waited for; matrix products, arithmetic and copies ran while one was open for 4% of the time, Pallas kernels for 0%

profile of v1, /device:TPU:0, one launch (start us, length us, event | category | flops | bytes accessed | tf_op | source)
XLA Modules:
  0.0 791.4 jit_solution(1349895520250601656)
XLA Ops:
  18.9 125.8 %shard_map.390 = (bf16[4,4,2,2,128,768]{5,4,3,2,1,0:T(8,128)(2,1)}, bf16[4,2,2,64,768]{4,3,2,1,0:T(8,128)(2,1)}, bf16[4,2,2,128,512]{4,3,2,1,0:T(8,128)(2,1)}, b...) custom-call(bf16[2,4,128,768]{3,2,1,0:T(8,128)(2,1)} %maximum_bitcas, ...), custom_call_target="tpu_custom_call" | custom-call | tf_op jit(solution)/shard_map/pallas_call | solution.py:299
  170.0 70.1 %shard_map.391 = (f32[544,256]{1,0:T(8,128)}, bf16[4,4,544,256]{3,2,1,0:T(8,128)(2,1)}) custom-call(bf16[4,2,544,256]{3,2,1,0:T(8,128)(2,1)} %pad_maximum_fusion.4.terms, bf16[544,256]{1,0:T(8,128)(2,1)} %pad_maximum_fusion.7.xb), custom_call_target="tpu_custom_call" | custom-call | tf_op jit(solution)/shard_map/pallas_call | solution.py:394
  281.2 4.8 multiply_convert_fusion.6
  289.6 4.4 fusion.28
  294.0 4.3 fusion.52
  300.6 4.4 fusion.53
  310.3 4.4 fusion.27
  317.1 4.3 fusion.44
  324.0 4.4 fusion.45
  333.7 4.3 fusion.26
  340.4 4.5 fusion.36
  347.2 4.4 fusion.37
  357.1 4.4 fusion.29
  375.7 4.5 convolution_convert_fusion.3
  380.2 18.6 %add_convert_fusion.1 = bf16[960,2048]{1,0:T(8,128)(2,1)S(1)} fusion(f32[960,2048]{1,0:T(8,128)} %fusion.29, f32[960,2048]{1,0:T(8,128)} %fusion.37, f32[960,2048]{1,0:T(8,128)} %fusion.36, f32[960,2048]{1,0:T(8,128)} %fusion.45, f32[960,2048]{1,0:T(8,128)} %fusion.44, f32[960,2048]{1,0:T(8,128)} %fusion.53, f32[960,2048]{1,0:T(8,128)} %fusion.52, ...), kind=kOutput, calls=%fused_computation.1 | convolution fusion | flops 1022361600 | bytes 60522496 | tf_op jit(solution)/shard_map/dot_general | solution.py:502
  406.0 4.5 convolution_convert_fusion.2
  410.5 9.4 %add_convert_fusion = bf16[960,2048]{1,0:T(8,128)(2,1)S(1)} fusion(f32[960,2048]{1,0:T(8,128)} %fusion.26, f32[960,2048]{1,0:T(8,128)} %fusion.28, f32[960,2048]{1,0:T(8,128)} %fusion.27, bf16[960,256]{1,0:T(8,128)(2,1)S(1)} %copy-done.72, bf16[4,2048,768]{2,1,0:T(8,128)(2,1)} %bitcast.462), kind=kOutput, calls=%fused_computation | convolution fusion | flops 1014497280 | bytes 29065216 | tf_op jit(solution)/shard_map/dot_general | solution.py:502
  431.5 76.3 %shard_map.392 = (bf16[4,2,544,256]{3,2,1,0:T(8,128)(2,1)}, bf16[544,256]{1,0:T(8,128)(2,1)}) custom-call(bf16[4,4,544,256]{3,2,1,0:T(8,128)(2,1)} %maximum_maximum_fusion.back, bf16[4,4,544,256]{3,2,1,0:T(8,128)(2,1)} %maximum_maximum_fusion.1.down), custom_call_target="tpu_custom_call" | custom-call | tf_op jit(solution)/shard_map/pallas_call | solution.py:394
  513.3 4.7 copy.446
  518.1 4.1 multiply_reduce_fusion.1
  565.0 4.4 add_convert_fusion.2
  588.7 102.2 %shard_map.393 = (bf16[2,128,768]{2,1,0:T(8,128)(2,1)}, bf16[2,128,768]{2,1,0:T(8,128)(2,1)}, bf16[2,128,768]{2,1,0:T(8,128)(2,1)}, bf16[2,128,768]{2,1,0:T(8,12...) custom-call(bf16[2,4,2,128,768]{4,3,2,1,0:T(8,128)(2,1)} %copy_bitca, ...), custom_call_target="tpu_custom_call" | custom-call | tf_op jit(solution)/shard_map/pallas_call | solution.py:394
  707.4 18.2 %all-reduce.7 = (f32[480,1]{0,1:T(1,128)S(1)}, f32[128,1]{0,1:T(1,128)S(1)}) all-reduce(f32[480,1]{0,1:T(1,128)S(1)} %bitcast.628, f32[128,1]{0,1:T(1,128)S(1)} %bitcast.631), channel_id=1, replica_groups=mesh['wide'=16,'narrow'=8] {'narrow'}, use_global_device_ids=true, to_apply=%region_13.14 | all-reduce | flops 608 | bytes 4864 | tf_op jit(solution)/shard_map/psum | solution.py:647
  744.7 36.2 %all-reduce.6 = (f32[256]{0:T(256)}, f32[256]{0:T(256)}, f32[128]{0:T(128)}, f32[128]{0:T(128)}) all-reduce(f32[256]{0:T(256)S(1)} %copy-done.145, f32[256]{0:T(256)S(1)} %copy-done.146, f32[128]{0:T(128)S(1)} %copy-done.149, f32[128]{0:T(128)S(1)} %copy-done.150), channel_id=1, replica_groups=mesh['wide'=16,'narrow'=8] {'wide'}, use_global_device_ids=true, to_apply=%region_17.18 | all-reduce | flops 768 | bytes 6144 | tf_op jit(solution)/shard_map/psum | solution.py:652
  (630 shorter events, 246.8 us)
Async XLA Ops:
  7.3 6.8 copy-start.84
  7.4 774.1 %all-reduce.10.cloned.1.call-start = ((), (), s32[]{:S(2)}) async-start(), calls=%async_computation | async-start | bytes 524288
  8.8 6.8 copy-start.143
  8.8 6.8 copy-start.153
  147.0 114.3 %copy-start.88 = (f32[8,1,256]{2,1,0:T(1,128)}, f32[8,1,256]{2,1,0:T(1,128)S(1)}, u32[]{:S(2)}) copy-start(f32[8,1,256]{2,1,0:T(1,128)S(1)} %get-tuple-element.247) | copy-start | bytes 24580
  250.0 11.4 %copy-start = (f32[960,2048]{1,0:T(8,128)}, f32[960,2048]{1,0:T(8,128)S(1)}, u32[]{:S(2)}) copy-start(f32[960,2048]{1,0:T(8,128)S(1)} %constant_dynamic-update-slice_fusion.2) | copy-start | bytes 23592964
  250.0 6.6 slice-start.2
  250.6 10.8 %copy-start.123 = (f32[960]{0:T(1024)}, f32[960]{0:T(1024)S(1)}, u32[]{:S(2)}) copy-start(f32[960]{0:T(1024)S(1)} %add_rsqrt_fusion.1) | copy-start | bytes 11524
  262.1 14.8 %copy-start.19 = (bf16[960,2048]{1,0:T(8,128)(2,1)}, bf16[960,2048]{1,0:T(8,128)(2,1)S(1)}, u32[]{:S(2)}) copy-start(bf16[960,2048]{1,0:T(8,128)(2,1)S(1)} %multiply_convert_fusion) | copy-start | bytes 11796484
  264.5 14.5 %copy-start.6 = (bf16[960,2048]{1,0:T(8,128)(2,1)}, bf16[960,2048]{1,0:T(8,128)(2,1)S(1)}, u32[]{:S(2)}) copy-start(bf16[960,2048]{1,0:T(8,128)(2,1)S(1)} %constant_dynamic-update-slice_fusion) | copy-start | bytes 11796484
  281.1 7.4 slice-start.3
  281.1 7.4 slice-start.4
  518.1 6.8 copy-start.8
  588.7 104.0 %copy-start.82 = (bf16[544,256]{1,0:T(8,128)(2,1)S(1)}, bf16[544,256]{1,0:T(8,128)(2,1)}, u32[]{:S(2)}) copy-start(bf16[544,256]{1,0:T(8,128)(2,1)} %get-tuple-element.56) | copy-start | bytes 835588
  694.6 7.7 copy-start.67
  694.6 9.6 %copy-start.128 = (f32[256]{0:T(256)S(1)}, f32[256]{0:T(256)}, u32[]{:S(2)}) copy-start(f32[256]{0:T(256)} %param.28) | copy-start | bytes 3076
  694.6 11.3 %copy-start.144 = (f32[128]{0:T(128)S(1)}, f32[128]{0:T(128)}, u32[]{:S(2)}) copy-start(f32[128]{0:T(128)} %param.37) | copy-start | bytes 1540
  698.7 28.3 %copy-start.148 = (f32[128]{0:T(128)S(1)}, f32[128]{0:T(128)}, u32[]{:S(2)}) copy-start(f32[128]{0:T(128)} %copy-done.147) | copy-start | bytes 1540
  698.7 32.1 %copy-start.74 = (bf16[2,128,768]{2,1,0:T(8,128)(2,1)S(1)}, bf16[2,128,768]{2,1,0:T(8,128)(2,1)}, u32[]{:S(2)}) copy-start(bf16[2,128,768]{2,1,0:T(8,128)(2,1)} %get-tuple-element.62) | copy-start | bytes 1179652
  698.7 32.1 %copy-start.75 = (bf16[2,128,768]{2,1,0:T(8,128)(2,1)S(1)}, bf16[2,128,768]{2,1,0:T(8,128)(2,1)}, u32[]{:S(2)}) copy-start(bf16[2,128,768]{2,1,0:T(8,128)(2,1)} %get-tuple-element.63) | copy-start | bytes 1179652
  738.0 6.7 copy-start.145
  738.0 6.7 copy-start.146
  738.0 6.7 copy-start.149
  738.0 6.7 copy-start.150
  (147 other events, 509.9 us)
Sparse Core Ops, SparseCore 0:
  692.8 73.4 all-reduce.9

commit v2 on v1

v2 whole, which is shorter than its diff:
```python
import functools
import jax
import jax.numpy as jnp
from jax import lax
from jax.experimental import pallas as pl
from jax.experimental.pallas import tpu as pltpu
from jax.sharding import PartitionSpec as P

MESH = pl.DeviceIdType.MESH
BF = jnp.bfloat16
F32 = jnp.float32
SEMS = 256
VMEM_CAP = 62 * 1024 * 1024


class Place:
    def __init__(self):
        wide, narrow = lax.axis_index("wide"), lax.axis_index("narrow")
        self.core = lax.rem(wide, 2)
        self.zh = lax.rem(lax.div(wide, 2), 2)
        self.y = lax.div(wide, 4)
        self.zl = lax.rem(narrow, 2)
        self.x = lax.div(narrow, 2)
        self.z = self.zh * 2 + self.zl

    def wide_at(self, y, zh, core):
        return (y * 2 + zh) * 2 + core

    def coord(self, axis):
        return {"x": self.x, "y": self.y, "z": self.z}[axis]

    def off(self, axis, step):
        return lax.rem(self.coord(axis) + step + 4, 4)

    def peer(self, name):
        if name == "sib":
            return {"wide": self.wide_at(self.y, self.zh, 1 - self.core)}
        if name == "z2":
            return {"wide": self.wide_at(self.y, 1 - self.zh, self.core)}
        if name == "zl":
            return {"narrow": self.x * 2 + 1 - self.zl}
        axis, step = name[0], 1 if name[1] == "+" else -1
        at = self.off(axis, step)
        if axis == "y":
            return {"wide": self.wide_at(at, self.zh, self.core)}
        if axis == "x":
            return {"narrow": at * 2 + self.zl}
        return {"wide": self.wide_at(self.y, lax.div(at, 2), self.core), "narrow": self.x * 2 + lax.rem(at, 2)}


class Link:
    def __init__(self, out, into):
        self.out, self.into = out, into

    def arrive(self):
        self.into.wait_recv()

    def left(self):
        self.out.wait_send()


class Comm:
    def __init__(self, send_sems, recv_sems, local_sems):
        self.place = Place()
        self.send_sems, self.recv_sems, self.local_sems = send_sems, recv_sems, local_sems
        self.count, self.local_count = 0, 0
        self.links = []

    def enter(self, peers):
        barrier = pltpu.get_barrier_semaphore()
        for name in peers:
            pl.semaphore_signal(barrier, inc=1, device_id=self.place.peer(name), device_id_type=MESH)
        pl.semaphore_wait(barrier, len(peers))

    def send(self, src, dst, name, incoming):
        index = self.count
        self.count += 1
        make = lambda to: pltpu.make_async_remote_copy(
            src_ref=src, dst_ref=to, send_sem=self.send_sems.at[index], recv_sem=self.recv_sems.at[index],
            device_id=self.place.peer(name), device_id_type=MESH)
        out = make(dst)
        out.start()
        link = Link(out, make(incoming))
        self.links.append(link)
        return link

    def local(self, src, dst):
        index = self.local_count
        self.local_count += 1
        copy = pltpu.make_async_copy(src, dst, self.local_sems.at[index])
        copy.start()
        return copy

    def settle(self):
        for link in self.links:
            link.left()
        self.links = []

    def close(self):
        self.settle()

    def ring_gather(self, axis, view, parts, own=None):
        place = self.place
        at = lambda step: place.off(axis, step)
        src = own if own is not None else (lambda part: view(at(0), part))
        plus = [self.send(src(p), view(at(0), p), axis + "+", view(at(-1), p)) for p, _ in parts]
        minus = [self.send(src(p), view(at(0), p), axis + "-", view(at(1), p)) for p, _ in parts]
        yield
        far = []
        for (p, way), up in zip(parts, plus):
            up.arrive()
            if way > 0:
                far.append(self.send(view(at(-1), p), view(at(-1), p), axis + "+", view(at(-2), p)))
        for (p, way), down in zip(parts, minus):
            down.arrive()
            if way < 0:
                far.append(self.send(view(at(1), p), view(at(1), p), axis + "-", view(at(2), p)))
        yield
        for link in far:
            link.arrive()

    def pair_ring_gather(self, pair, axis, view, parts, own, give, whole):
        place = self.place
        mine = {"z2": place.zh, "zl": place.zl}[pair]
        here = place.coord(axis)
        swap = self.send(give, view(here, mine, whole), pair, view(here, 1 - mine, whole))
        first = self.ring_gather(axis, lambda k, p: view(k, mine, p), parts, own)
        next(first)
        yield
        swap.arrive()
        second = self.ring_gather(axis, lambda k, p: view(k, 1 - mine, p), parts)
        next(second)
        yield
        next(first)
        yield
        next(second)
        yield
        drain(first)
        drain(second)

    def plane_gather(self, view, parts_x, parts_z):
        place = self.place
        every = slice(None)
        ax = self.ring_gather("x", lambda k, p: view(k, place.z, p), parts_x)
        bz = self.ring_gather("z", lambda k, p: view(place.x, k, p), parts_z)
        next(ax), next(bz)
        yield
        next(ax), next(bz)
        yield
        drain(ax)
        az = self.ring_gather("z", lambda k, p: view(every, k, p), parts_x)
        next(az)
        drain(bz)
        bx = self.ring_gather("x", lambda k, p: view(k, every, p), parts_z)
        next(bx)
        yield
        next(az), next(bx)
        yield
        drain(az), drain(bx)

    def ring_sum(self, axis, view, parts, relay, plus, minus):
        place = self.place
        at = lambda step: place.off(axis, step)
        far = []
        for p, way in parts:
            far.append(self.send(view(at(2), p), relay(p), axis + ("+" if way > 0 else "-"), relay(p)))
        yield
        ups, downs = [], []
        for (p, way), link in zip(parts, far):
            link.arrive()
            add_to(view(at(way), p), relay(p))
            if way > 0:
                ups.append(self.send(view(at(1), p), plus(p), axis + "+", plus(p)))
            else:
                downs.append(self.send(view(at(-1), p), minus(p), axis + "-", minus(p)))
        for p, way in parts:
            if way > 0:
                downs.append(self.send(view(at(-1), p), minus(p), axis + "-", minus(p)))
            else:
                ups.append(self.send(view(at(1), p), plus(p), axis + "+", plus(p)))
        yield
        for link in ups + downs:
            link.arrive()
        for p, _ in parts:
            add_to(view(at(0), p), plus(p), minus(p))


def add_to(ref, *others):
    total = ref[...].astype(F32)
    for other in others:
        total = total + other[...].astype(F32)
    ref[...] = total.astype(ref.dtype)


def drain(task):
    for _ in task:
        pass


def rows(lo, hi):
    return pl.ds(lo, hi - lo)
T = 544
CH = 4


def halves(n):
    return [(rows(0, n // 2), 1), (rows(n // 2, n), -1)]


PARTS_8 = [(rows(0, 272), 1), (rows(272, 544), -1)]
PARTS_A = [(rows(0, 144), 1), (rows(144, 272), -1)]
PARTS_B = [(rows(272, 416), 1), (rows(416, 544), -1)]
PEERS = ("y+", "y-", "z2", "sib", "x+", "x-", "z+", "z-")


def wide_gather(comm, out, own, give, n, parts=None):
    place = comm.place
    core = place.core
    copy = comm.local(own, out.at[place.y, place.zh, core])
    task = comm.pair_ring_gather(
        "z2", "y", lambda k, j, p: out.at[k, j, core, p], parts or halves(n),
        lambda p: own.at[p], give, slice(None))
    yield from task
    copy.wait()
    link = comm.send(out.at[:, :, core], out.at[:, :, core], "sib", out.at[:, :, 1 - core])
    yield
    link.arrive()


def block_gather(comm, out, own, parts):
    place = comm.place
    copy = comm.local(own, out.at[place.x, place.zl])
    yield from comm.pair_ring_gather(
        "zl", "x", lambda k, j, p: out.at[k, j, p], parts, lambda p: own.at[p], own, slice(None))
    copy.wait()


def plane_spread(comm, out, own):
    place = comm.place
    copy = comm.local(own, out.at[place.x, place.z])
    copy.wait()
    yield from comm.plane_gather(lambda k, j, p: out.at[k, j, p], PARTS_A, PARTS_B)


def pack_hidden(gate, up, down):
    n, hidden = gate.shape
    cut = lambda m: m.reshape(n, 2, hidden // 512, 256)
    return jnp.concatenate([cut(gate), cut(up), cut(down.T)], axis=-1).transpose(1, 2, 0, 3)


def pack_tokens(pre, act):
    low = jnp.concatenate([act[0], act[1]], axis=1)
    low = jnp.pad(low, ((0, 14), (0, 0)))
    return jnp.concatenate([pre.reshape(480, 256), low], axis=0)
def loop_add(ref, n, *others):
    def step(i, carry):
        add_to(ref.at[i], *[other.at[i] for other in others])
        return carry
    lax.fori_loop(0, n, step, 0)


def block_sum(comm, blocks, lands, swap, parts=PARTS_8):
    place = comm.place
    relay, plus, minus = lands
    yield from comm.ring_sum(
        "x", lambda k, p: blocks.at[k, :, p], parts,
        lambda p: relay.at[:, p], lambda p: plus.at[:, p], lambda p: minus.at[:, p])
    link = comm.send(blocks.at[place.x, 1 - place.zl], swap, "zl", swap)
    yield
    link.arrive()
    add_to(blocks.at[place.x, place.zl], swap)


def plane_sum(comm, blocks, lands_far, lands_near):
    place = comm.place
    az = comm.ring_sum("z", lambda k, p: blocks.at[:, k, p], PARTS_A,
                       lambda p: lands_far.at[0, :, p], lambda p: lands_far.at[1, :, p], lambda p: lands_far.at[2, :, p])
    bx = comm.ring_sum("x", lambda k, p: blocks.at[k, :, p], PARTS_B,
                       lambda p: lands_far.at[0, :, p], lambda p: lands_far.at[1, :, p], lambda p: lands_far.at[2, :, p])
    next(az), next(bx)
    yield
    next(az), next(bx)
    yield
    drain(az)
    ax = comm.ring_sum("x", lambda k, p: blocks.at[k, place.z, p], PARTS_A,
                       lambda p: lands_near.at[0, p], lambda p: lands_near.at[1, p], lambda p: lands_near.at[2, p])
    next(ax)
    drain(bx)
    bz = comm.ring_sum("z", lambda k, p: blocks.at[place.x, k, p], PARTS_B,
                       lambda p: lands_near.at[0, p], lambda p: lands_near.at[1, p], lambda p: lands_near.at[2, p])
    next(bz)
    yield
    next(ax), next(bz)
    yield
    drain(ax), drain(bz)


def wide_sum(comm, grad, half, relay, plus, minus, swap, n, add):
    place = comm.place
    core, zh = place.core, place.zh
    link = comm.send(grad.at[1 - core], half, "sib", half)
    yield
    link.arrive()
    loop_add(grad.at[core], 4, half)
    yield from comm.ring_sum(
        "y", lambda k, p: grad.at[core, k, :, p], halves(n),
        lambda p: relay.at[:, p], lambda p: plus.at[:, p], lambda p: minus.at[:, p])
    link = comm.send(grad.at[core, place.y, 1 - zh], swap, "z2", swap)
    yield
    link.arrive()
    if add:
        add_to(grad.at[core, place.y, zh], swap)


SEM_SCRATCH = [pltpu.SemaphoreType.DMA((SEMS,)), pltpu.SemaphoreType.DMA((SEMS,)), pltpu.SemaphoreType.DMA((32,))]
ANY = pl.BlockSpec(memory_space=pl.ANY)


LAND_8 = [pltpu.VMEM((2, T, 256), BF)] * 3 + [pltpu.VMEM((T, 256), BF)]


LAND_16 = [pltpu.VMEM((3, 4, T, 256), BF), pltpu.VMEM((3, T, 256), BF)]


EPSILON = 1e-06
MASKED = -1000000000.0
KEYS = 384


def dot(a, b, ca, cb):
    return lax.dot_general(a, b, (((ca,), (cb,)), ((), ())), preferred_element_type=F32)


_open = []


def mark(name):
    if _open:
        _open.pop().__exit__(None, None, None)
    if name:
        scope = jax.named_scope(name)
        scope.__enter__()
        _open.append(scope)


def pump(*tasks):
    for task in tasks:
        next(task, None)


def seen(length):
    s = lax.broadcasted_iota(jnp.int32, (304, KEYS), 0)
    t = lax.broadcasted_iota(jnp.int32, (304, KEYS), 1)
    live = (t < 192) | ((t >= 240) & (t < 290)) | ((t < 240) & (t - 192 < length))
    return live & ((t < 240) | (s >= 240))


def soft(q, k, length):
    scores = dot(q, k, 1, 1) * 0.0625
    scores = jnp.where(seen(length), scores, MASKED)
    weights = jnp.exp(scores - jnp.max(scores, axis=1, keepdims=True))
    return weights / jnp.sum(weights, axis=1, keepdims=True)


def pairs8():
    return [(x, zl) for x in range(4) for zl in range(2)]


def norm_block_rows(get, gain, width, put):
    total = sum(jnp.sum(get(n) * get(n), axis=1, keepdims=True) for n in range(8))
    scale = lax.rsqrt(total / (8 * width) + EPSILON)
    for n in range(8):
        put(n, (get(n) * scale * gain(n)).astype(BF))
    return scale


def attend_kernel(lens, wf, wfa, wq, wqa, kvs, xb, cb, gb,
                  out_f, out_fa, out_q, out_qa, out_kv, out_kva, out_c, out_g, out_n1p, out_n1a, out_qkvo, out_r1,
                  out_h, out_h16, out_n2p, out_n2a, out_r2,
                  kv8, kvf, qo, qoa, kv, kva, x8, c16, g8, n1p, n1a, qkvo, r1, xv, hv, full, n2p, n2a, r2,
                  blocks, l0, l1, l2, l3, *sems):
    comm = Comm(*sems)
    place = comm.place
    zh = place.zh
    first = comm.local(xb, xv)
    zero = jnp.zeros((KEYS - 304, 256), BF)
    for i in range(2):
        for j in (1, 2):
            qkvo[j, i, 304:KEYS, :] = zero
    comm.enter(PEERS)

    mark('start')
    kv_task = block_gather(comm, kv8, kvs, halves(192))
    g_task = block_gather(comm, g8, gb, [(slice(None), 1)])
    x_task = block_gather(comm, x8, xb, PARTS_8)
    q_tasks = [wide_gather(comm, qo, wq, wq, 128), wide_gather(comm, qoa, wqa, wqa, 64)]
    f_tasks = [wide_gather(comm, out_f.at[i], wf.at[zh, i], wf.at[1 - zh, i], 128) for i in range(CH)]
    f_tasks.append(wide_gather(comm, out_fa, wfa.at[zh], wfa.at[1 - zh], 64))
    c_task = plane_spread(comm, c16, cb)
    pump(kv_task, x_task, *q_tasks, g_task)
    pump(kv_task, g_task), pump(kv_task, g_task), drain(kv_task)
    total = jnp.zeros((192, 512), F32)
    lane = lax.broadcasted_iota(jnp.int32, (128, 512), 0)
    col = lax.broadcasted_iota(jnp.int32, (128, 512), 1)
    for n in range(8):
        pick = ((lane < 32) & (col == 32 * n + lane)) | ((lane >= 32) & (lane < 64) & (col == 224 + 32 * n + lane))
        total = total + dot(kv8[n // 2, n % 2], pick.astype(F32).astype(BF), 1, 0)
    kvf[...] = total.astype(BF)
    kv_a, kv_b = kvf.at[0:128], kvf.at[128:192]
    kv_tasks = [wide_gather(comm, kv, kv_a, kv_a, 128), wide_gather(comm, kva, kv_b, kv_b, 64)]
    pump(*kv_tasks)
    pump(x_task, *q_tasks)
    pump(f_tasks[0], f_tasks[1])
    pump(*kv_tasks)
    pump(*q_tasks)
    pump(x_task)
    pump(*q_tasks)
    pump(*kv_tasks)
    pump(f_tasks[0], f_tasks[2], f_tasks[3], f_tasks[4])
    pump(*q_tasks)
    pump(x_task)
    pump(*kv_tasks)
    mark('xwait')
    drain(g_task)
    drain(x_task)
    pump(c_task)

    mark('norm1')
    for i in range(2):
        here = pl.ds(240 * i, 240)
        get = lambda n: x8[n // 2, n % 2, here, :].astype(F32)
        def put(n, v):
            n1p[here, 256 * n:256 * n + 256] = v
        r1[here, :] = jnp.broadcast_to(norm_block_rows(get, lambda n: g8[n // 2, n % 2, 0:1, :], 256, put), (240, 128))
        low = pl.ds(480, 64)
        get = lambda n: x8[n // 2, n % 2, low, 128 * i:128 * i + 128].astype(F32)
        def put(n, v):
            n1a[64 * i:64 * i + 64, 128 * n:128 * n + 128] = v
        r1[480 + 64 * i:544 + 64 * i, :] = jnp.broadcast_to(
            norm_block_rows(get, lambda n: g8[n // 2, n % 2, 2:3, 0:128], 128, put), (64, 128))
    for task in q_tasks:
        drain(task)
    pump(f_tasks[1])
    mark('qkv')
    def queries(i, carry):
        here = pl.ds(pl.multiple_of(240 * i, 16), 240)
        qkvo[0, i, 0:240, :] = dot(n1p[here, :], qo[:, :, :, :, 0:256].reshape(2048, 256), 1, 0).astype(BF)
        return carry
    lax.fori_loop(0, 2, queries, 0)
    for task in kv_tasks:
        drain(task)
    def keys(i, carry):
        here = pl.ds(pl.multiple_of(240 * i, 16), 240)
        for j in range(2):
            qkvo[1 + j, i, 0:240, :] = dot(
                n1p[here, :], kv[:, :, :, :, 256 * j:256 * j + 256].reshape(2048, 256), 1, 0).astype(BF)
        return carry
    lax.fori_loop(0, 2, keys, 0)
    low = [dot(n1a[...], qoa[:, :, :, :, 0:256].reshape(1024, 256), 1, 0).astype(BF)]
    for j in range(2):
        low.append(dot(n1a[...], kva[:, :, :, :, 256 * j:256 * j + 256].reshape(1024, 256), 1, 0).astype(BF))
    for i in range(2):
        for j in range(3):
            qkvo[j, i, 240:304, :] = low[j][64 * i:64 * i + 64]
    saves = [comm.local(qo, out_q), comm.local(qoa, out_qa), comm.local(kv, out_kv), comm.local(kva, out_kva),
             comm.local(n1p, out_n1p), comm.local(n1a, out_n1a), comm.local(r1, out_r1), comm.local(g8, out_g)]
    pump(c_task, f_tasks[2])
    mark('attn')
    for i in range(2):
        probs = soft(qkvo[0, i, 0:304, :], qkvo[1, i], lens[i])
        qkvo[3, i, 0:304, :] = dot(probs.astype(BF), qkvo[2, i], 1, 0).astype(BF)
    saves.append(comm.local(qkvo, out_qkvo))
    pump(f_tasks[3], f_tasks[0])
    mark('outproj')
    oa = jnp.concatenate([qkvo[3, 0, 240:304, :], qkvo[3, 1, 240:304, :]], axis=0)

    def terms(step):
        k = place.off("x", step)
        for j in range(2):
            weight = qo[k, j, :, :, 256:512].reshape(256, 256)
            for i in range(2):
                blocks[k, j, 240 * i:240 * i + 240, :] = dot(qkvo[3, i, 0:240, :], weight, 1, 1).astype(BF)
            small = dot(oa, qoa[k, j, :, :, 256:512].reshape(128, 256), 1, 1).astype(BF)
            for i in range(2):
                blocks[k, j, 480:544, 128 * i:128 * i + 128] = small[64 * i:64 * i + 64]

    mark('rs8')
    sum_task = block_sum(comm, blocks, (l0, l1, l2), l3)
    terms(2)
    pump(sum_task)
    terms(1), terms(3)
    pump(c_task)
    pump(sum_task)
    terms(0)
    pump(f_tasks[4], f_tasks[1])
    pump(f_tasks[0], f_tasks[2])
    pump(sum_task)
    drain(c_task)
    saves.append(comm.local(c16, out_c))
    pump(f_tasks[1])
    drain(sum_task)
    mark('hmake')
    first.wait()
    hv[...] = xv[...].astype(F32) + blocks[place.x, place.zl].astype(F32)
    full[place.x, place.z] = hv[...].astype(BF)
    saves.append(comm.local(hv, out_h))
    mark('hplane')
    h_task = comm.plane_gather(lambda k, j, p: full.at[k, j, p], PARTS_A, PARTS_B)
    pump(h_task)
    pump(f_tasks[0], f_tasks[3])
    pump(h_task)
    pump(f_tasks[1], f_tasks[2], f_tasks[4])
    pump(h_task)
    pump(f_tasks[3], f_tasks[4])
    pump(h_task)
    drain(h_task)
    saves.append(comm.local(full, out_h16))
    mark('norm2')
    for zhi in range(2):
        def rows_norm(i, carry):
            here = pl.ds(pl.multiple_of(240 * i, 16), 240)
            there = pl.ds(pl.multiple_of(480 * zhi + 240 * i, 16), 240)
            get = lambda n: full[n // 2, 2 * zhi + n % 2, here, :].astype(F32)
            def put(n, v):
                n2p[there, 256 * n:256 * n + 256] = v
            scale = norm_block_rows(get, lambda n: g8[n // 2, n % 2, 1:2, :], 256, put)
            r2[zhi, here, :] = jnp.broadcast_to(scale, (240, 128))
            return carry
        lax.fori_loop(0, 2, rows_norm, 0)
        for i in range(2):
            get = lambda n: full[n // 2, 2 * zhi + n % 2, 480:544, 128 * i:128 * i + 128].astype(F32)
            base = 128 * zhi + 64 * i
            def put(n, v):
                n2a[base:base + 64, 128 * n:128 * n + 128] = v
            scale = norm_block_rows(get, lambda n: g8[n // 2, n % 2, 2:3, 128:256], 128, put)
            r2[zhi, 480 + 64 * i:544 + 64 * i, :] = jnp.broadcast_to(scale, (64, 128))
    mark('tail')
    saves += [comm.local(n2p, out_n2p), comm.local(n2a, out_n2a), comm.local(r2.at[zh], out_r2)]
    for task in f_tasks:
        drain(task)
    for copy in saves:
        copy.wait()
    mark(None)
    comm.close()


def attend(lens, *args):
    wide5 = lambda n, c: (4, 2, 2, n, c)
    outs = [((CH,) + wide5(128, 768), BF), (wide5(64, 768), BF), (wide5(128, 512), BF), (wide5(64, 512), BF),
            (wide5(128, 512), BF), (wide5(64, 512), BF), ((4, 4, T, 256), BF), ((4, 2, 8, 256), F32),
            ((480, 2048), BF), ((128, 1024), BF), ((4, 2, KEYS, 256), BF), ((608, 128), F32), ((T, 256), F32),
            ((4, 4, T, 256), BF), ((960, 2048), BF), ((256, 1024), BF), ((608, 128), F32)]
    vm = pltpu.VMEM
    scratch = [vm((4, 2, 192, 128), BF), vm((192, 512), BF)] + [vm(s, d) for s, d in outs[2:6]] + [
        vm((4, 2, T, 256), BF), vm((4, 4, T, 256), BF), vm((4, 2, 8, 256), F32), vm((480, 2048), BF), vm((128, 1024), BF),
        vm((4, 2, KEYS, 256), BF), vm((608, 128), F32), vm((T, 256), BF), vm((T, 256), F32), vm((4, 4, T, 256), BF),
        vm((960, 2048), BF), vm((256, 1024), BF), vm((2, 608, 128), F32), vm((4, 2, T, 256), BF)] + LAND_8
    return pl.pallas_call(
        attend_kernel,
        out_shape=[jax.ShapeDtypeStruct(s, d) for s, d in outs],
        in_specs=[pl.BlockSpec(memory_space=pltpu.SMEM)] + [ANY] * len(args),
        out_specs=[ANY] * len(outs),
        scratch_shapes=scratch + SEM_SCRATCH,
        compiler_params=pltpu.CompilerParams(collective_id=0, has_side_effects=True, vmem_limit_bytes=VMEM_CAP),
        name="attend",
    )(lens, *args)
EARLY = 2
TILE = 240


def gelu_parts(z):
    a, b = 0.7978845608028654, 0.044715
    t = jnp.tanh(a * (z + b * z * z * z))
    half = 0.5 * (1.0 + t)
    return z * half, half + 0.5 * z * (1.0 - t * t) * a * (1.0 + 3.0 * b * z * z)


def side_rows(full, z_low, base, count):
    return jnp.concatenate([full[x, z_low + zl, pl.ds(base, count), :] for x, zl in pairs8()], axis=1)


def feed_forward_kernel(f, fa, n2p, n2a, c16, out_g2, out_g3, out_s0, out_s1, out_sa, out_d8, out_y,
                        wv, wav, np_, na, gc, ga, dd, aa, dda, aaa, bb, bf, bn, d8, yb, g0, g1, ga_, s0, s1, sa,
                        r0, r1, ra, z0, z1, za, *sems):
    comm = Comm(*sems)
    place = comm.place
    loads = [comm.local(n2p, np_), comm.local(f.at[0], wv.at[0]), comm.local(c16, gc), comm.local(n2a, na),
             comm.local(f.at[1], wv.at[1]), comm.local(f.at[2], wv.at[2]), comm.local(f.at[3], wv.at[3]),
             comm.local(fa, wav)]
    comm.enter(PEERS)
    mark("units")
    loads[0].wait()
    for i in range(CH):
        loads[(1, 4, 5, 6)[i]].wait()
        if i == 0:
            loads[2].wait()
        def unit(t, carry):
            here = pl.ds(pl.multiple_of(TILE * t, 16), TILE)
            weight = lambda j: wv[i, :, :, :, :, 256 * j:256 * j + 256].reshape(2048, 256)
            rows_n = np_[here, :]
            gate, up = dot(rows_n, weight(0), 1, 0), dot(rows_n, weight(1), 1, 0)
            rows_c = side_rows(gc, 2 * lax.div(t, 2), pl.multiple_of(TILE * lax.rem(t, 2), 16), TILE)
            dact = dot(rows_c, weight(2), 1, 0)
            value, slope = gelu_parts(gate)
            aa[here, 256 * i:256 * i + 256] = (value * up).astype(BF)
            dd[here, 512 * i:512 * i + 256] = (dact * up * slope).astype(BF)
            dd[here, 512 * i + 256:512 * i + 512] = (dact * value).astype(BF)
            return carry
        lax.fori_loop(0, 4, unit, 0)
    loads[3].wait(), loads[7].wait()
    for zhi in range(2):
        for i in range(2):
            base = 128 * zhi + 64 * i
            for n in range(8):
                ga[base:base + 64, 128 * n:128 * n + 128] = gc[n // 2, 2 * zhi + n % 2, 480:544, 128 * i:128 * i + 128]
    weight = lambda j: wav[:, :, :, :, 256 * j:256 * j + 256].reshape(1024, 256)
    gate, up, dact = dot(na[...], weight(0), 1, 0), dot(na[...], weight(1), 1, 0), dot(ga[...], weight(2), 1, 0)
    value, slope = gelu_parts(gate)
    aaa[...] = (value * up).astype(BF)
    dda[:, 0:256] = (dact * up * slope).astype(BF)
    dda[:, 256:512] = (dact * value).astype(BF)

    mark("back")

    def product(ref, x, z, left, left_a, lo, hi):
        zh_, zl_ = lax.div(z, 2), lax.rem(z, 2)
        here = pl.ds(pl.multiple_of(480 * zh_, 16), 480)
        rows_w = jnp.concatenate([wv[i, x, zl_, :, :, lo:hi].reshape(256, hi - lo) for i in range(CH)], axis=1)
        ref[0:480, :] = dot(left[here, :], rows_w, 1, 1).astype(BF)
        there = pl.ds(pl.multiple_of(128 * zh_, 16), 128)
        small = dot(left_a[there, :], wav[x, zl_, :, :, lo:hi].reshape(128, hi - lo), 1, 1).astype(BF)
        ref[480:544, 0:128] = small[0:64]
        ref[480:544, 128:256] = small[64:128]

    far_x, far_z = place.off("x", 2), place.off("z", 2)

    def far_terms(t, carry):
        x = jnp.where(t < 4, t, far_x)
        z = jnp.where(t < 4, far_z, lax.rem(far_z + jnp.where(t < 4, 0, t - 3), 4))
        product(bb.at[x, z], x, z, dd, dda, 0, 512)
        return carry

    def near_terms(t, carry):
        x, z = lax.rem(far_x + 1 + lax.div(t, 3), 4), lax.rem(far_z + 1 + lax.rem(t, 3), 4)
        product(bb.at[x, z], x, z, dd, dda, 0, 512)
        return carry

    lax.fori_loop(0, 7, far_terms, 0)
    b_task = plane_sum(comm, bb, bf, bn)
    pump(b_task)
    lax.fori_loop(0, 9, near_terms, 0)
    pump(b_task)

    mark("grads")

    def weight_grads(grad, i):
        def block_rows(y, carry):
            here = pl.ds(pl.multiple_of(512 * y, 512), 512)
            left_n = np_[:, here]
            left_c = jnp.concatenate(
                [jnp.concatenate([gc[y, zl, 0:480, :], gc[y, 2 + zl, 0:480, :]], axis=0) for zl in range(2)], axis=1)
            for j in range(3):
                if j < 2:
                    value = dot(left_n, dd[:, 512 * i + 256 * j:512 * i + 256 * j + 256], 0, 0).astype(BF)
                else:
                    value = dot(left_c, aa[:, 256 * i:256 * i + 256], 0, 0).astype(BF)
                for q in range(4):
                    grad[q % 2, y, q // 2, :, 256 * j:256 * j + 256] = value[128 * q:128 * q + 128]
            return carry
        lax.fori_loop(0, 4, block_rows, 0)

    weight_grads(g0, 0)
    w0 = wide_sum(comm, g0, s0, r0.at[0], r0.at[1], r0.at[2], z0, 128, False)
    pump(w0)
    weight_grads(g1, 1)
    w1 = wide_sum(comm, g1, s1, r1.at[0], r1.at[1], r1.at[2], z1, 128, False)
    pump(w0, w1)
    pump(b_task)
    for y in range(4):
        left_n, left_c = na[:, 256 * y:256 * y + 256], ga[:, 256 * y:256 * y + 256]
        for j in range(3):
            value = dot(left_n, dda[:, 256 * j:256 * j + 256], 0, 0) if j < 2 else dot(left_c, aaa[...], 0, 0)
            value = value.astype(BF)
            for q in range(4):
                ga_[q % 2, y, q // 2, :, 256 * j:256 * j + 256] = value[64 * q:64 * q + 64]
    wa = wide_sum(comm, ga_, sa, ra.at[0], ra.at[1], ra.at[2], za, 64, False)
    pump(wa, w0, w1)
    pump(b_task)
    drain(b_task)
    mark("dn2")
    d8[place.x, place.zl] = bb[place.x, place.z]
    d_task = comm.pair_ring_gather("zl", "x", lambda k, j, p: d8.at[k, j, p], PARTS_8,
                                   lambda p: d8.at[place.x, place.zl, p], d8.at[place.x, place.zl], slice(None))
    pump(d_task)
    pump(wa, w0, w1)
    mark("late")
    late = []
    for i, out in ((2, out_g2), (3, out_g3)):
        pump(d_task)
        weight_grads(yb, i)
        late.append(comm.local(yb, out))
        late[-1].wait()
        pump(w0, w1, wa)
    mark("ydown")

    def down_terms(t, carry):
        x, z = lax.div(t, 4), lax.rem(t, 4)
        product(bb.at[x, z], x, z, aa, aaa, 512, 768)
        return carry

    drain(d_task)
    comm.settle()
    lax.fori_loop(0, 16, down_terms, 0)
    saves = [comm.local(bb, out_y), comm.local(d8, out_d8)]
    for task in (w0, w1, wa):
        drain(task)
    for grad, swap, out in ((g0, z0, out_s0), (g1, z1, out_s1), (ga_, za, out_sa)):
        saves.append(comm.local(grad.at[place.core, place.y, place.zh], out.at[place.zh]))
        saves.append(comm.local(swap, out.at[1 - place.zh]))
    for copy in saves:
        copy.wait()
    mark(None)
    comm.close()


def feed_forward(f, fa, n2p, n2a, c16):
    grad = (2, 4, 2, 128, 768)
    outs = [(grad, BF), (grad, BF), ((2, 128, 768), BF), ((2, 128, 768), BF), ((2, 64, 768), BF),
            ((4, 2, T, 256), BF), ((4, 4, T, 256), BF)]
    vm = lambda *s: pltpu.VMEM(s, BF)
    scratch = [vm(CH, 4, 2, 2, 128, 768), vm(4, 2, 2, 64, 768), vm(960, 2048), vm(256, 1024), vm(4, 4, T, 256),
               vm(256, 1024), vm(960, 2048), vm(960, 1024), vm(256, 512), vm(256, 256)]
    scratch += [vm(4, 4, T, 256)] + LAND_16 + [vm(4, 2, T, 256), vm(*grad)]
    scratch += [vm(*grad), vm(*grad), vm(2, 4, 2, 64, 768), vm(*grad[1:]), vm(*grad[1:]), vm(4, 2, 64, 768)]
    scratch += [vm(3, 2, 128, 768), vm(3, 2, 128, 768), vm(3, 2, 64, 768), vm(128, 768), vm(128, 768), vm(64, 768)]
    return pl.pallas_call(
        feed_forward_kernel,
        out_shape=[jax.ShapeDtypeStruct(s, d) for s, d in outs],
        in_specs=[ANY] * 5,
        out_specs=[ANY] * len(outs),
        scratch_shapes=scratch + SEM_SCRATCH,
        compiler_params=pltpu.CompilerParams(collective_id=2, has_side_effects=True, vmem_limit_bytes=VMEM_CAP),
        name="feed_forward",
    )(f, fa, n2p, n2a, c16)
def attend_back_kernel(lens, d8, h16, c16, r2, r1, g8, qo, qoa, kv, kva, n1p, n1a, qkvo, xb, cotb, g2, g3, yt, h_own,
                       out_s2, out_s3, out_q, out_qa, out_kv, out_x, out_y, out_g,
                       dv8, hv, cv, r2v, r1v, g8v, qov, qoav, kvv, kvav, npv, nav, qv, xv, cotv, g2v, g3v, yv, how,
                       mean, ghp, gha, dhb, dov, dqp, dqa, stat, st8, gains, gsum, gains16, outx, outy,
                       gq, gkv, gqa, gkva, kvb, blocks, yf, yn, l0, l1, l2, l3, k0, k1, k2, k3,
                       s2, s3, sq, skv, sqa, skva, t2, t3, tq, tkv, tqa, tkva, z2, z3, zq, zkv, zqa, zkva, *sems):
    comm = Comm(*sems)
    place = comm.place
    x, y, zh, zl, core = place.x, place.y, place.zh, place.zl, place.core
    side = pl.ds(2 * zh, 2)
    load = comm.local
    la = [load(d8, dv8), load(h16.at[:, side], hv), load(r2, r2v), load(g8, g8v), load(c16.at[:, side], cv), load(cotb, cotv)]
    lg = [load(g2, g2v), load(g3, g3v)]
    lb = [load(qo, qov), load(qoa, qoav), load(qkvo, qv)]
    ly = load(yt, yv)
    lc = [load(kv, kvv), load(kva, kvav), load(n1p, npv), load(n1a, nav), load(xb, xv), load(r1, r1v), load(h_own, how)]
    comm.enter(PEERS)
    mark("dh")
    for copy in la:
        copy.wait()
    for i in range(2):
        here = pl.ds(240 * i, 240)
        scale = r2v[here, 0:1]
        gain = lambda n: g8v[n // 2, n % 2, 1:2, :]
        grad = lambda n: dv8[n // 2, n % 2, here, :].astype(F32) * gain(n)
        unit = lambda n: hv[n // 2, n % 2, here, :].astype(F32) * scale
        m = sum(jnp.sum(grad(n) * unit(n), axis=1, keepdims=True) for n in range(8)) / 2048
        mean[here, :] = jnp.broadcast_to(m, (240, 128))
        for n in range(8):
            value = cv[n // 2, n % 2, here, :].astype(F32) + scale * (grad(n) - unit(n) * m)
            ghp[here, 256 * n:256 * n + 256] = value.astype(BF)
        here, there, lanes = pl.ds(480, 64), pl.ds(480 + 64 * i, 64), pl.ds(128 * i, 128)
        scale_a = r2v[there, 0:1]
        gain_a = lambda n: g8v[n // 2, n % 2, 2:3, 128:256]
        grad_a = lambda n: dv8[n // 2, n % 2, here, lanes].astype(F32) * gain_a(n)
        unit_a = lambda n: hv[n // 2, n % 2, here, lanes].astype(F32) * scale_a
        m = sum(jnp.sum(grad_a(n) * unit_a(n), axis=1, keepdims=True) for n in range(8)) / 1024
        mean[there, :] = jnp.broadcast_to(m, (64, 128))
        for n in range(8):
            value = cv[n // 2, n % 2, here, lanes].astype(F32) + scale_a * (grad_a(n) - unit_a(n) * m)
            gha[64 * i:64 * i + 64, 128 * n:128 * n + 128] = value.astype(BF)
    mark("attnback")
    for copy in lb:
        copy.wait()
    for i in range(2):
        here = pl.ds(240 * i, 240)
        dov[i, 0:240, :] = dot(ghp[here, :], qov[:, :, :, :, 256:512].reshape(2048, 256), 1, 0).astype(BF)
    low = dot(gha[...], qoav[:, :, :, :, 256:512].reshape(1024, 256), 1, 0).astype(BF)
    for i in range(2):
        dov[i, 240:304, :] = low[64 * i:64 * i + 64]
    for i in range(2):
        q, k, v, do = qv[0, i, 0:304, :], qv[1, i], qv[2, i], dov[i]
        probs = soft(q, k, lens[i])
        inner = probs * dot(do, v, 1, 1)
        dscores = (inner - probs * jnp.sum(inner, axis=1, keepdims=True)).astype(BF)
        dq = (dot(dscores, k, 1, 0) * 0.0625).astype(BF)
        dk = (dot(dscores, q, 0, 0) * 0.0625).astype(BF)[0:304]
        dv = dot(probs.astype(BF), do, 0, 0).astype(BF)[0:304]
        for j, value in enumerate((dq, dk, dv)):
            dqp[240 * i:240 * i + 240, 256 * j:256 * j + 256] = value[0:240]
            dqa[64 * i:64 * i + 64, 256 * j:256 * j + 256] = value[240:304]
        total = dq.astype(F32) * q.astype(F32) + dk.astype(F32) * k[0:304].astype(F32) + dv.astype(F32) * v[0:304].astype(F32)
        total = jnp.broadcast_to(jnp.sum(total, axis=1, keepdims=True), (304, 128))
        stat[240 * i:240 * i + 240, :] = total[0:240]
        stat[480 + 64 * i:544 + 64 * i, :] = total[240:304]
    stat[608:640, :] = jnp.zeros((32, 128), F32)
    st8[x, zl] = stat[...].T[0:8]
    for copy in lc:
        copy.wait()
    mark("terms")

    def terms(step):
        k = place.off("x", step)
        for j in range(2):
            weight = jnp.concatenate([qov[k, j, :, :, 0:256].reshape(256, 256), kvv[k, j].reshape(256, 512)], axis=1)
            blocks[k, j, 0:480, :] = dot(dqp[...], weight, 1, 1).astype(BF)
            weight = jnp.concatenate([qoav[k, j, :, :, 0:256].reshape(128, 256), kvav[k, j].reshape(128, 512)], axis=1)
            small = dot(dqa[...], weight, 1, 1).astype(BF)
            for i in range(2):
                blocks[k, j, 480:544, 128 * i:128 * i + 128] = small[64 * i:64 * i + 64]

    terms(2)
    sum_task = block_sum(comm, blocks, (l0, l1, l2), l3)
    pump(sum_task)
    stat_task = comm.pair_ring_gather("zl", "x", lambda k, j, p: st8.at[k, j, p], [(slice(None), 1)],
                                      lambda p: st8.at[x, zl, p], st8.at[x, zl], slice(None))
    pump(stat_task)
    terms(1), terms(3)
    pump(sum_task)
    terms(0)

    def outer(grad, n, left, right, lo, width):
        def block_rows(k, carry):
            here = pl.ds(pl.multiple_of(4 * n * k, 4 * n), 4 * n)
            value = dot(left[:, here], right, 0, 0).astype(BF)
            for c in range(4):
                grad[c % 2, k, c // 2, :, lo:lo + width] = value[n * c:n * c + n]
            return carry
        lax.fori_loop(0, 4, block_rows, 0)

    mark("attngrads")
    outer(gkv, 128, npv, dqp[:, 256:768], 0, 512)
    outer(gkva, 64, nav, dqa[:, 256:768], 0, 512)
    kv_tasks = [wide_sum(comm, gkv, skv, tkv.at[0], tkv.at[1], tkv.at[2], zkv, 128, True),
                wide_sum(comm, gkva, skva, tkva.at[0], tkva.at[1], tkva.at[2], zkva, 64, True)]
    pump(*kv_tasks)
    outer(gq, 128, npv, dqp[:, 0:256], 0, 256)
    o_act = jnp.concatenate([qv[3, 0, 240:304, :], qv[3, 1, 240:304, :]], axis=0)
    o_pre = jnp.concatenate([qv[3, 0, 0:240, :], qv[3, 1, 0:240, :]], axis=0)
    outer(gq, 128, ghp, o_pre, 256, 256)
    outer(gqa, 64, nav, dqa[:, 0:256], 0, 256)
    outer(gqa, 64, gha, o_act, 256, 256)
    q_tasks = [wide_sum(comm, gq, sq, tq.at[0], tq.at[1], tq.at[2], zq, 128, True),
               wide_sum(comm, gqa, sqa, tqa.at[0], tqa.at[1], tqa.at[2], zqa, 64, True)]
    pump(*q_tasks)
    pump(*kv_tasks)
    mark("late")
    for copy in lg:
        copy.wait()
    late = [wide_sum(comm, g2v, s2, t2.at[0], t2.at[1], t2.at[2], z2, 128, False),
            wide_sum(comm, g3v, s3, t3.at[0], t3.at[1], t3.at[2], z3, 128, False)]
    pump(*late)
    ly.wait()
    y_task = plane_sum(comm, yv, yf, yn)
    pump(y_task)
    pump(stat_task, sum_task)
    pump(*q_tasks), pump(*kv_tasks)
    pump(*late)
    pump(stat_task, y_task)
    drain(sum_task), drain(stat_task)
    mark("dx")
    g_pre, g_act = g8v[x, zl, 0:1, :], g8v[x, zl, 2:3, 0:128]
    f_pre, f_act = g8v[x, zl, 1:2, :], g8v[x, zl, 2:3, 128:256]
    total = sum(st8[n // 2, n % 2] for n in range(8))
    stat[...] = jnp.broadcast_to(total[0:1], (128, 640)).T

    def own_norm(here, there, lanes, gain_f, gain_a, width):
        s2_, s1_ = r2v[there, 0:1], r1v[there, 0:1]
        back, unit = dv8[x, zl, here, lanes].astype(F32), hv[x, zl, here, lanes].astype(F32) * s2_
        dh = cotv[here, lanes] + s2_ * (back * gain_f - unit * mean[there, 0:1])
        gain_f_grad = jnp.sum(back * unit, axis=0, keepdims=True)
        back, unit = blocks[x, zl, here, lanes].astype(F32), xv[here, lanes].astype(F32) * s1_
        outx[here, lanes] = dh + s1_ * (back * gain_a - unit * (stat[there, 0:1] / width))
        return jnp.sum(back * unit, axis=0, keepdims=True), gain_f_grad

    pre = [own_norm(pl.ds(240 * i, 240), pl.ds(240 * i, 240), pl.ds(0, 256), f_pre, g_pre, 2048) for i in range(2)]
    act = [own_norm(pl.ds(480, 64), pl.ds(480 + 64 * i, 64), pl.ds(128 * i, 128), f_act, g_act, 1024) for i in range(2)]
    gains[...] = jnp.concatenate(
        [pre[0][0] + pre[1][0], pre[0][1] + pre[1][1],
         jnp.concatenate([act[0][0] + act[1][0], act[0][1] + act[1][1]], axis=1), jnp.zeros((5, 256), F32)], axis=0)
    saves = [load(outx, out_x)]
    g_task = wide_gather(comm, gains16, gains, gains, 8, [(slice(None), 1)])
    pump(g_task)
    mark("tail")
    pump(y_task, g_task), pump(*late), pump(g_task)
    pump(*kv_tasks), pump(*q_tasks), pump(g_task, y_task)
    drain(kv_tasks[0]), drain(kv_tasks[1])
    own = jnp.concatenate([gkv[core, y, zh], gkva[core, y, zh]], axis=0)
    lane = lax.broadcasted_iota(jnp.int32, (128, 512), 0)
    col = lax.broadcasted_iota(jnp.int32, (128, 512), 1)
    for n in range(8):
        pick = ((lane < 32) & (col == 32 * n + lane)) | ((lane >= 32) & (lane < 64) & (col == 224 + 32 * n + lane))
        kvb[n // 2, n % 2] = dot(own, pick.astype(F32).astype(BF), 1, 1).astype(BF)
    share = block_sum(comm, kvb, (k0, k1, k2), k3, halves(192))
    pump(share)
    pump(g_task), pump(*late), pump(*q_tasks)
    pump(share)
    drain(y_task)
    outy[...] = (yv[x, place.z].astype(F32) + how[...]).astype(BF)
    saves.append(load(outy, out_y))
    pump(share, g_task)
    for task in q_tasks + late:
        drain(task)
    drain(share), drain(g_task)
    gsum[...] = sum(gains16[a, b, c] for a in range(4) for b in range(2) for c in range(2))
    saves += [load(gsum, out_g), load(kvb.at[x, zl], out_kv), load(gq.at[core, y, zh], out_q), load(gqa.at[core, y, zh], out_qa)]
    for grad, swap, out in ((g2v, z2, out_s2), (g3v, z3, out_s3)):
        saves += [load(grad.at[core, y, zh], out.at[zh]), load(swap, out.at[1 - zh])]
    for copy in saves:
        copy.wait()
    mark(None)
    comm.close()


def attend_back(lens, *args):
    outs = [((2, 128, 768), BF), ((2, 128, 768), BF), ((128, 512), BF), ((64, 512), BF), ((192, 128), BF), ((T, 256), F32),
            ((T, 256), BF), ((8, 256), F32)]
    vm = lambda *s: pltpu.VMEM(s, BF)
    vf = lambda *s: pltpu.VMEM(s, F32)
    wide = lambda n, c: (2, 4, 2, n, c)
    back = [(128, 768), (128, 768), (128, 512), (128, 512), (64, 512), (64, 512)]
    scratch = [vm(4, 2, T, 256), vm(4, 2, T, 256), vm(4, 2, T, 256), vf(608, 128), vf(608, 128), vf(4, 2, 8, 256),
               vm(4, 2, 2, 128, 512), vm(4, 2, 2, 64, 512), vm(4, 2, 2, 128, 512), vm(4, 2, 2, 64, 512),
               vm(480, 2048), vm(128, 1024), vm(4, 2, KEYS, 256), vm(T, 256), vf(T, 256), vm(*wide(128, 768)),
               vm(*wide(128, 768)), vm(4, 4, T, 256), vf(T, 256)]
    scratch += [vf(608, 128), vm(480, 2048), vm(128, 1024), vf(8, 128), vm(2, 304, 256), vm(480, 768), vm(128, 768),
                vf(640, 128), vf(4, 2, 8, 640), vf(8, 256), vf(8, 256), vf(4, 2, 2, 8, 256), vf(T, 256), vm(T, 256)]
    scratch += [vm(*wide(n, c)) for n, c in back[2:]]
    scratch += [vm(4, 2, 192, 128), vm(4, 2, T, 256)] + LAND_16 + LAND_8 + [vm(2, 192, 128)] * 3 + [vm(192, 128)]
    scratch += [vm(4, 2, n, c) for n, c in back] + [vm(3, 2, n, c) for n, c in back] + [vm(n, c) for n, c in back]
    return pl.pallas_call(
        attend_back_kernel,
        out_shape=[jax.ShapeDtypeStruct(s, d) for s, d in outs],
        in_specs=[pl.BlockSpec(memory_space=pltpu.SMEM)] + [ANY] * len(args),
        out_specs=[ANY] * len(outs),
        scratch_shapes=scratch + SEM_SCRATCH,
        compiler_params=pltpu.CompilerParams(collective_id=3, has_side_effects=True, vmem_limit_bytes=VMEM_CAP),
        name="attend_back",
    )(lens, *args)
def local(x_pre, x_act, lengths, cot_pre, cot_act, attn_gain_pre, query_pre, key_pre, value_pre, out_pre, ffn_gain_pre,
          gate_pre, up_pre, down_pre, attn_gain_act, query_act, key_act, value_act, out_act, ffn_gain_act, gate_act,
          up_act, down_act):
    wf, wfa = pack_hidden(gate_pre, up_pre, down_pre), pack_hidden(gate_act, up_act, down_act)[:, 0]
    wq, wqa = jnp.concatenate([query_pre, out_pre.T], axis=1), jnp.concatenate([query_act, out_act.T], axis=1)
    kvs = jnp.concatenate([jnp.concatenate([key_pre, value_pre], axis=1), jnp.concatenate([key_act, value_act], axis=1)])
    kvs = jnp.pad(kvs, ((0, 0), (0, 64)))
    xb, cot = pack_tokens(x_pre, x_act), pack_tokens(cot_pre, cot_act)
    gb = jnp.pad(jnp.stack([attn_gain_pre, ffn_gain_pre, jnp.concatenate([attn_gain_act, ffn_gain_act])]), ((0, 5), (0, 0)))
    (f, fa, qo, qoa, kv, kva, c16, g8, n1p, n1a, qkvo, r1, h_own, h16, n2p, n2a, r2) = attend(
        lengths, wf, wfa, wq, wqa, kvs, xb, cot.astype(BF), gb)
    g2, g3, s0, s1, sa, d8, yt = feed_forward(f, fa, n2p, n2a, c16)
    s2, s3, sq, sqa, skv, gx, y, gains = attend_back(
        lengths, d8, h16, c16, r2, r1, g8, qo, qoa, kv, kva, n1p, n1a, qkvo, xb, cot, g2, g3, yt, h_own)
    unact = lambda m: m.reshape(64, 2, 128)[:50].transpose(1, 0, 2)

    def open_hidden(m, n):
        m = m.astype(F32).reshape(2, -1, n, 768).transpose(2, 0, 1, 3)
        gate, up, down = (m[..., 256 * j:256 * j + 256].reshape(n, -1) for j in range(3))
        return gate, up, down.T

    dgate_p, dup_p, ddown_p = open_hidden(jnp.stack([s0, s1, s2, s3], axis=1), 128)
    dgate_a, dup_a, ddown_a = open_hidden(sa, 64)
    sq, sqa, skv = sq.astype(F32), sqa.astype(F32), skv.astype(F32)
    return (y[:480].reshape(2, 240, 256), unact(y[480:]), gx[:480].reshape(2, 240, 256), unact(gx[480:]),
            gains[0], sq[:, :256], skv[:128, :32], skv[:128, 32:64], sq[:, 256:].T, gains[1], dgate_p, dup_p, ddown_p,
            gains[2, :128], sqa[:, :256], skv[128:, :32], skv[128:, 32:64], sqa[:, 256:].T, gains[2, 128:],
            dgate_a, dup_a, ddown_a)


def solution(mesh):
    tok, row, col, vec = P("wide", None, "narrow"), P("wide", "narrow"), P("narrow", "wide"), P("narrow")
    expert = (vec, row, row, row, col, vec, row, row, col)
    return jax.shard_map(
        local, mesh=mesh, in_specs=(tok, tok, P("wide"), tok, tok) + expert + expert,
        out_specs=(tok,) * 4 + expert + expert, check_vma=False)
```

time: 802 us -> 417 us (0.52)
  matrix products: 181 us -> 0 us
  local copies, waits for them, and re-layouts: 98.3 us -> 24.2 us
  other arithmetic: 66.5 us -> 10.4 us
  blocking collectives: 54.3 us -> 0 us
  between operations: 17.2 us -> 1.38 us
    dot_general x81 -> x0, matrix products: 181 us -> none  [dot(): lax.dot_general(a, b, (((ca,), (cb,)), ((), ())), preferred_element_type=...]
    psum x2 -> x0, blocking collectives: 54.3 us -> none  [the longest x1 36.2 us: local(): lax.psum((jnp.sum(d1p * xps, axis=0), jnp.sum(b2ps * u2ps, axis=0), jnp.s...]
    unnamed x375 -> x71, local copies, waits for them, and re-layouts: 38.6 us -> 9.33 us
    reshape x24 -> x0, local copies, waits for them, and re-layouts: 18.6 us -> none  [the longest x6 7.85 us: block(): top = pre.reshape(480, 8, 256).transpose(1, 0, 2)]
    slice x43 -> x7, local copies, waits for them, and re-layouts: 22.8 us -> 4.32 us  [the longest x1 1.34 us: local(): gains[1]]
    transpose x9 -> x0, other arithmetic: 13.7 us -> none  [by_core(): grad.astype(BF).reshape(4, 2, 2, n, grad.shape[1]).transpose(2, 0, 1, 3, 4)]
    reduce_sum x12 -> x0, other arithmetic: 12.3 us -> none  [the longest x2 4.33 us: norm_back(): jnp.mean(inner * unit, axis=1, keepdims=True)]
    concatenate x7 -> x2, other arithmetic: 11.9 us -> 2.51 us  [pack_tokens(): return jnp.concatenate([pre.reshape(480, 256), low], axis=0)]
  transfers between devices with their start and end apart: 1 -> 0, of which waited for: 0 -> 0; matrix products, arithmetic and copies ran while one was open for 4% -> 0% of each run, Pallas kernels for 0% -> 0%
where the time goes in v2:
time: 417 us; the launch traced here: 414 us
  Pallas kernels  378 us (91%)
  local copies, waits for them, and re-layouts  24.2 us (6%)
  other arithmetic  10.4 us (2%)
    pallas_call x1, Pallas kernels, attend(): pl.pallas_call(attend_kernel, out_shape=[jax.ShapeDtypeStruct(s, d) for s...  173 us
    pallas_call x1, Pallas kernels, attend_back(): pl.pallas_call(attend_back_kernel, out_shape=[jax.ShapeDtypeStruct(s, d)...  103 us
    pallas_call x1, Pallas kernels, feed_forward(): pl.pallas_call(feed_forward_kernel, out_shape=[jax.ShapeDtypeStruct(s, d)...  102 us
    unnamed x71, local copies, waits for them, and re-layouts  9.33 us

profile of v2, /device:TPU:0, one launch (start us, length us, event | category | flops | bytes accessed | tf_op | source)
XLA Modules:
  0.0 413.8 jit_solution(11494828944191197826)
XLA Ops:
  0.7 1.0 fusion.13
  1.7 1.8 fusion.10.cb
  3.4 0.9 fusion.16
  4.3 1.7 pad_maximum_fusion.1.xb
  7.4 1.3 maximum_bitcast_fusion.wf
  8.9 0.7 maximum_bitcast_fusion.1.wfa
  10.9 0.7 fusion.7.kvs
  12.9 172.8 %attend.1 = (bf16[4,4,2,2,128,768]{5,4,3,2,1,0:T(8,128)(2,1)}, bf16[4,2,2,64,768]{4,3,2,1,0:T(8,128)(2,1)}, bf16[4,2,2,128,512]{4,3,2,1,0:T(8,128)(2,1)}, bf16[4...) custom-call(s32[2]{0:T(128)} %lens.3, ...), custom_call_target="tpu_custom_call" | custom-call | tf_op jit(solution)/shard_map/attend/pallas_call | solution.py:558
  185.7 101.8 %feed_forward.1 = (bf16[2,4,2,128,768]{4,3,2,1,0:T(8,128)(2,1)}, bf16[2,4,2,128,768]{4,3,2,1,0:T(8,128)(2,1)}, bf16[2,128,768]{2,1,0:T(8,128)(2,1)}, bf16[2,128,...) custom-call(bf16[4,4,2,2,128,768]{5,4,3,2,1,0:T(8,128)(2,1)} %get-tu, ...), custom_call_target="tpu_custom_call" | custom-call | tf_op jit(solution)/shard_map/feed_forward/pallas_call | solution.py:736
  287.5 0.8 pad_maximum_fusion.cotb
  288.4 103.2 %attend_back.1 = (bf16[2,128,768]{2,1,0:T(8,128)(2,1)}, bf16[2,128,768]{2,1,0:T(8,128)(2,1)}, bf16[128,512]{1,0:T(8,128)(2,1)}, bf16[64,512]{1,0:T(8,128)(2,1)},...) custom-call(s32[2]{0:T(128)} %lens.3, ...), custom_call_target="tpu_custom_call" | custom-call | tf_op jit(solution)/shard_map/attend_back/pallas_call | solution.py:945
  391.6 1.4 convert_bitcast_fusion
  393.0 1.3 fusion.11
  394.3 1.5 copy.76
  395.8 1.3 copy.85
  397.5 1.3 copy.86
  398.8 1.3 copy.78
  400.1 0.8 copy.84
  400.9 0.8 slice.95
  401.7 0.7 slice.92
  403.2 0.7 copy.82
  406.6 0.7 copy.88
  408.6 1.3 fusion.17
  409.9 1.2 slice_bitcast_fusion.2
  (101 shorter events, 11.4 us)
Async XLA Ops:
  0.7 5.4 %copy-start.4 = (bf16[128,2048]{1,0:T(8,128)(2,1)S(1)}, bf16[128,2048]{1,0:T(8,128)(2,1)}, u32[]{:S(2)}) copy-start(bf16[128,2048]{1,0:T(8,128)(2,1)} %param.34) | copy-start | bytes 1572868
  0.7 5.8 %copy-start.5 = (bf16[128,2048]{1,0:T(8,128)(2,1)S(1)}, bf16[128,2048]{1,0:T(8,128)(2,1)}, u32[]{:S(2)}) copy-start(bf16[128,2048]{1,0:T(8,128)(2,1)} %param.35) | copy-start | bytes 1572868
  7.1 1.7 copy-start.13
  7.3 2.3 copy-start.15
  7.3 2.4 copy-start.16
  7.3 3.1 copy-start.19
  7.3 3.2 copy-start.20
  7.3 3.3 copy-start.21
  7.4 3.4 copy-start.22
  7.4 4.2 %copy-start.17 = (bf16[256,64]{0,1:T(8,128)(2,1)S(1)}, bf16[256,64]{0,1:T(8,128)(2,1)}, u32[]{:S(2)}) copy-start(bf16[256,64]{0,1:T(8,128)(2,1)} %param.41) | copy-start | bytes 98308
  7.4 4.2 %copy-start.18 = (bf16[64,256]{1,0:T(8,128)(2,1)S(1)}, bf16[64,256]{1,0:T(8,128)(2,1)}, u32[]{:S(2)}) copy-start(bf16[64,256]{1,0:T(8,128)(2,1)} %param.38) | copy-start | bytes 98308
  7.4 4.8 %copy-start.25 = (f32[128]{0:T(128)S(1)}, f32[128]{0:T(128)}, u32[]{:S(2)}) copy-start(f32[128]{0:T(128)} %param.42) | copy-start | bytes 1540
  7.4 4.8 %copy-start.26 = (f32[128]{0:T(128)S(1)}, f32[128]{0:T(128)}, u32[]{:S(2)}) copy-start(f32[128]{0:T(128)} %param.37) | copy-start | bytes 1540
  7.4 4.8 %copy-start.23 = (f32[256]{0:T(256)S(1)}, f32[256]{0:T(256)}, u32[]{:S(2)}) copy-start(f32[256]{0:T(256)} %param.33) | copy-start | bytes 3076
  7.4 4.8 %copy-start.24 = (f32[256]{0:T(256)S(1)}, f32[256]{0:T(256)}, u32[]{:S(2)}) copy-start(f32[256]{0:T(256)} %param.28) | copy-start | bytes 3076
  185.7 101.8 %copy-start = (f32[2,240,256]{2,1,0:T(8,128)S(1)}, f32[2,240,256]{2,1,0:T(8,128)}, u32[]{:S(2)}) copy-start(f32[2,240,256]{2,1,0:T(8,128)} %param.26) | copy-start | bytes 1474564
  288.4 103.2 %copy-start.7 = (bf16[2,128,768]{2,1,0:T(8,128)(2,1)S(1)}, bf16[2,128,768]{2,1,0:T(8,128)(2,1)}, u32[]{:S(2)}) copy-start(bf16[2,128,768]{2,1,0:T(8,128)(2,1)} %get-tuple-element.80) | copy-start | bytes 1179652
  288.4 103.2 %copy-start.8 = (bf16[2,128,768]{2,1,0:T(8,128)(2,1)S(1)}, bf16[2,128,768]{2,1,0:T(8,128)(2,1)}, u32[]{:S(2)}) copy-start(bf16[2,128,768]{2,1,0:T(8,128)(2,1)} %get-tuple-element.81) | copy-start | bytes 1179652
  397.4 2.6 copy-start.3
  397.5 3.4 copy-start.2
  398.8 2.9 copy-start.9
  398.8 3.6 copy-start.10
  398.8 4.3 %copy-start.1 = (bf16[192,128]{1,0:T(8,128)(2,1)S(1)}, bf16[192,128]{1,0:T(8,128)(2,1)}, u32[]{:S(2)}) copy-start(bf16[192,128]{1,0:T(8,128)(2,1)} %get-tuple-element.79) | copy-start | bytes 147460
  400.1 11.0 %copy-start.11 = (bf16[2,64,768]{2,1,0:T(8,128)(2,1)S(1)}, bf16[2,64,768]{2,1,0:T(8,128)(2,1)}, u32[]{:S(2)}) copy-start(bf16[2,64,768]{2,1,0:T(8,128)(2,1)} %get-tuple-element.85) | copy-start | bytes 589828
  (3 other events, 4.3 us)

commit v3 on v2

--- a/solution.py
+++ b/solution.py
@@ -10,6 +10,7 @@
 BF = jnp.bfloat16
 F32 = jnp.float32
 SEMS = 256
+LOCAL_SEMS = 48
 VMEM_CAP = 62 * 1024 * 1024
 
 
@@ -39,6 +40,10 @@
             return {"wide": self.wide_at(self.y, 1 - self.zh, self.core)}
         if name == "zl":
             return {"narrow": self.x * 2 + 1 - self.zl}
+        if name[0] == "w":
+            step, flip = int(name[1]), int(name[2])
+            zh = 1 - self.zh if flip else self.zh
+            return {"wide": self.wide_at(self.off("y", step), zh, self.core)}
         axis, step = name[0], 1 if name[1] == "+" else -1
         at = self.off(axis, step)
         if axis == "y":
@@ -75,6 +80,7 @@
     def send(self, src, dst, name, incoming):
         index = self.count
         self.count += 1
+        assert index < SEMS
         make = lambda to: pltpu.make_async_remote_copy(
             src_ref=src, dst_ref=to, send_sem=self.send_sems.at[index], recv_sem=self.recv_sems.at[index],
             device_id=self.place.peer(name), device_id_type=MESH)
@@ -87,6 +93,7 @@
     def local(self, src, dst):
         index = self.local_count
         self.local_count += 1
+        assert index < LOCAL_SEMS
         copy = pltpu.make_async_copy(src, dst, self.local_sems.at[index])
         copy.start()
         return copy
@@ -123,30 +130,33 @@
         place = self.place
         mine = {"z2": place.zh, "zl": place.zl}[pair]
         here = place.coord(axis)
+        first = self.ring_gather(axis, lambda k, p: view(k, mine, p), parts, own)
+        next(first)
+        yield
         swap = self.send(give, view(here, mine, whole), pair, view(here, 1 - mine, whole))
-        first = self.ring_gather(axis, lambda k, p: view(k, mine, p), parts, own)
+        yield
         next(first)
         yield
         swap.arrive()
         second = self.ring_gather(axis, lambda k, p: view(k, 1 - mine, p), parts)
         next(second)
         yield
-        next(first)
-        yield
         next(second)
         yield
         drain(first)
         drain(second)
 
-    def plane_gather(self, view, parts_x, parts_z):
+    def plane_gather(self, view, parts_x, parts_z, own=None, ready=None):
         place = self.place
         every = slice(None)
-        ax = self.ring_gather("x", lambda k, p: view(k, place.z, p), parts_x)
-        bz = self.ring_gather("z", lambda k, p: view(place.x, k, p), parts_z)
+        ax = self.ring_gather("x", lambda k, p: view(k, place.z, p), parts_x, own)
+        bz = self.ring_gather("z", lambda k, p: view(place.x, k, p), parts_z, own)
         next(ax), next(bz)
         yield
         next(ax), next(bz)
         yield
+        if ready is not None:
+            ready()
         drain(ax)
         az = self.ring_gather("z", lambda k, p: view(every, k, p), parts_x)
         next(az)
@@ -238,8 +248,7 @@
 def plane_spread(comm, out, own):
     place = comm.place
     copy = comm.local(own, out.at[place.x, place.z])
-    copy.wait()
-    yield from comm.plane_gather(lambda k, j, p: out.at[k, j, p], PARTS_A, PARTS_B)
+    yield from comm.plane_gather(lambda k, j, p: out.at[k, j, p], PARTS_A, PARTS_B, lambda p: own.at[p], copy.wait)
 
 
 def pack_hidden(gate, up, down):
@@ -252,13 +261,6 @@
     low = jnp.concatenate([act[0], act[1]], axis=1)
     low = jnp.pad(low, ((0, 14), (0, 0)))
     return jnp.concatenate([pre.reshape(480, 256), low], axis=0)
-def loop_add(ref, n, *others):
-    def step(i, carry):
-        add_to(ref.at[i], *[other.at[i] for other in others])
-        return carry
-    lax.fori_loop(0, n, step, 0)
-
-
 def block_sum(comm, blocks, lands, swap, parts=PARTS_8):
     place = comm.place
     relay, plus, minus = lands
@@ -295,24 +297,48 @@
     drain(ax), drain(bz)
 
 
+CHIPS = [(step, flip) for flip in range(2) for step in range(4) if step or flip]
+
+
+def small_total(comm, slots, pair, own, out):
+    place = comm.place
+    mine = place.y * 2 + place.zh
+    links = []
+    for step, flip in CHIPS:
+        back = place.off("y", -step) * 2 + (1 - place.zh if flip else place.zh)
+        links.append(comm.send(own, slots.at[mine], f"w{step}{flip}", slots.at[back]))
+    slots[mine] = own[...]
+    yield
+    for link in links:
+        link.arrive()
+    pair[0] = sum(slots[i] for i in range(8))
+    link = comm.send(pair.at[0], pair.at[1], "sib", pair.at[1])
+    yield
+    link.arrive()
+    out[...] = pair[0] + pair[1]
+
+
 def wide_sum(comm, grad, half, relay, plus, minus, swap, n, add):
     place = comm.place
     core, zh = place.core, place.zh
-    link = comm.send(grad.at[1 - core], half, "sib", half)
+    link = comm.send(grad.at[:, :, 1 - core], half, "sib", half)
     yield
     link.arrive()
-    loop_add(grad.at[core], 4, half)
+    def fold(k, carry):
+        add_to(grad.at[k, :, core], half.at[k])
+        return carry
+    lax.fori_loop(0, 4, fold, 0)
     yield from comm.ring_sum(
-        "y", lambda k, p: grad.at[core, k, :, p], halves(n),
+        "y", lambda k, p: grad.at[k, :, core, p], halves(n),
         lambda p: relay.at[:, p], lambda p: plus.at[:, p], lambda p: minus.at[:, p])
-    link = comm.send(grad.at[core, place.y, 1 - zh], swap, "z2", swap)
+    link = comm.send(grad.at[place.y, 1 - zh, core], swap, "z2", swap)
     yield
     link.arrive()
     if add:
-        add_to(grad.at[core, place.y, zh], swap)
-
-
-SEM_SCRATCH = [pltpu.SemaphoreType.DMA((SEMS,)), pltpu.SemaphoreType.DMA((SEMS,)), pltpu.SemaphoreType.DMA((32,))]
+        add_to(grad.at[place.y, zh, core], swap)
+
+
+SEM_SCRATCH = [pltpu.SemaphoreType.DMA((SEMS,)), pltpu.SemaphoreType.DMA((SEMS,)), pltpu.SemaphoreType.DMA((LOCAL_SEMS,))]
 ANY = pl.BlockSpec(memory_space=pl.ANY)
 
 
@@ -374,10 +400,10 @@
     return scale
 
 
-def attend_kernel(lens, wf, wfa, wq, wqa, kvs, xb, cb, gb,
-                  out_f, out_fa, out_q, out_qa, out_kv, out_kva, out_c, out_g, out_n1p, out_n1a, out_qkvo, out_r1,
+def attend_kernel(lens, wf, wfa, wq, wqa, kvs, xb, gb,
+                  out_f, out_fa, out_q, out_qa, out_kv, out_kva, out_g, out_n1p, out_n1a, out_qkvo, out_r1,
                   out_h, out_h16, out_n2p, out_n2a, out_r2,
-                  kv8, kvf, qo, qoa, kv, kva, x8, c16, g8, n1p, n1a, qkvo, r1, xv, hv, full, n2p, n2a, r2,
+                  kv8, kvf, qo, qoa, kv, kva, x8, g8, n1p, n1a, qkvo, r1, xv, hv, full, n2p, n2a, r2,
                   blocks, l0, l1, l2, l3, *sems):
     comm = Comm(*sems)
     place = comm.place
@@ -396,9 +422,17 @@
     q_tasks = [wide_gather(comm, qo, wq, wq, 128), wide_gather(comm, qoa, wqa, wqa, 64)]
     f_tasks = [wide_gather(comm, out_f.at[i], wf.at[zh, i], wf.at[1 - zh, i], 128) for i in range(CH)]
     f_tasks.append(wide_gather(comm, out_fa, wfa.at[zh], wfa.at[1 - zh], 64))
-    c_task = plane_spread(comm, c16, cb)
-    pump(kv_task, x_task, *q_tasks, g_task)
-    pump(kv_task, g_task), pump(kv_task, g_task), drain(kv_task)
+    pump(kv_task), pump(kv_task)
+    pump(x_task), pump(x_task)
+    pump(g_task), pump(g_task)
+    pump(*q_tasks)
+    pump(kv_task), pump(kv_task)
+    pump(x_task)
+    pump(kv_task)
+    pump(x_task)
+    pump(*q_tasks), pump(*q_tasks)
+    pump(g_task)
+    drain(kv_task)
     total = jnp.zeros((192, 512), F32)
     lane = lax.broadcasted_iota(jnp.int32, (128, 512), 0)
     col = lax.broadcasted_iota(jnp.int32, (128, 512), 1)
@@ -408,22 +442,15 @@
     kvf[...] = total.astype(BF)
     kv_a, kv_b = kvf.at[0:128], kvf.at[128:192]
     kv_tasks = [wide_gather(comm, kv, kv_a, kv_a, 128), wide_gather(comm, kva, kv_b, kv_b, 64)]
-    pump(*kv_tasks)
-    pump(x_task, *q_tasks)
-    pump(f_tasks[0], f_tasks[1])
+    pump(*kv_tasks), pump(*kv_tasks)
+    pump(*q_tasks)
+    pump(g_task), pump(g_task)
+    pump(x_task)
     pump(*kv_tasks)
     pump(*q_tasks)
-    pump(x_task)
-    pump(*q_tasks)
+    drain(g_task)
     pump(*kv_tasks)
-    pump(f_tasks[0], f_tasks[2], f_tasks[3], f_tasks[4])
-    pump(*q_tasks)
-    pump(x_task)
-    pump(*kv_tasks)
-    mark('xwait')
-    drain(g_task)
     drain(x_task)
-    pump(c_task)
 
     mark('norm1')
     for i in range(2):
@@ -438,15 +465,19 @@
             n1a[64 * i:64 * i + 64, 128 * n:128 * n + 128] = v
         r1[480 + 64 * i:544 + 64 * i, :] = jnp.broadcast_to(
             norm_block_rows(get, lambda n: g8[n // 2, n % 2, 2:3, 0:128], 128, put), (64, 128))
+    pump(*q_tasks)
+    pump(*kv_tasks)
+    for task in f_tasks:
+        pump(task), pump(task)
     for task in q_tasks:
         drain(task)
-    pump(f_tasks[1])
     mark('qkv')
     def queries(i, carry):
         here = pl.ds(pl.multiple_of(240 * i, 16), 240)
         qkvo[0, i, 0:240, :] = dot(n1p[here, :], qo[:, :, :, :, 0:256].reshape(2048, 256), 1, 0).astype(BF)
         return carry
     lax.fori_loop(0, 2, queries, 0)
+    pump(*kv_tasks)
     for task in kv_tasks:
         drain(task)
     def keys(i, carry):
@@ -464,13 +495,11 @@
             qkvo[j, i, 240:304, :] = low[j][64 * i:64 * i + 64]
     saves = [comm.local(qo, out_q), comm.local(qoa, out_qa), comm.local(kv, out_kv), comm.local(kva, out_kva),
              comm.local(n1p, out_n1p), comm.local(n1a, out_n1a), comm.local(r1, out_r1), comm.local(g8, out_g)]
-    pump(c_task, f_tasks[2])
     mark('attn')
     for i in range(2):
         probs = soft(qkvo[0, i, 0:304, :], qkvo[1, i], lens[i])
         qkvo[3, i, 0:304, :] = dot(probs.astype(BF), qkvo[2, i], 1, 0).astype(BF)
     saves.append(comm.local(qkvo, out_qkvo))
-    pump(f_tasks[3], f_tasks[0])
     mark('outproj')
     oa = jnp.concatenate([qkvo[3, 0, 240:304, :], qkvo[3, 1, 240:304, :]], axis=0)
 
@@ -489,15 +518,13 @@
     terms(2)
     pump(sum_task)
     terms(1), terms(3)
-    pump(c_task)
+    pump(f_tasks[0], f_tasks[1])
     pump(sum_task)
     terms(0)
-    pump(f_tasks[4], f_tasks[1])
-    pump(f_tasks[0], f_tasks[2])
+    pump(f_tasks[2], f_tasks[3], f_tasks[4])
+    pump(f_tasks[0], f_tasks[1])
     pump(sum_task)
-    drain(c_task)
-    saves.append(comm.local(c16, out_c))
-    pump(f_tasks[1])
+    pump(f_tasks[2], f_tasks[3], f_tasks[4])
     drain(sum_task)
     mark('hmake')
     first.wait()
@@ -507,12 +534,13 @@
     mark('hplane')
     h_task = comm.plane_gather(lambda k, j, p: full.at[k, j, p], PARTS_A, PARTS_B)
     pump(h_task)
-    pump(f_tasks[0], f_tasks[3])
+    pump(f_tasks[0], f_tasks[1])
     pump(h_task)
-    pump(f_tasks[1], f_tasks[2], f_tasks[4])
     pump(h_task)
-    pump(f_tasks[3], f_tasks[4])
+    pump(f_tasks[2], f_tasks[3], f_tasks[4])
+    pump(f_tasks[0], f_tasks[1])
     pump(h_task)
+    pump(f_tasks[2], f_tasks[3])
     drain(h_task)
     saves.append(comm.local(full, out_h16))
     mark('norm2')
@@ -547,12 +575,12 @@
 def attend(lens, *args):
     wide5 = lambda n, c: (4, 2, 2, n, c)
     outs = [((CH,) + wide5(128, 768), BF), (wide5(64, 768), BF), (wide5(128, 512), BF), (wide5(64, 512), BF),
-            (wide5(128, 512), BF), (wide5(64, 512), BF), ((4, 4, T, 256), BF), ((4, 2, 8, 256), F32),
+            (wide5(128, 512), BF), (wide5(64, 512), BF), ((4, 2, 8, 256), F32),
             ((480, 2048), BF), ((128, 1024), BF), ((4, 2, KEYS, 256), BF), ((608, 128), F32), ((T, 256), F32),
             ((4, 4, T, 256), BF), ((960, 2048), BF), ((256, 1024), BF), ((608, 128), F32)]
     vm = pltpu.VMEM
     scratch = [vm((4, 2, 192, 128), BF), vm((192, 512), BF)] + [vm(s, d) for s, d in outs[2:6]] + [
-        vm((4, 2, T, 256), BF), vm((4, 4, T, 256), BF), vm((4, 2, 8, 256), F32), vm((480, 2048), BF), vm((128, 1024), BF),
+        vm((4, 2, T, 256), BF), vm((4, 2, 8, 256), F32), vm((480, 2048), BF), vm((128, 1024), BF),
         vm((4, 2, KEYS, 256), BF), vm((608, 128), F32), vm((T, 256), BF), vm((T, 256), F32), vm((4, 4, T, 256), BF),
         vm((960, 2048), BF), vm((256, 1024), BF), vm((2, 608, 128), F32), vm((4, 2, T, 256), BF)] + LAND_8
     return pl.pallas_call(
@@ -579,48 +607,41 @@
     return jnp.concatenate([full[x, z_low + zl, pl.ds(base, count), :] for x, zl in pairs8()], axis=1)
 
 
-def feed_forward_kernel(f, fa, n2p, n2a, c16, out_g2, out_g3, out_s0, out_s1, out_sa, out_d8, out_y,
-                        wv, wav, np_, na, gc, ga, dd, aa, dda, aaa, bb, bf, bn, d8, yb, g0, g1, ga_, s0, s1, sa,
-                        r0, r1, ra, z0, z1, za, *sems):
-    comm = Comm(*sems)
+def feed_forward_kernel(f, fa, n2p, n2a, cb, *refs):
+    out_s, out_late, refs = refs[:EARLY + 1], refs[EARLY + 1:CH + 1], refs[CH + 1:]
+    out_d8, out_y, out_c, wv, wav, np_, na, gc, ga, dd, aa, dda, aaa, bb, bf, bn, d8, grad_act = refs[:18]
+    lands = [refs[18 + 3 * i:21 + 3 * i] for i in range(EARLY + 1)]
+    comm = Comm(*refs[-3:])
     place = comm.place
-    loads = [comm.local(n2p, np_), comm.local(f.at[0], wv.at[0]), comm.local(c16, gc), comm.local(n2a, na),
+    loads = [comm.local(n2p, np_), comm.local(f.at[0], wv.at[0]), comm.local(n2a, na),
              comm.local(f.at[1], wv.at[1]), comm.local(f.at[2], wv.at[2]), comm.local(f.at[3], wv.at[3]),
              comm.local(fa, wav)]
+    c_task = plane_spread(comm, gc, cb)
     comm.enter(PEERS)
+    pump(c_task)
     mark("units")
     loads[0].wait()
+
+    def gate_up(left, weight):
+        both = dot(left, weight, 1, 0)
+        up = both[:, 256:512]
+        value, slope = gelu_parts(both[:, 0:256])
+        return (value * up).astype(BF), (up * slope).astype(BF), value.astype(BF)
+
     for i in range(CH):
-        loads[(1, 4, 5, 6)[i]].wait()
-        if i == 0:
-            loads[2].wait()
+        loads[(1, 3, 4, 5)[i]].wait()
         def unit(t, carry):
             here = pl.ds(pl.multiple_of(TILE * t, 16), TILE)
-            weight = lambda j: wv[i, :, :, :, :, 256 * j:256 * j + 256].reshape(2048, 256)
-            rows_n = np_[here, :]
-            gate, up = dot(rows_n, weight(0), 1, 0), dot(rows_n, weight(1), 1, 0)
-            rows_c = side_rows(gc, 2 * lax.div(t, 2), pl.multiple_of(TILE * lax.rem(t, 2), 16), TILE)
-            dact = dot(rows_c, weight(2), 1, 0)
-            value, slope = gelu_parts(gate)
-            aa[here, 256 * i:256 * i + 256] = (value * up).astype(BF)
-            dd[here, 512 * i:512 * i + 256] = (dact * up * slope).astype(BF)
-            dd[here, 512 * i + 256:512 * i + 512] = (dact * value).astype(BF)
+            a, b, c = gate_up(np_[here, :], wv[i, :, :, :, :, 0:512].reshape(2048, 512))
+            aa[here, 256 * i:256 * i + 256] = a
+            dd[here, 512 * i:512 * i + 256] = b
+            dd[here, 512 * i + 256:512 * i + 512] = c
             return carry
         lax.fori_loop(0, 4, unit, 0)
-    loads[3].wait(), loads[7].wait()
-    for zhi in range(2):
-        for i in range(2):
-            base = 128 * zhi + 64 * i
-            for n in range(8):
-                ga[base:base + 64, 128 * n:128 * n + 128] = gc[n // 2, 2 * zhi + n % 2, 480:544, 128 * i:128 * i + 128]
-    weight = lambda j: wav[:, :, :, :, 256 * j:256 * j + 256].reshape(1024, 256)
-    gate, up, dact = dot(na[...], weight(0), 1, 0), dot(na[...], weight(1), 1, 0), dot(ga[...], weight(2), 1, 0)
-    value, slope = gelu_parts(gate)
-    aaa[...] = (value * up).astype(BF)
-    dda[:, 0:256] = (dact * up * slope).astype(BF)
-    dda[:, 256:512] = (dact * value).astype(BF)
-
-    mark("back")
+        if i in (0, 1):
+            pump(c_task)
+    loads[2].wait(), loads[6].wait()
+    aaa[...], dda[:, 0:256], dda[:, 256:512] = gate_up(na[...], wav[:, :, :, :, 0:512].reshape(1024, 512))
 
     def product(ref, x, z, left, left_a, lo, hi):
         zh_, zl_ = lax.div(z, 2), lax.rem(z, 2)
@@ -632,6 +653,42 @@
         ref[480:544, 0:128] = small[0:64]
         ref[480:544, 128:256] = small[64:128]
 
+    def down_terms(t, carry):
+        x, z = lax.div(t, 4), lax.rem(t, 4)
+        product(bb.at[x, z], x, z, aa, aaa, 512, 768)
+        return carry
+
+    mark("ydown")
+    lax.fori_loop(0, 12, down_terms, 0)
+    pump(c_task)
+    lax.fori_loop(12, 16, down_terms, 0)
+    saves = [comm.local(bb, out_y)]
+    mark("cwait")
+    drain(c_task)
+    saves.append(comm.local(gc.at[:, pl.ds(2 * place.zh, 2)], out_c))
+    mark("dact")
+    for i in range(CH):
+        def dact_unit(t, carry):
+            here = pl.ds(pl.multiple_of(TILE * t, 16), TILE)
+            rows_c = side_rows(gc, 2 * lax.div(t, 2), pl.multiple_of(TILE * lax.rem(t, 2), 16), TILE)
+            dact = dot(rows_c, wv[i, :, :, :, :, 512:768].reshape(2048, 256), 1, 0)
+            for j in range(2):
+                there = slice(512 * i + 256 * j, 512 * i + 256 * j + 256)
+                dd[here, there] = (dact * dd[here, there].astype(F32)).astype(BF)
+            return carry
+        lax.fori_loop(0, 4, dact_unit, 0)
+    for zhi in range(2):
+        for i in range(2):
+            base = 128 * zhi + 64 * i
+            for n in range(8):
+                ga[base:base + 64, 128 * n:128 * n + 128] = gc[n // 2, 2 * zhi + n % 2, 480:544, 128 * i:128 * i + 128]
+    dact = dot(ga[...], wav[:, :, :, :, 512:768].reshape(1024, 256), 1, 0)
+    for j in range(2):
+        there = slice(256 * j, 256 * j + 256)
+        dda[:, there] = (dact * dda[:, there].astype(F32)).astype(BF)
+    saves[0].wait()
+
+    mark("back")
     far_x, far_z = place.off("x", 2), place.off("z", 2)
 
     def far_terms(t, carry):
@@ -653,7 +710,7 @@
 
     mark("grads")
 
-    def weight_grads(grad, i):
+    def weight_grads(i):
         def block_rows(y, carry):
             here = pl.ds(pl.multiple_of(512 * y, 512), 512)
             left_n = np_[:, here]
@@ -664,88 +721,88 @@
                     value = dot(left_n, dd[:, 512 * i + 256 * j:512 * i + 256 * j + 256], 0, 0).astype(BF)
                 else:
                     value = dot(left_c, aa[:, 256 * i:256 * i + 256], 0, 0).astype(BF)
-                for q in range(4):
-                    grad[q % 2, y, q // 2, :, 256 * j:256 * j + 256] = value[128 * q:128 * q + 128]
+                wv[i, y, :, :, :, 256 * j:256 * j + 256] = value.reshape(2, 2, 128, 256)
             return carry
         lax.fori_loop(0, 4, block_rows, 0)
 
-    weight_grads(g0, 0)
-    w0 = wide_sum(comm, g0, s0, r0.at[0], r0.at[1], r0.at[2], z0, 128, False)
-    pump(w0)
-    weight_grads(g1, 1)
-    w1 = wide_sum(comm, g1, s1, r1.at[0], r1.at[1], r1.at[2], z1, 128, False)
-    pump(w0, w1)
+    def act_grads():
+        for y in range(4):
+            left_n, left_c = na[:, 256 * y:256 * y + 256], ga[:, 256 * y:256 * y + 256]
+            for j in range(3):
+                value = dot(left_n, dda[:, 256 * j:256 * j + 256], 0, 0) if j < 2 else dot(left_c, aaa[...], 0, 0)
+                grad_act[y, :, :, :, 256 * j:256 * j + 256] = value.astype(BF).reshape(2, 2, 64, 256)
+
+    grads = [wv.at[i] for i in range(EARLY)] + [grad_act]
+    sums = [wide_sum(comm, grad, s, r.at[0], r.at[1], r.at[2], z, 64 if i == EARLY else 128, False)
+            for i, (grad, (s, r, z)) in enumerate(zip(grads, lands))]
+    weight_grads(0)
+    pump(sums[0])
+    weight_grads(1)
+    pump(sums[0], sums[1])
     pump(b_task)
-    for y in range(4):
-        left_n, left_c = na[:, 256 * y:256 * y + 256], ga[:, 256 * y:256 * y + 256]
-        for j in range(3):
-            value = dot(left_n, dda[:, 256 * j:256 * j + 256], 0, 0) if j < 2 else dot(left_c, aaa[...], 0, 0)
-            value = value.astype(BF)
-            for q in range(4):
-                ga_[q % 2, y, q // 2, :, 256 * j:256 * j + 256] = value[64 * q:64 * q + 64]
-    wa = wide_sum(comm, ga_, sa, ra.at[0], ra.at[1], ra.at[2], za, 64, False)
-    pump(wa, w0, w1)
+    act_grads()
+    pump(sums[2])
+    pump(sums[1])
+    weight_grads(2)
+    saves.append(comm.local(wv.at[2], out_late[0]))
     pump(b_task)
+    pump(sums[0])
+    pump(sums[2])
     drain(b_task)
     mark("dn2")
     d8[place.x, place.zl] = bb[place.x, place.z]
     d_task = comm.pair_ring_gather("zl", "x", lambda k, j, p: d8.at[k, j, p], PARTS_8,
                                    lambda p: d8.at[place.x, place.zl, p], d8.at[place.x, place.zl], slice(None))
+    pump(d_task), pump(d_task)
+    pump(sums[1])
+    weight_grads(3)
+    saves.append(comm.local(wv.at[3], out_late[1]))
+    pump(d_task), pump(d_task)
+    pump(sums[0], sums[2])
     pump(d_task)
-    pump(wa, w0, w1)
-    mark("late")
-    late = []
-    for i, out in ((2, out_g2), (3, out_g3)):
-        pump(d_task)
-        weight_grads(yb, i)
-        late.append(comm.local(yb, out))
-        late[-1].wait()
-        pump(w0, w1, wa)
-    mark("ydown")
-
-    def down_terms(t, carry):
-        x, z = lax.div(t, 4), lax.rem(t, 4)
-        product(bb.at[x, z], x, z, aa, aaa, 512, 768)
-        return carry
-
+    pump(sums[1], sums[2])
     drain(d_task)
-    comm.settle()
-    lax.fori_loop(0, 16, down_terms, 0)
-    saves = [comm.local(bb, out_y), comm.local(d8, out_d8)]
-    for task in (w0, w1, wa):
+    saves.append(comm.local(d8, out_d8))
+    mark("sums")
+    for task in sums:
         drain(task)
-    for grad, swap, out in ((g0, z0, out_s0), (g1, z1, out_s1), (ga_, za, out_sa)):
-        saves.append(comm.local(grad.at[place.core, place.y, place.zh], out.at[place.zh]))
+    for grad, (_, _, swap), out in zip(grads, lands, out_s):
+        saves.append(comm.local(grad.at[place.y, place.zh, place.core], out.at[place.zh]))
         saves.append(comm.local(swap, out.at[1 - place.zh]))
-    for copy in saves:
+    for copy in saves[1:]:
         copy.wait()
     mark(None)
     comm.close()
 
 
-def feed_forward(f, fa, n2p, n2a, c16):
-    grad = (2, 4, 2, 128, 768)
-    outs = [(grad, BF), (grad, BF), ((2, 128, 768), BF), ((2, 128, 768), BF), ((2, 64, 768), BF),
-            ((4, 2, T, 256), BF), ((4, 4, T, 256), BF)]
+def feed_forward(f, fa, n2p, n2a, cb):
+    grad = (4, 2, 2, 128, 768)
+    outs = [(2, 128, 768)] * EARLY + [(2, 64, 768)] + [grad] * (CH - EARLY) + [(4, 2, T, 256), (4, 4, T, 256), (4, 2, T, 256)]
     vm = lambda *s: pltpu.VMEM(s, BF)
-    scratch = [vm(CH, 4, 2, 2, 128, 768), vm(4, 2, 2, 64, 768), vm(960, 2048), vm(256, 1024), vm(4, 4, T, 256),
+    scratch = [vm(CH, *grad), vm(4, 2, 2, 64, 768), vm(960, 2048), vm(256, 1024), vm(4, 4, T, 256),
                vm(256, 1024), vm(960, 2048), vm(960, 1024), vm(256, 512), vm(256, 256)]
-    scratch += [vm(4, 4, T, 256)] + LAND_16 + [vm(4, 2, T, 256), vm(*grad)]
-    scratch += [vm(*grad), vm(*grad), vm(2, 4, 2, 64, 768), vm(*grad[1:]), vm(*grad[1:]), vm(4, 2, 64, 768)]
-    scratch += [vm(3, 2, 128, 768), vm(3, 2, 128, 768), vm(3, 2, 64, 768), vm(128, 768), vm(128, 768), vm(64, 768)]
+    scratch += [vm(4, 4, T, 256)] + LAND_16 + [vm(4, 2, T, 256), vm(4, 2, 2, 64, 768)]
+    for n in [128] * EARLY + [64]:
+        scratch += [vm(4, 2, n, 768), vm(3, 2, n, 768), vm(n, 768)]
     return pl.pallas_call(
         feed_forward_kernel,
-        out_shape=[jax.ShapeDtypeStruct(s, d) for s, d in outs],
+        out_shape=[jax.ShapeDtypeStruct(s, BF) for s in outs],
         in_specs=[ANY] * 5,
         out_specs=[ANY] * len(outs),
         scratch_shapes=scratch + SEM_SCRATCH,
         compiler_params=pltpu.CompilerParams(collective_id=2, has_side_effects=True, vmem_limit_bytes=VMEM_CAP),
         name="feed_forward",
-    )(f, fa, n2p, n2a, c16)
+    )(f, fa, n2p, n2a, cb)
+TS = T + 16
+SUM_PARTS = [(rows(0, 272), 1), (rows(272, TS), -1)]
+FAR_PEERS = tuple(f"w{step}{flip}" for step, flip in CHIPS if (step, flip) not in ((1, 0), (3, 0), (0, 1)))
+KV_PARTS = [(rows(0, 160), 1), (rows(160, 304), -1)]
+
+
 def attend_back_kernel(lens, d8, h16, c16, r2, r1, g8, qo, qoa, kv, kva, n1p, n1a, qkvo, xb, cotb, g2, g3, yt, h_own,
-                       out_s2, out_s3, out_q, out_qa, out_kv, out_x, out_y, out_g,
+                       out_s2, out_s3, out_q, out_qa, out_kv, out_kva, out_x, out_y, out_g,
                        dv8, hv, cv, r2v, r1v, g8v, qov, qoav, kvv, kvav, npv, nav, qv, xv, cotv, g2v, g3v, yv, how,
-                       mean, ghp, gha, dhb, dov, dqp, dqa, stat, st8, gains, gsum, gains16, outx, outy,
+                       mean, ghp, gha, dhb, dov, dqp, dqa, stat, gains, gsum, gains16, gains2, outx, outy,
                        gq, gkv, gqa, gkva, kvb, blocks, yf, yn, l0, l1, l2, l3, k0, k1, k2, k3,
                        s2, s3, sq, skv, sqa, skva, t2, t3, tq, tkv, tqa, tkva, z2, z3, zq, zkv, zqa, zkva, *sems):
     comm = Comm(*sems)
@@ -753,12 +810,21 @@
     x, y, zh, zl, core = place.x, place.y, place.zh, place.zl, place.core
     side = pl.ds(2 * zh, 2)
     load = comm.local
-    la = [load(d8, dv8), load(h16.at[:, side], hv), load(r2, r2v), load(g8, g8v), load(c16.at[:, side], cv), load(cotb, cotv)]
+    la = [load(d8, dv8), load(h16.at[:, side], hv), load(r2, r2v), load(g8, g8v), load(c16, cv), load(cotb, cotv)]
+    ly = load(yt, yv)
     lg = [load(g2, g2v), load(g3, g3v)]
     lb = [load(qo, qov), load(qoa, qoav), load(qkvo, qv)]
-    ly = load(yt, yv)
     lc = [load(kv, kvv), load(kva, kvav), load(n1p, npv), load(n1a, nav), load(xb, xv), load(r1, r1v), load(h_own, how)]
-    comm.enter(PEERS)
+    comm.enter(PEERS + FAR_PEERS)
+    late = [wide_sum(comm, g2v, s2, t2.at[0], t2.at[1], t2.at[2], z2, 128, False),
+            wide_sum(comm, g3v, s3, t3.at[0], t3.at[1], t3.at[2], z3, 128, False)]
+    y_task = plane_sum(comm, yv, yf, yn)
+    ly.wait()
+    pump(y_task)
+    lg[0].wait()
+    pump(late[0])
+    lg[1].wait()
+    pump(late[1])
     mark("dh")
     for copy in la:
         copy.wait()
@@ -783,6 +849,8 @@
         for n in range(8):
             value = cv[n // 2, n % 2, here, lanes].astype(F32) + scale_a * (grad_a(n) - unit_a(n) * m)
             gha[64 * i:64 * i + 64, 128 * n:128 * n + 128] = value.astype(BF)
+    pump(late[0])
+    pump(late[1])
     mark("attnback")
     for copy in lb:
         copy.wait()
@@ -792,6 +860,7 @@
     low = dot(gha[...], qoav[:, :, :, :, 256:512].reshape(1024, 256), 1, 0).astype(BF)
     for i in range(2):
         dov[i, 240:304, :] = low[64 * i:64 * i + 64]
+    pump(y_task)
     for i in range(2):
         q, k, v, do = qv[0, i, 0:304, :], qv[1, i], qv[2, i], dov[i]
         probs = soft(q, k, lens[i])
@@ -808,7 +877,24 @@
         stat[240 * i:240 * i + 240, :] = total[0:240]
         stat[480 + 64 * i:544 + 64 * i, :] = total[240:304]
     stat[608:640, :] = jnp.zeros((32, 128), F32)
-    st8[x, zl] = stat[...].T[0:8]
+    line = stat[...].T[0:1]
+    line = jnp.concatenate([line[:, 0:256], line[:, 256:512], jnp.concatenate([line[:, 512:640], jnp.zeros((1, 128), F32)], axis=1),
+                            jnp.zeros((13, 256), F32)], axis=0).astype(BF)
+    for n in range(8):
+        blocks[n // 2, n % 2, T:TS, :] = line
+    lane = lax.broadcasted_iota(jnp.int32, (512, 128), 1)
+    col = lax.broadcasted_iota(jnp.int32, (512, 128), 0)
+    kv_sum = block_sum(comm, kvb, (k0, k1, k2), k3, KV_PARTS)
+    for n in range(8):
+        total = []
+        for i in range(2):
+            at = lane - 64 * i
+            pick = ((at >= 0) & (at < 32) & (col == 32 * n + at)) | ((at >= 32) & (at < 64) & (col == 224 + 32 * n + at))
+            pick = pick.astype(F32).astype(BF)
+            total.append((dot(dqp[240 * i:240 * i + 240, 256:768], pick, 1, 0), dot(dqa[64 * i:64 * i + 64, 256:768], pick, 1, 0)))
+        kvb[n // 2, n % 2, 0:240, :] = (total[0][0] + total[1][0]).astype(BF)
+        kvb[n // 2, n % 2, 240:304, :] = (total[0][1] + total[1][1]).astype(BF)
+    pump(kv_sum)
     for copy in lc:
         copy.wait()
     mark("terms")
@@ -823,60 +909,66 @@
             for i in range(2):
                 blocks[k, j, 480:544, 128 * i:128 * i + 128] = small[64 * i:64 * i + 64]
 
-    terms(2)
-    sum_task = block_sum(comm, blocks, (l0, l1, l2), l3)
-    pump(sum_task)
-    stat_task = comm.pair_ring_gather("zl", "x", lambda k, j, p: st8.at[k, j, p], [(slice(None), 1)],
-                                      lambda p: st8.at[x, zl, p], st8.at[x, zl], slice(None))
-    pump(stat_task)
-    terms(1), terms(3)
-    pump(sum_task)
-    terms(0)
-
     def outer(grad, n, left, right, lo, width):
         def block_rows(k, carry):
             here = pl.ds(pl.multiple_of(4 * n * k, 4 * n), 4 * n)
             value = dot(left[:, here], right, 0, 0).astype(BF)
-            for c in range(4):
-                grad[c % 2, k, c // 2, :, lo:lo + width] = value[n * c:n * c + n]
+            grad[k, :, :, :, lo:lo + width] = value.reshape(2, 2, n, width)
             return carry
         lax.fori_loop(0, 4, block_rows, 0)
 
+    terms(2)
+    sum_task = block_sum(comm, blocks, (l0, l1, l2), l3, SUM_PARTS)
+    pump(sum_task)
+    terms(1), terms(3)
     mark("attngrads")
-    outer(gkv, 128, npv, dqp[:, 256:768], 0, 512)
-    outer(gkva, 64, nav, dqa[:, 256:768], 0, 512)
-    kv_tasks = [wide_sum(comm, gkv, skv, tkv.at[0], tkv.at[1], tkv.at[2], zkv, 128, True),
-                wide_sum(comm, gkva, skva, tkva.at[0], tkva.at[1], tkva.at[2], zkva, 64, True)]
-    pump(*kv_tasks)
-    outer(gq, 128, npv, dqp[:, 0:256], 0, 256)
     o_act = jnp.concatenate([qv[3, 0, 240:304, :], qv[3, 1, 240:304, :]], axis=0)
     o_pre = jnp.concatenate([qv[3, 0, 0:240, :], qv[3, 1, 0:240, :]], axis=0)
     outer(gq, 128, ghp, o_pre, 256, 256)
+    outer(gqa, 64, gha, o_act, 256, 256)
+    pump(late[0], late[1])
+    terms(0)
+    outer(gq, 128, npv, dqp[:, 0:256], 0, 256)
     outer(gqa, 64, nav, dqa[:, 0:256], 0, 256)
-    outer(gqa, 64, gha, o_act, 256, 256)
     q_tasks = [wide_sum(comm, gq, sq, tq.at[0], tq.at[1], tq.at[2], zq, 128, True),
                wide_sum(comm, gqa, sqa, tqa.at[0], tqa.at[1], tqa.at[2], zqa, 64, True)]
+    kv_tasks = [wide_sum(comm, gkv, skv, tkv.at[0], tkv.at[1], tkv.at[2], zkv, 128, True),
+                wide_sum(comm, gkva, skva, tkva.at[0], tkva.at[1], tkva.at[2], zkva, 64, True)]
     pump(*q_tasks)
+    pump(kv_sum)
+    pump(y_task)
+    pump(*q_tasks)
+    pump(sum_task)
+    pump(kv_sum)
+    pump(y_task)
+    drain(kv_sum)
+    own = kvb[x, zl]
+    share = []
+    for i in range(2):
+        lane = lax.broadcasted_iota(jnp.int32, (128, 128), 0)
+        col = lax.broadcasted_iota(jnp.int32, (128, 128), 1)
+        pick = ((col < 64) & (lane == col + 64 * i)).astype(F32).astype(BF)
+        share.append(dot(own, pick, 1, 0).astype(BF))
+    outer(gkv, 128, npv, jnp.concatenate([share[0][0:240], share[1][0:240]], axis=0), 0, 128)
+    outer(gkva, 64, nav, jnp.concatenate([share[0][240:304], share[1][240:304]], axis=0), 0, 128)
     pump(*kv_tasks)
     mark("late")
-    for copy in lg:
-        copy.wait()
-    late = [wide_sum(comm, g2v, s2, t2.at[0], t2.at[1], t2.at[2], z2, 128, False),
-            wide_sum(comm, g3v, s3, t3.at[0], t3.at[1], t3.at[2], z3, 128, False)]
-    pump(*late)
-    ly.wait()
-    y_task = plane_sum(comm, yv, yf, yn)
-    pump(y_task)
-    pump(stat_task, sum_task)
-    pump(*q_tasks), pump(*kv_tasks)
-    pump(*late)
-    pump(stat_task, y_task)
-    drain(sum_task), drain(stat_task)
+    pump(late[0], late[1])
+    pump(*kv_tasks)
+    pump(*q_tasks)
+    pump(sum_task)
+    pump(*kv_tasks)
+    drain(y_task)
+    outy[...] = (yv[x, place.z].astype(F32) + how[...]).astype(BF)
+    saves = [load(outy, out_y)]
+    pump(*q_tasks)
+    drain(sum_task)
     mark("dx")
     g_pre, g_act = g8v[x, zl, 0:1, :], g8v[x, zl, 2:3, 0:128]
     f_pre, f_act = g8v[x, zl, 1:2, :], g8v[x, zl, 2:3, 128:256]
-    total = sum(st8[n // 2, n % 2] for n in range(8))
-    stat[...] = jnp.broadcast_to(total[0:1], (128, 640)).T
+    line = blocks[x, zl, T:TS, :].astype(F32)
+    line = jnp.concatenate([line[0:1], line[1:2], line[2:3, 0:128]], axis=1)
+    stat[...] = jnp.broadcast_to(line, (128, 640)).T
 
     def own_norm(here, there, lanes, gain_f, gain_a, width):
         s2_, s1_ = r2v[there, 0:1], r1v[there, 0:1]
@@ -892,34 +984,20 @@
     gains[...] = jnp.concatenate(
         [pre[0][0] + pre[1][0], pre[0][1] + pre[1][1],
          jnp.concatenate([act[0][0] + act[1][0], act[0][1] + act[1][1]], axis=1), jnp.zeros((5, 256), F32)], axis=0)
-    saves = [load(outx, out_x)]
-    g_task = wide_gather(comm, gains16, gains, gains, 8, [(slice(None), 1)])
+    saves.append(load(outx, out_x))
+    g_task = small_total(comm, gains16, gains2, gains, gsum)
     pump(g_task)
     mark("tail")
-    pump(y_task, g_task), pump(*late), pump(g_task)
-    pump(*kv_tasks), pump(*q_tasks), pump(g_task, y_task)
-    drain(kv_tasks[0]), drain(kv_tasks[1])
-    own = jnp.concatenate([gkv[core, y, zh], gkva[core, y, zh]], axis=0)
-    lane = lax.broadcasted_iota(jnp.int32, (128, 512), 0)
-    col = lax.broadcasted_iota(jnp.int32, (128, 512), 1)
-    for n in range(8):
-        pick = ((lane < 32) & (col == 32 * n + lane)) | ((lane >= 32) & (lane < 64) & (col == 224 + 32 * n + lane))
-        kvb[n // 2, n % 2] = dot(own, pick.astype(F32).astype(BF), 1, 1).astype(BF)
-    share = block_sum(comm, kvb, (k0, k1, k2), k3, halves(192))
-    pump(share)
-    pump(g_task), pump(*late), pump(*q_tasks)
-    pump(share)
-    drain(y_task)
-    outy[...] = (yv[x, place.z].astype(F32) + how[...]).astype(BF)
-    saves.append(load(outy, out_y))
-    pump(share, g_task)
-    for task in q_tasks + late:
+    pump(g_task)
+    pump(*kv_tasks)
+    pump(g_task)
+    pump(*q_tasks)
+    for task in q_tasks + kv_tasks + late:
         drain(task)
-    drain(share), drain(g_task)
-    gsum[...] = sum(gains16[a, b, c] for a in range(4) for b in range(2) for c in range(2))
-    saves += [load(gsum, out_g), load(kvb.at[x, zl], out_kv), load(gq.at[core, y, zh], out_q), load(gqa.at[core, y, zh], out_qa)]
-    for grad, swap, out in ((g2v, z2, out_s2), (g3v, z3, out_s3)):
-        saves += [load(grad.at[core, y, zh], out.at[zh]), load(swap, out.at[1 - zh])]
+    drain(g_task)
+    saves += [load(gsum, out_g), load(gkv.at[y, zh, core], out_kv), load(gkva.at[y, zh, core], out_kva), load(gq.at[y, zh, core], out_q), load(gqa.at[y, zh, core], out_qa)]
+    saves += [load(g2v.at[y, zh, core], out_s2.at[zh]), load(z2, out_s2.at[1 - zh])]
+    saves += [load(g3v.at[y, zh, core], out_s3.at[zh]), load(z3, out_s3.at[1 - zh])]
     for copy in saves:
         copy.wait()
     mark(None)
@@ -927,20 +1005,20 @@
 
 
 def attend_back(lens, *args):
-    outs = [((2, 128, 768), BF), ((2, 128, 768), BF), ((128, 512), BF), ((64, 512), BF), ((192, 128), BF), ((T, 256), F32),
+    outs = [((2, 128, 768), BF), ((2, 128, 768), BF), ((128, 512), BF), ((64, 512), BF), ((128, 128), BF), ((64, 128), BF), ((T, 256), F32),
             ((T, 256), BF), ((8, 256), F32)]
     vm = lambda *s: pltpu.VMEM(s, BF)
     vf = lambda *s: pltpu.VMEM(s, F32)
-    wide = lambda n, c: (2, 4, 2, n, c)
-    back = [(128, 768), (128, 768), (128, 512), (128, 512), (64, 512), (64, 512)]
+    wide = lambda n, c: (4, 2, 2, n, c)
+    back = [(128, 768), (128, 768), (128, 512), (128, 128), (64, 512), (64, 128)]
     scratch = [vm(4, 2, T, 256), vm(4, 2, T, 256), vm(4, 2, T, 256), vf(608, 128), vf(608, 128), vf(4, 2, 8, 256),
                vm(4, 2, 2, 128, 512), vm(4, 2, 2, 64, 512), vm(4, 2, 2, 128, 512), vm(4, 2, 2, 64, 512),
                vm(480, 2048), vm(128, 1024), vm(4, 2, KEYS, 256), vm(T, 256), vf(T, 256), vm(*wide(128, 768)),
                vm(*wide(128, 768)), vm(4, 4, T, 256), vf(T, 256)]
     scratch += [vf(608, 128), vm(480, 2048), vm(128, 1024), vf(8, 128), vm(2, 304, 256), vm(480, 768), vm(128, 768),
-                vf(640, 128), vf(4, 2, 8, 640), vf(8, 256), vf(8, 256), vf(4, 2, 2, 8, 256), vf(T, 256), vm(T, 256)]
+                vf(640, 128), vf(8, 256), vf(8, 256), vf(8, 8, 256), vf(2, 8, 256), vf(T, 256), vm(T, 256)]
     scratch += [vm(*wide(n, c)) for n, c in back[2:]]
-    scratch += [vm(4, 2, 192, 128), vm(4, 2, T, 256)] + LAND_16 + LAND_8 + [vm(2, 192, 128)] * 3 + [vm(192, 128)]
+    scratch += [vm(4, 2, 304, 128), vm(4, 2, TS, 256)] + LAND_16 + [vm(2, TS, 256)] * 3 + [vm(TS, 256)] + [vm(2, 304, 128)] * 3 + [vm(304, 128)]
     scratch += [vm(4, 2, n, c) for n, c in back] + [vm(3, 2, n, c) for n, c in back] + [vm(n, c) for n, c in back]
     return pl.pallas_call(
         attend_back_kernel,
@@ -960,11 +1038,11 @@
     kvs = jnp.pad(kvs, ((0, 0), (0, 64)))
     xb, cot = pack_tokens(x_pre, x_act), pack_tokens(cot_pre, cot_act)
     gb = jnp.pad(jnp.stack([attn_gain_pre, ffn_gain_pre, jnp.concatenate([attn_gain_act, ffn_gain_act])]), ((0, 5), (0, 0)))
-    (f, fa, qo, qoa, kv, kva, c16, g8, n1p, n1a, qkvo, r1, h_own, h16, n2p, n2a, r2) = attend(
-        lengths, wf, wfa, wq, wqa, kvs, xb, cot.astype(BF), gb)
-    g2, g3, s0, s1, sa, d8, yt = feed_forward(f, fa, n2p, n2a, c16)
-    s2, s3, sq, sqa, skv, gx, y, gains = attend_back(
-        lengths, d8, h16, c16, r2, r1, g8, qo, qoa, kv, kva, n1p, n1a, qkvo, xb, cot, g2, g3, yt, h_own)
+    (f, fa, qo, qoa, kv, kva, g8, n1p, n1a, qkvo, r1, h_own, h16, n2p, n2a, r2) = attend(
+        lengths, wf, wfa, wq, wqa, kvs, xb, gb)
+    s0, s1, sa, g2, g3, d8, yt, c8 = feed_forward(f, fa, n2p, n2a, cot.astype(BF))
+    s2, s3, sq, sqa, skv, skva, gx, y, gains = attend_back(
+        lengths, d8, h16, c8, r2, r1, g8, qo, qoa, kv, kva, n1p, n1a, qkvo, xb, cot, g2, g3, yt, h_own)
     unact = lambda m: m.reshape(64, 2, 128)[:50].transpose(1, 0, 2)
 
     def open_hidden(m, n):
@@ -974,10 +1052,10 @@
 
     dgate_p, dup_p, ddown_p = open_hidden(jnp.stack([s0, s1, s2, s3], axis=1), 128)
     dgate_a, dup_a, ddown_a = open_hidden(sa, 64)
-    sq, sqa, skv = sq.astype(F32), sqa.astype(F32), skv.astype(F32)
+    sq, sqa, skv, skva = (m.astype(F32) for m in (sq, sqa, skv, skva))
     return (y[:480].reshape(2, 240, 256), unact(y[480:]), gx[:480].reshape(2, 240, 256), unact(gx[480:]),
-            gains[0], sq[:, :256], skv[:128, :32], skv[:128, 32:64], sq[:, 256:].T, gains[1], dgate_p, dup_p, ddown_p,
-            gains[2, :128], sqa[:, :256], skv[128:, :32], skv[128:, 32:64], sqa[:, 256:].T, gains[2, 128:],
+            gains[0], sq[:, :256], skv[:, :32], skv[:, 32:64], sq[:, 256:].T, gains[1], dgate_p, dup_p, ddown_p,
+            gains[2, :128], sqa[:, :256], skva[:, :32], skva[:, 32:64], sqa[:, 256:].T, gains[2, 128:],
             dgate_a, dup_a, ddown_a)
 
 

time: 417 us -> 344 us (0.82)
  Pallas kernels: 378 us -> 307 us
    pallas_call x1, Pallas kernels: 173 us -> 122 us  [attend(): pl.pallas_call(attend_kernel, out_shape=[jax.ShapeDtypeStruct(s, d) for s...]
    pallas_call x1, Pallas kernels: 103 us -> 76.4 us  [attend_back(): pl.pallas_call(attend_back_kernel, out_shape=[jax.ShapeDtypeStruct(s, d)...]
    pallas_call x1, Pallas kernels: 102 us -> 108 us  [feed_forward(): pl.pallas_call(feed_forward_kernel, out_shape=[jax.ShapeDtypeStruct(s, BF...]
    unnamed x71 -> x73, local copies, waits for them, and re-layouts: 9.33 us -> 10.4 us
where the time goes in v3:
time: 344 us; the launch traced here: 342 us
  Pallas kernels  307 us (89%)
  local copies, waits for them, and re-layouts  24.3 us (7%)
  other arithmetic  9.34 us (3%)
    pallas_call x1, Pallas kernels, attend(): pl.pallas_call(attend_kernel, out_shape=[jax.ShapeDtypeStruct(s, d) for s...  122 us
    pallas_call x1, Pallas kernels, feed_forward(): pl.pallas_call(feed_forward_kernel, out_shape=[jax.ShapeDtypeStruct(s, BF...  108 us
    pallas_call x1, Pallas kernels, attend_back(): pl.pallas_call(attend_back_kernel, out_shape=[jax.ShapeDtypeStruct(s, d)...  76.4 us
    unnamed x73, local copies, waits for them, and re-layouts  10.4 us

profile of v3, /device:TPU:0, one launch (start us, length us, event | category | flops | bytes accessed | tf_op | source)
XLA Modules:
  0.0 341.6 jit_solution(15230556175995007499)
XLA Ops:
  0.7 0.9 fusion.15
  1.6 1.7 pad_maximum_fusion.1.xb
  3.2 1.4 copy.59
  5.8 1.3 maximum_bitcast_fusion.wf
  7.2 0.7 maximum_bitcast_fusion.1.wfa
  9.2 0.7 fusion.7.kvs
  11.2 122.1 %attend.1 = (bf16[4,4,2,2,128,768]{5,4,3,2,1,0:T(8,128)(2,1)}, bf16[4,2,2,64,768]{4,3,2,1,0:T(8,128)(2,1)}, bf16[4,2,2,128,512]{4,3,2,1,0:T(8,128)(2,1)}, bf16[4...) custom-call(s32[2]{0:T(128)} %lens.3, ...), custom_call_target="tpu_custom_call" | custom-call | tf_op jit(solution)/shard_map/attend/pallas_call | solution.py:586
  133.4 0.7 fusion.10.cb
  134.1 108.0 %feed_forward.1 = (bf16[2,128,768]{2,1,0:T(8,128)(2,1)}, bf16[2,128,768]{2,1,0:T(8,128)(2,1)}, bf16[2,64,768]{2,1,0:T(8,128)(2,1)}, bf16[4,2,2,128,768]{4,3,2,1,...) custom-call(bf16[4,4,2,2,128,768]{5,4,3,2,1,0:T(8,128)(2,1)} %get-tu, ...), custom_call_target="tpu_custom_call" | custom-call | tf_op jit(solution)/shard_map/feed_forward/pallas_call | solution.py:787
  242.1 0.8 pad_maximum_fusion.cotb
  243.0 76.4 %attend_back.1 = (bf16[2,128,768]{2,1,0:T(8,128)(2,1)}, bf16[2,128,768]{2,1,0:T(8,128)(2,1)}, bf16[128,512]{1,0:T(8,128)(2,1)}, bf16[64,512]{1,0:T(8,128)(2,1)},...) custom-call(s32[2]{0:T(128)} %lens.3, ...), custom_call_target="tpu_custom_call" | custom-call | tf_op jit(solution)/shard_map/attend_back/pallas_call | solution.py:1023
  319.4 1.4 convert_bitcast_fusion
  320.8 1.3 fusion.11
  322.1 1.5 copy.76
  323.7 1.3 copy.85
  325.3 1.3 copy.86
  326.7 1.3 copy.78
  328.0 0.8 copy.84
  328.8 0.8 slice.95
  329.6 0.7 slice.92
  331.0 0.7 copy.82
  333.8 0.7 copy.87
  336.4 1.3 fusion.17
  337.8 1.2 slice_bitcast_fusion.2
  (103 shorter events, 11.2 us)
Async XLA Ops:
  0.7 4.2 %copy-start.3 = (bf16[128,2048]{1,0:T(8,128)(2,1)S(1)}, bf16[128,2048]{1,0:T(8,128)(2,1)}, u32[]{:S(2)}) copy-start(bf16[128,2048]{1,0:T(8,128)(2,1)} %param.35) | copy-start | bytes 1572868
  5.6 2.3 copy-start.15
  5.6 2.4 copy-start.16
  5.6 3.1 copy-start.20
  5.7 3.2 copy-start.21
  5.7 3.3 copy-start.22
  5.7 3.4 copy-start.23
  5.7 4.2 %copy-start.18 = (bf16[256,64]{0,1:T(8,128)(2,1)S(1)}, bf16[256,64]{0,1:T(8,128)(2,1)}, u32[]{:S(2)}) copy-start(bf16[256,64]{0,1:T(8,128)(2,1)} %param.41) | copy-start | bytes 98308
  5.7 4.2 %copy-start.19 = (bf16[64,256]{1,0:T(8,128)(2,1)S(1)}, bf16[64,256]{1,0:T(8,128)(2,1)}, u32[]{:S(2)}) copy-start(bf16[64,256]{1,0:T(8,128)(2,1)} %param.38) | copy-start | bytes 98308
  5.7 4.8 %copy-start.26 = (f32[128]{0:T(128)S(1)}, f32[128]{0:T(128)}, u32[]{:S(2)}) copy-start(f32[128]{0:T(128)} %param.42) | copy-start | bytes 1540
  5.7 4.8 %copy-start.27 = (f32[128]{0:T(128)S(1)}, f32[128]{0:T(128)}, u32[]{:S(2)}) copy-start(f32[128]{0:T(128)} %param.37) | copy-start | bytes 1540
  5.7 4.8 %copy-start.24 = (f32[256]{0:T(256)S(1)}, f32[256]{0:T(256)}, u32[]{:S(2)}) copy-start(f32[256]{0:T(256)} %param.33) | copy-start | bytes 3076
  5.7 4.8 %copy-start.25 = (f32[256]{0:T(256)S(1)}, f32[256]{0:T(256)}, u32[]{:S(2)}) copy-start(f32[256]{0:T(256)} %param.28) | copy-start | bytes 3076
  7.1 126.2 %copy-start.17 = (f32[2,50,128]{2,0,1:T(2,128)S(1)}, f32[2,50,128]{2,0,1:T(2,128)}, u32[]{:S(2)}) copy-start(f32[2,50,128]{2,0,1:T(2,128)} %param.27) | copy-start | bytes 153604
  7.2 126.2 %copy-start = (f32[2,240,256]{2,1,0:T(8,128)S(1)}, f32[2,240,256]{2,1,0:T(8,128)}, u32[]{:S(2)}) copy-start(f32[2,240,256]{2,1,0:T(8,128)} %param.26) | copy-start | bytes 1474564
  243.0 76.4 %copy-start.6 = (bf16[2,128,768]{2,1,0:T(8,128)(2,1)S(1)}, bf16[2,128,768]{2,1,0:T(8,128)(2,1)}, u32[]{:S(2)}) copy-start(bf16[2,128,768]{2,1,0:T(8,128)(2,1)} %get-tuple-element.81) | copy-start | bytes 1179652
  243.0 76.4 %copy-start.7 = (bf16[2,128,768]{2,1,0:T(8,128)(2,1)S(1)}, bf16[2,128,768]{2,1,0:T(8,128)(2,1)}, u32[]{:S(2)}) copy-start(bf16[2,128,768]{2,1,0:T(8,128)(2,1)} %get-tuple-element.82) | copy-start | bytes 1179652
  325.3 2.6 copy-start.2
  325.3 3.4 %copy-start.1 = (f32[544,256]{1,0:T(8,128)S(1)}, f32[544,256]{1,0:T(8,128)}, u32[]{:S(2)}) copy-start(f32[544,256]{1,0:T(8,128)} %get-tuple-element.77) | copy-start | bytes 1671172
  326.7 2.9 copy-start.8
  326.7 3.6 %copy-start.9 = (bf16[64,512]{1,0:T(8,128)(2,1)S(1)}, bf16[64,512]{1,0:T(8,128)(2,1)}, u32[]{:S(2)}) copy-start(bf16[64,512]{1,0:T(8,128)(2,1)} %get-tuple-element.85) | copy-start | bytes 196612
  326.7 4.3 %copy-start.5 = (bf16[128,128]{1,0:T(8,128)(2,1)S(1)}, bf16[128,128]{1,0:T(8,128)(2,1)}, u32[]{:S(2)}) copy-start(bf16[128,128]{1,0:T(8,128)(2,1)} %get-tuple-element.80) | copy-start | bytes 98308
  328.0 5.8 %copy-start.10 = (bf16[64,128]{1,0:T(8,128)(2,1)S(1)}, bf16[64,128]{1,0:T(8,128)(2,1)}, u32[]{:S(2)}) copy-start(bf16[64,128]{1,0:T(8,128)(2,1)} %get-tuple-element.86) | copy-start | bytes 49156
  328.0 11.0 %copy-start.11 = (bf16[2,64,768]{2,1,0:T(8,128)(2,1)S(1)}, bf16[2,64,768]{2,1,0:T(8,128)(2,1)}, u32[]{:S(2)}) copy-start(bf16[2,64,768]{2,1,0:T(8,128)(2,1)} %get-tuple-element.87) | copy-start | bytes 589828
  (4 other events, 7.1 us)
